TPU v7x, 32 devices: a whole 2x2x4 slice. The times are simulated.
32 devices in a mesh: fsdp: 8 (over y, x, core), tp: 4 (over z).
Axes of the slice: x: 2, y: 2, z: 4, core: 2. Of those that a mesh axis runs over, the one named last changes fastest.
Arguments:
- in_first: float32 [16384, 1024], P(('fsdp', 'tp')), may hold values from -6 to 6
- in_second: float32 [16384, 1024], P(('fsdp', 'tp')), may hold values from -6 to 6
- cot_first: float32 [16384, 1024], P(('fsdp', 'tp')), may hold values from -6 to 6
- cot_second: float32 [16384, 1024], P(('fsdp', 'tp')), may hold values from -6 to 6
- hash_order: int32 [8, 8, 4, 2048], P('fsdp', 'tp'), may hold values from 0 to 2047, each once within a row
- prefix_len: int32 [8], P('fsdp'), may hold values from 204 to 1024
- weight_shared: bfloat16 [1024, 1024], P('fsdp', 'tp'), may hold values from -0.1875 to 0.1875
- weight_value: bfloat16 [1024, 1024], P('fsdp', 'tp'), may hold values from -0.1875 to 0.1875
- weight_out: bfloat16 [1024, 1024], P('tp', 'fsdp'), may hold values from -2 to 2
- weight_up: bfloat16 [1024, 4096], P('fsdp', 'tp'), may hold values from -0.1875 to 0.1875
- bias_up: bfloat16 [4096], P(('tp', 'fsdp')), may hold values from -3 to 3
- weight_down: bfloat16 [4096, 1024], P('tp', 'fsdp'), may hold values from -0.09375 to 0.09375
- bias_down: bfloat16 [1024], P('fsdp'), may hold values from -3 to 3
- gain_one: bfloat16 [1024], P('fsdp'), may hold values from 0.25 to 1.75
- shift_one: bfloat16 [1024], P('fsdp'), may hold values from -3 to 3
- gain_two: bfloat16 [1024], P('fsdp'), may hold values from 0.25 to 1.75
- shift_two: bfloat16 [1024], P('fsdp'), may hold values from -3 to 3
Outputs:
- out_first: float32 [16384, 1024], P(('fsdp', 'tp'))
- out_second: float32 [16384, 1024], P(('fsdp', 'tp'))
- grad_in_first: float32 [16384, 1024], P(('fsdp', 'tp'))
- grad_in_second: float32 [16384, 1024], P(('fsdp', 'tp'))
- grad_weight_shared: float32 [1024, 1024], P('fsdp', 'tp')
- grad_weight_value: float32 [1024, 1024], P('fsdp', 'tp')
- grad_weight_out: float32 [1024, 1024], P('tp', 'fsdp')
- grad_weight_up: float32 [1024, 4096], P('fsdp', 'tp')
- grad_bias_up: float32 [4096], P(('tp', 'fsdp'))
- grad_weight_down: float32 [4096, 1024], P('tp', 'fsdp')
- grad_bias_down: float32 [1024], P(('fsdp', 'tp'))
- grad_gain_one: float32 [1024], P(('fsdp', 'tp'))
- grad_shift_one: float32 [1024], P(('fsdp', 'tp'))
- grad_gain_two: float32 [1024], P(('fsdp', 'tp'))
- grad_shift_two: float32 [1024], P(('fsdp', 'tp'))
Inputs may be any that keep to these rules, and one draw needn't show every extreme that they name: `hash_order`: each row is a permutation of the 2048 positions.
All inputs are finite; a program needn't handle non-finite values.
Results may differ from a plain program's by a relative error of at most 0.02.
Values may be sent and summed in bfloat16 or wider, within the bound.
A program may use at most 256 MiB of HBM per device.

v0:
```python
import jax
import jax.numpy as jnp
from jax import lax
from jax.sharding import PartitionSpec as P

HEAD_DIM = 128
BLOCK = 64


NEG_SELF = -100000.0
NEG_MASK = -1000000000.0


def normalize(row_values):
    center = row_values - jnp.mean(row_values, axis=-1, keepdims=True)
    factor = lax.rsqrt(jnp.mean(center * center, axis=-1, keepdims=True) + 1e-05)
    return (center * factor, factor)


def norm_backward(grad_rows, normed, factor, gain_vec):
    grad_normed = grad_rows * gain_vec
    inner_sum = (
        grad_normed
        - jnp.mean(grad_normed, axis=-1, keepdims=True)
        - normed * jnp.mean(grad_normed * normed, axis=-1, keepdims=True)
    )
    return (factor * inner_sum, jnp.sum(grad_rows * normed, axis=0), jnp.sum(grad_rows, axis=0))


def gelu_tanh(values):
    inner = 0.7978845608028654 * (values + 0.044715 * values * values * values)
    return 0.5 * values * (1.0 + jnp.tanh(inner))


def gelu_slope(values):
    inner = 0.7978845608028654 * (values + 0.044715 * values * values * values)
    bent = jnp.tanh(inner)
    return 0.5 * (1.0 + bent) + 0.5 * values * (1.0 - bent * bent) * 0.7978845608028654 * (
        1.0 + 3.0 * 0.044715 * values * values
    )


def sorted_rows(source, index_all):
    return jax.vmap(jax.vmap(lambda source_rows, index_list: source_rows[index_list]))(
        source, index_all
    )


def invert(sort_order):
    length = sort_order.shape[-1]
    ranks = jnp.broadcast_to(jnp.arange(length, dtype=jnp.int32), sort_order.shape)
    return jax.vmap(
        jax.vmap(
            lambda index_list, rank_list: jnp.zeros((length,), jnp.int32)
            .at[index_list]
            .set(rank_list)
        )
    )(sort_order, ranks)


def head_major(packed, heads_here):
    return packed.reshape(packed.shape[0], heads_here, -1).transpose(1, 0, 2)


def to_rows(grads_head):
    return grads_head.transpose(1, 0, 2).reshape(grads_head.shape[1], -1)


def windows(blocks):
    return jnp.concatenate([jnp.roll(blocks, 1, axis=-3), blocks], axis=-2)


def unwindow(grad_window):
    return grad_window[..., BLOCK:, :] + jnp.roll(grad_window[..., :BLOCK, :], -1, axis=-3)


def arrange(shared, values_in, sort_order, prefix):
    heads_here, rounds, length = sort_order.shape
    block_count = length // BLOCK
    queries = head_major(shared, heads_here)
    query_f = queries.astype(jnp.float32)
    inv_norm = lax.rsqrt(jnp.mean(query_f * query_f, axis=-1, keepdims=True) + 1e-06)
    key_rows = (query_f * inv_norm).astype(jnp.bfloat16)
    values = head_major(values_in, heads_here)

    def spread_sorted(source):
        widened = jnp.broadcast_to(source[:, None], (heads_here, rounds) + source.shape[1:])
        return sorted_rows(widened, sort_order).reshape(heads_here, rounds, block_count, BLOCK, -1)

    query_sorted = spread_sorted(queries)
    key_window = windows(spread_sorted(key_rows))
    value_window = windows(spread_sorted(values))
    query_pos = sort_order.reshape(heads_here, rounds, block_count, BLOCK)
    key_pos = windows(query_pos[..., None])[..., 0]
    query_at = query_pos[..., :, None]
    key_at = key_pos[..., None, :]
    allowed = (key_at < query_at) | (query_at < prefix) & (key_at < prefix)
    same_token = key_at == query_at
    raw_scores = jnp.einsum(
        "hrncd,hrnkd->hrnck", query_sorted, key_window, preferred_element_type=jnp.float32
    ) * HEAD_DIM ** (-0.5)
    scores = jnp.where(same_token, NEG_SELF, jnp.where(allowed, raw_scores, NEG_MASK))
    return (query_f, inv_norm, query_sorted, key_window, value_window, allowed, same_token, scores)


def attend(shared, values_in, sort_order, prefix):
    heads_here, rounds, length = sort_order.shape
    query_f, inv_norm, query_sorted, key_window, value_window, allowed, same_token, scores = (
        arrange(shared, values_in, sort_order, prefix)
    )
    row_peak = jnp.max(scores, axis=-1, keepdims=True)
    round_lse = row_peak[..., 0] + jnp.log(jnp.sum(jnp.exp(scores - row_peak), axis=-1))
    attn_probs = jnp.exp(scores - round_lse[..., None]).astype(jnp.bfloat16)
    round_out = jnp.einsum(
        "hrnck,hrnkd->hrncd", attn_probs, value_window, preferred_element_type=jnp.float32
    )
    inverse = invert(sort_order)
    round_out = sorted_rows(round_out.reshape(heads_here, rounds, length, -1), inverse)
    lse_tokens = sorted_rows(round_lse.reshape(heads_here, rounds, length, 1), inverse)[..., 0]
    round_peak = jnp.max(lse_tokens, axis=1, keepdims=True)
    total_lse = round_peak + jnp.log(
        jnp.sum(jnp.exp(lse_tokens - round_peak), axis=1, keepdims=True)
    )
    weight = jnp.exp(lse_tokens - total_lse)
    merged = jnp.sum(weight[..., None] * round_out, axis=1)
    return (to_rows(merged).astype(jnp.bfloat16), round_out, weight, round_lse)


def attend_back(shared, values_in, sort_order, prefix, round_out, weight, round_lse, grad_packed):
    heads_here, rounds, length = sort_order.shape
    block_count = length // BLOCK
    query_f, inv_norm, query_sorted, key_window, value_window, allowed, same_token, scores = (
        arrange(shared, values_in, sort_order, prefix)
    )
    probs_full = jnp.exp(scores - round_lse[..., None])
    grad_merged = head_major(grad_packed, heads_here).astype(jnp.float32)
    merged = jnp.sum(weight[..., None] * round_out, axis=1)
    grad_lse = weight * jnp.sum(grad_merged[:, None] * (round_out - merged[:, None]), axis=-1)
    grad_round = (weight[..., None] * grad_merged[:, None]).astype(jnp.bfloat16)
    grad_round = sorted_rows(grad_round, sort_order).reshape(
        heads_here, rounds, block_count, BLOCK, -1
    )
    grad_lse = sorted_rows(grad_lse[..., None], sort_order).reshape(
        heads_here, rounds, block_count, BLOCK, 1
    )
    grad_probs = jnp.einsum(
        "hrncd,hrnkd->hrnck", grad_round, value_window, preferred_element_type=jnp.float32
    )
    inner_sum = jnp.sum(probs_full * grad_probs, axis=-1, keepdims=True)
    live = allowed & jnp.logical_not(same_token)
    grad_scores = jnp.where(live, probs_full * (grad_probs - inner_sum + grad_lse), 0.0).astype(
        jnp.bfloat16
    )
    factor = HEAD_DIM ** (-0.5)
    grad_query = (
        jnp.einsum(
            "hrnck,hrnkd->hrncd", grad_scores, key_window, preferred_element_type=jnp.float32
        )
        * factor
    )
    grad_keywin = (
        jnp.einsum(
            "hrnck,hrncd->hrnkd", grad_scores, query_sorted, preferred_element_type=jnp.float32
        )
        * factor
    )
    grad_valwin = jnp.einsum(
        "hrnck,hrncd->hrnkd",
        probs_full.astype(jnp.bfloat16),
        grad_round,
        preferred_element_type=jnp.float32,
    )
    inverse = invert(sort_order)

    def gather_back(grad_blocks):
        return jnp.sum(
            sorted_rows(grad_blocks.reshape(heads_here, rounds, length, -1), inverse), axis=1
        )

    grad_direct = gather_back(grad_query)
    grad_keys = gather_back(unwindow(grad_keywin))
    grad_values = gather_back(unwindow(grad_valwin))
    grad_total = (
        grad_direct
        + inv_norm * grad_keys
        - query_f * inv_norm**3 * jnp.mean(grad_keys * query_f, axis=-1, keepdims=True)
    )
    return (to_rows(grad_total).astype(jnp.bfloat16), to_rows(grad_values).astype(jnp.bfloat16))


def cross(left, right):
    return lax.dot_general(
        left, right, (((0,), (0,)), ((), ())), preferred_element_type=jnp.float32
    )


def on_device(
    in_first,
    in_second,
    cot_first,
    cot_second,
    hash_order,
    prefix_len,
    weight_shared,
    weight_value,
    weight_out,
    weight_up,
    bias_up,
    weight_down,
    bias_down,
    gain_one,
    shift_one,
    gain_two,
    shift_two,
):
    seq_count = hash_order.shape[0]
    length = hash_order.shape[3]
    (
        full_shared,
        full_value,
        full_out,
        full_up,
        full_down,
        full_bias,
        gain_a,
        shift_a,
        gain_b,
        shift_b,
        bias_last,
    ) = (
        lax.all_gather(weight_shared, "fsdp", axis=0, tiled=True),
        lax.all_gather(weight_value, "fsdp", axis=0, tiled=True),
        lax.all_gather(weight_out, "fsdp", axis=1, tiled=True),
        lax.all_gather(weight_up, "fsdp", axis=0, tiled=True),
        lax.all_gather(weight_down, "fsdp", axis=1, tiled=True),
        lax.all_gather(bias_up, "fsdp", axis=0, tiled=True),
        lax.all_gather(gain_one, "fsdp", axis=0, tiled=True),
        lax.all_gather(shift_one, "fsdp", axis=0, tiled=True),
        lax.all_gather(gain_two, "fsdp", axis=0, tiled=True),
        lax.all_gather(shift_two, "fsdp", axis=0, tiled=True),
        lax.all_gather(bias_down, "fsdp", axis=0, tiled=True),
    )
    norm_one, factor_one = normalize(in_second)
    first_low = (norm_one * gain_a.astype(jnp.float32) + shift_a.astype(jnp.float32)).astype(
        jnp.bfloat16
    )
    first_all = lax.all_gather(first_low, "tp", axis=0, tiled=True)
    shared = jnp.dot(first_all, full_shared, preferred_element_type=jnp.float32).astype(
        jnp.bfloat16
    )
    values = jnp.dot(first_all, full_value, preferred_element_type=jnp.float32).astype(jnp.bfloat16)
    shared_seq = shared.reshape(seq_count, length, -1)
    values_seq = values.reshape(seq_count, length, -1)
    packed, round_out, weight, round_lse = jax.vmap(attend)(
        shared_seq, values_seq, hash_order, prefix_len
    )
    merged_all = packed.reshape(seq_count * length, -1)
    out_first = in_first + lax.psum_scatter(
        jnp.dot(merged_all, full_out, preferred_element_type=jnp.float32).astype(jnp.bfloat16),
        "tp",
        scatter_dimension=0,
        tiled=True,
    ).astype(jnp.float32)
    norm_two, factor_two = normalize(out_first)
    second_low = (norm_two * gain_b.astype(jnp.float32) + shift_b.astype(jnp.float32)).astype(
        jnp.bfloat16
    )
    second_all = lax.all_gather(second_low, "tp", axis=0, tiled=True)
    pre_act = jnp.dot(second_all, full_up, preferred_element_type=jnp.float32) + full_bias.astype(
        jnp.float32
    )
    hidden = gelu_tanh(pre_act).astype(jnp.bfloat16)
    out_second = (
        in_second
        + lax.psum_scatter(
            jnp.dot(hidden, full_down, preferred_element_type=jnp.float32).astype(jnp.bfloat16),
            "tp",
            scatter_dimension=0,
            tiled=True,
        ).astype(jnp.float32)
        + bias_last.astype(jnp.float32)
    )
    (
        back_shared,
        back_value,
        back_out,
        back_up,
        back_down,
        back_bias,
        gain_c,
        shift_c,
        gain_d,
        shift_d,
        bias_again,
    ) = (
        lax.all_gather(weight_shared, "fsdp", axis=0, tiled=True),
        lax.all_gather(weight_value, "fsdp", axis=0, tiled=True),
        lax.all_gather(weight_out, "fsdp", axis=1, tiled=True),
        lax.all_gather(weight_up, "fsdp", axis=0, tiled=True),
        lax.all_gather(weight_down, "fsdp", axis=1, tiled=True),
        lax.all_gather(bias_up, "fsdp", axis=0, tiled=True),
        lax.all_gather(gain_one, "fsdp", axis=0, tiled=True),
        lax.all_gather(shift_one, "fsdp", axis=0, tiled=True),
        lax.all_gather(gain_two, "fsdp", axis=0, tiled=True),
        lax.all_gather(shift_two, "fsdp", axis=0, tiled=True),
        lax.all_gather(bias_down, "fsdp", axis=0, tiled=True),
    )
    grad_up_all = lax.all_gather(cot_second.astype(jnp.bfloat16), "tp", axis=0, tiled=True)
    grad_hidden = jnp.dot(grad_up_all, back_down.T, preferred_element_type=jnp.float32)
    grad_pre = (grad_hidden * gelu_slope(pre_act)).astype(jnp.bfloat16)
    grad_weight_down = cross(hidden, grad_up_all)
    grad_weight_up = cross(second_all, grad_pre)
    grad_bias_up = jnp.sum(grad_pre, axis=0, dtype=jnp.float32)
    grad_bias_down = jnp.sum(cot_second, axis=0)
    grad_second = lax.psum_scatter(
        jnp.dot(grad_pre, back_up.T, preferred_element_type=jnp.float32).astype(jnp.bfloat16),
        "tp",
        scatter_dimension=0,
        tiled=True,
    ).astype(jnp.float32)
    part_first, grad_gain_two, grad_shift_two = norm_backward(
        grad_second, norm_two, factor_two, gain_d.astype(jnp.float32)
    )
    grad_in_first = cot_first + part_first
    grad_branch = lax.all_gather(grad_in_first.astype(jnp.bfloat16), "tp", axis=0, tiled=True)
    grad_merged = jnp.dot(grad_branch, back_out.T, preferred_element_type=jnp.float32).astype(
        jnp.bfloat16
    )
    grad_weight_out = cross(merged_all, grad_branch)
    grad_shared, grad_value = jax.vmap(attend_back)(
        shared_seq,
        values_seq,
        hash_order,
        prefix_len,
        round_out,
        weight,
        round_lse,
        grad_merged.reshape(seq_count, length, -1),
    )
    grad_shared = grad_shared.reshape(seq_count * length, -1)
    grad_value = grad_value.reshape(seq_count * length, -1)
    grad_weight_shared = cross(first_all, grad_shared)
    grad_weight_value = cross(first_all, grad_value)
    part_shared = jnp.dot(grad_shared, back_shared.T, preferred_element_type=jnp.float32)
    part_value = jnp.dot(grad_value, back_value.T, preferred_element_type=jnp.float32)
    grad_first = lax.psum_scatter(
        (part_shared + part_value).astype(jnp.bfloat16), "tp", scatter_dimension=0, tiled=True
    ).astype(jnp.float32)
    part_second, grad_gain_one, grad_shift_one = norm_backward(
        grad_first, norm_one, factor_one, gain_c.astype(jnp.float32)
    )
    grad_in_second = cot_second + part_second
    summed_shared, summed_value, summed_out, summed_up, summed_bias, summed_down = (
        lax.psum_scatter(grad_weight_shared, "fsdp", scatter_dimension=0, tiled=True),
        lax.psum_scatter(grad_weight_value, "fsdp", scatter_dimension=0, tiled=True),
        lax.psum_scatter(grad_weight_out, "fsdp", scatter_dimension=1, tiled=True),
        lax.psum_scatter(grad_weight_up, "fsdp", scatter_dimension=0, tiled=True),
        lax.psum_scatter(grad_bias_up, "fsdp", scatter_dimension=0, tiled=True),
        lax.psum_scatter(grad_weight_down, "fsdp", scatter_dimension=1, tiled=True),
    )
    norm_gain_a, norm_shift_a, norm_gain_b, norm_shift_b, norm_bias = (
        lax.psum_scatter(grad_gain_one, ("fsdp", "tp"), scatter_dimension=0, tiled=True),
        lax.psum_scatter(grad_shift_one, ("fsdp", "tp"), scatter_dimension=0, tiled=True),
        lax.psum_scatter(grad_gain_two, ("fsdp", "tp"), scatter_dimension=0, tiled=True),
        lax.psum_scatter(grad_shift_two, ("fsdp", "tp"), scatter_dimension=0, tiled=True),
        lax.psum_scatter(grad_bias_down, ("fsdp", "tp"), scatter_dimension=0, tiled=True),
    )
    return (
        out_first,
        out_second,
        grad_in_first,
        grad_in_second,
        summed_shared,
        summed_value,
        summed_out,
        summed_up,
        summed_bias,
        summed_down,
        norm_bias,
        norm_gain_a,
        norm_shift_a,
        norm_gain_b,
        norm_shift_b,
    )


def solution(mesh):
    in_specs = (
        P(("fsdp", "tp"), None),
        P(("fsdp", "tp"), None),
        P(("fsdp", "tp"), None),
        P(("fsdp", "tp"), None),
        P("fsdp", "tp", None, None),
        P("fsdp"),
        P("fsdp", "tp"),
        P("fsdp", "tp"),
        P("tp", "fsdp"),
        P("fsdp", "tp"),
        P(("tp", "fsdp")),
        P("tp", "fsdp"),
        P("fsdp"),
        P("fsdp"),
        P("fsdp"),
        P("fsdp"),
        P("fsdp"),
    )
    out_specs = (
        P(("fsdp", "tp"), None),
        P(("fsdp", "tp"), None),
        P(("fsdp", "tp"), None),
        P(("fsdp", "tp"), None),
        P("fsdp", "tp"),
        P("fsdp", "tp"),
        P("tp", "fsdp"),
        P("fsdp", "tp"),
        P(("tp", "fsdp")),
        P("tp", "fsdp"),
        P(("fsdp", "tp")),
        P(("fsdp", "tp")),
        P(("fsdp", "tp")),
        P(("fsdp", "tp")),
        P(("fsdp", "tp")),
    )
    return jax.shard_map(
        on_device, mesh=mesh, in_specs=in_specs, out_specs=out_specs, check_vma=False
    )
```

profile of v0, /device:TPU:0, one launch (start us, length us, event | category | flops | bytes accessed | tf_op | source)
XLA Modules:
  0.0 3827.6 jit_solution(5059140827395058450)
XLA Ops:
  11.9 10.3 all-gather
  22.2 8.6 all-gather.1
  35.3 60.3 %scatter_custom_fusion = s32[16384]{0:T(1024)S(1)} fusion(s32[16384]{0:T(1024)S(1)} %bitcast.217, s32[16384]{0:T(1024)S(1)} %bitcast.216, s32[]{:T(128)} %constant.13.clone.1), kind=kCustom, calls=%fused_computation.145 | custom fusion | bytes 65540
  96.1 9.0 all_gather.55
  105.1 9.7 all_gather.56
  114.8 9.1 all_gather.57
  132.9 285.2 %gather_fusion.3 = bf16[16384,128]{1,0:T(8,128)(2,1)} fusion(bf16[1,2,4,2048,128]{4,3,2,1,0:T(8,128)(2,1)} %broadcast_in_dim.41, s32[16384]{0:T(1024)S(1)} %bitcast.172), kind=kCustom, calls=%fused_computation.3 | custom fusion | bytes 8650752 | tf_op jit(solution)/shard_map/vmap(vmap(vmap()))/gather | solution.py:44
  432.7 285.3 %gather_fusion.1 = bf16[16384,128]{1,0:T(8,128)(2,1)} fusion(bf16[1,2,4,2048,128]{4,3,2,1,0:T(8,128)(2,1)} %broadcast_in_dim.36, s32[16384]{0:T(1024)S(1)} %bitcast.173), kind=kCustom, calls=%fused_computation.1 | custom fusion | bytes 8650752 | tf_op jit(solution)/shard_map/vmap(vmap(vmap()))/gather | solution.py:44
  726.4 285.2 %gather_fusion = bf16[16384,128]{1,0:T(8,128)(2,1)} fusion(bf16[1,2,4,2048,128]{4,3,2,1,0:T(8,128)(2,1)} %broadcast_in_dim.33, s32[16384]{0:T(1024)S(1)} %bitcast.174), kind=kCustom, calls=%fused_computation | custom fusion | bytes 8650752 | tf_op jit(solution)/shard_map/vmap(vmap(vmap()))/gather | solution.py:44
  1011.7 11.3 fusion.82
  1028.0 159.6 %gather_fusion.2 = f32[16384]{0:T(1024)S(1)} fusion(f32[1,2,4,2048]{3,2,1,0:T(4,128)S(1)} %reshape.468, s32[16384]{0:T(1024)S(1)} %bitcast.167), kind=kCustom, calls=%fused_computation.2 | custom fusion | bytes 393216 | tf_op jit(solution)/shard_map/vmap(vmap(vmap()))/gather | solution.py:44
  1187.8 9.6 fusion.15
  1197.4 249.5 %gather_fusion.4 = f32[16384,128]{1,0:T(8,128)} fusion(f32[1,2,4,2048,128]{4,3,2,1,0:T(8,128)} %bitcast.180, s32[16384]{0:T(1024)S(1)} %bitcast.168), kind=kCustom, calls=%fused_computation.4 | custom fusion | bytes 17039360 | tf_op jit(solution)/shard_map/vmap(vmap(vmap()))/gather | solution.py:44
  1458.2 8.5 all-gather.2
  1474.7 60.3 %reduce-scatter.10.cloned.1.call-done = bf16[512,1024]{1,0:T(8,128)(2,1)} async-done(((bf16[2048,1024]{1,0:T(8,128)(2,1)}), bf16[512,1024]{1,0:T(8,128)(2,1)}) %reduce-scatter.10.cloned.1.call-update) | async-done | bytes 1048592 | tf_op jit(solution)/shard_map/reduce_scatter | solution.py:258
  1543.7 8.7 all-gather.4
  1552.4 67.7 %all-gather.15.cloned.1.call-done = bf16[2048,1024]{1,0:T(8,128)(2,1)} async-done(((bf16[512,1024]{1,0:T(8,128)(2,1)}), bf16[2048,1024]{1,0:T(8,128)(2,1)}) %all-gather.15.cloned.1.call-update) | async-done | bytes 4194320 | tf_op jit(solution)/shard_map/all_gather | solution.py:268
  1620.1 10.6 fusion.83
  1630.7 17.9 all-gather.19.cloned.1.call-done
  1648.6 82.9 %all-gather.21.cloned.1.call-done = bf16[2048,1024]{1,0:T(8,128)(2,1)} async-done(((bf16[512,1024]{1,0:T(8,128)(2,1)}), bf16[2048,1024]{1,0:T(8,128)(2,1)}) %all-gather.21.cloned.1.call-update) | async-done | bytes 4194320 | tf_op jit(solution)/shard_map/all_gather | solution.py:308
  1731.5 14.0 convert_reduce_fusion
  1753.9 75.4 %reduce-scatter.14.cloned.1.call-done = bf16[512,1024]{1,0:T(8,128)(2,1)} async-done(((bf16[2048,1024]{1,0:T(8,128)(2,1)}), bf16[512,1024]{1,0:T(8,128)(2,1)}) %reduce-scatter.14.cloned.1.call-update) | async-done | bytes 1048592 | tf_op jit(solution)/shard_map/reduce_scatter | solution.py:315
  1836.4 81.1 %all-gather.23.cloned.1.call-done = bf16[2048,1024]{1,0:T(8,128)(2,1)} async-done(((bf16[512,1024]{1,0:T(8,128)(2,1)}), bf16[2048,1024]{1,0:T(8,128)(2,1)}) %all-gather.23.cloned.1.call-update) | async-done | bytes 4194320 | tf_op jit(solution)/shard_map/all_gather | solution.py:325
  1925.7 8.5 multiply_reduce_fusion
  1934.3 159.6 %gather_fusion.6 = f32[16384]{0:T(1024)S(1)} fusion(f32[1,2,4,2048]{3,2,1,0:T(4,128)S(1)} %fusion.67, s32[16384]{0:T(1024)S(1)} %bitcast.175), kind=kCustom, calls=%fused_computation.6 | custom fusion | bytes 393216 | tf_op jit(solution)/shard_map/vmap(vmap(vmap()))/gather | solution.py:44
  2093.9 285.2 %gather_fusion.5 = bf16[16384,128]{1,0:T(8,128)(2,1)} fusion(bf16[1,2,4,2048,128]{4,3,2,1,0:T(8,128)(2,1)} %get-tuple-element.39, s32[16384]{0:T(1024)S(1)} %bitcast.176), kind=kCustom, calls=%fused_computation.5 | custom fusion | bytes 8650752 | tf_op jit(solution)/shard_map/vmap(vmap(vmap()))/gather | solution.py:44
  2379.1 13.7 fusion.14
  2392.9 106.8 %broadcast_multiply_fusion = f32[2,4,32,64,128]{4,3,2,1,0:T(8,128)} fusion(bf16[1,2,4,32,64,128]{5,4,3,2,1,0:T(8,128)(2,1)} %bitcast.196, bf16[1,2,4,31,64,128]{5,4,3,2,1,0:T(8,128)(2,1)} %slice.113, bf16[1,2,4,1,64,128]{5,4,3,2,1,0:T(8,128)(2,1)S(1)} %copy-done.20, f32[2,4,32,64,128]{4,3,2,1,0:T(8,128)} %fusion.14, f32[2,4,32,64,128]{4,3,2,1,0:T(8,128)} %copy-done.5, ...), kind=kOutput, calls=%fused_computation.44 | convolution fusion | flops 593510528 | bytes 33931264 | tf_op jit(solution)/shard_map/vmap(hrnck,hrnkd->hrncd)/dot_general | solution.py:156
  2499.7 110.7 %multiply_bitcast_fusion = f32[1,2,4,32,128,128]{5,4,3,2,1,0:T(8,128)} fusion(bf16[2,4,32,64,128]{4,3,2,1,0:T(8,128)(2,1)} %bitcast.205, f32[2,4,32,64,128]{4,3,2,1,0:T(8,128)} %fusion.14, f32[2,4,32,64,128]{4,3,2,1,0:T(8,128)} %copy-done.5, f32[2,4,32,64]{3,2,1,0:T(8,128)S(1)} %add.216, f32[2,4,32,64]{3,2,1,0:T(8,128)S(1)} %log_add_fusion, ...), kind=kOutput, calls=%fused_computation.12 | convolution fusion | flops 570441856 | bytes 38125568 | tf_op jit(solution)/shard_map/vmap(hrnck,hrncd->hrnkd)/dot_general | solution.py:162
  2610.4 9.7 convolution_bitcast_fusion
  2630.8 8.1 slice.121
  2638.9 249.3 %gather_fusion.7 = f32[16384,128]{1,0:T(8,128)} fusion(f32[1,2,4,2048,128]{4,3,2,1,0:T(8,128)} %bitcast.179, s32[16384]{0:T(1024)S(1)} %bitcast.169), kind=kCustom, calls=%fused_computation.7 | custom fusion | bytes 17039360 | tf_op jit(solution)/shard_map/vmap(vmap(vmap()))/gather | solution.py:44
  2893.6 9.1 slice_add_fusion
  2902.7 249.2 %gather_fusion.9 = f32[16384,128]{1,0:T(8,128)} fusion(f32[1,2,4,2048,128]{4,3,2,1,0:T(8,128)} %bitcast.178, s32[16384]{0:T(1024)S(1)} %bitcast.170), kind=kCustom, calls=%fused_computation.9 | custom fusion | bytes 17039360 | tf_op jit(solution)/shard_map/vmap(vmap(vmap()))/gather | solution.py:44
  3157.5 9.1 slice_add_fusion.1
  3166.6 249.3 %gather_fusion.8 = f32[16384,128]{1,0:T(8,128)} fusion(f32[1,2,4,2048,128]{4,3,2,1,0:T(8,128)} %bitcast.177, s32[16384]{0:T(1024)S(1)} %bitcast.171), kind=kCustom, calls=%fused_computation.8 | custom fusion | bytes 17039360 | tf_op jit(solution)/shard_map/vmap(vmap(vmap()))/gather | solution.py:44
  3432.9 11.7 convolution_convert_fusion.2
  3444.7 12.6 fusion.77
  3457.6 10.1 fusion.88
  3482.6 8.8 all-gather.5
  3492.1 13.2 all-reduce
  3510.6 46.3 %all-reduce.6 = (f32[1024]{0:T(1024)S(1)}, f32[1024]{0:T(1024)S(1)}, f32[1024]{0:T(1024)S(1)}, f32[1024]{0:T(1024)S(1)}, f32[1024]{0:T(1024)S(1)}) all-reduce(f32[1024]{0:T(1024)S(1)} %copy-done.37, f32[1024]{0:T(1024)S(1)} %get-tuple-element.17, ...), channel_id=12, replica_groups=mesh['fsdp'=8,'tp'=4] {'fsdp','tp'}, use_global_device_ids=true, to_apply=%region_33.34.clone | all-reduce | flops 5120 | bytes 40960
  3559.8 29.1 reduce-scatter.12.cloned.1.call-done
  3594.0 50.7 %reduce-scatter.26.cloned.1.call-done = f32[1024,128]{1,0:T(8,128)} async-done(((f32[1024,1024]{1,0:T(8,128)}), f32[1024,128]{1,0:T(8,128)}) %reduce-scatter.26.cloned.1.call-update) | async-done | bytes 524304 | tf_op jit(solution)/shard_map/reduce_scatter | solution.py:359
  3644.7 55.7 %reduce-scatter.24.cloned.1.call-done = f32[128,1024]{1,0:T(8,128)} async-done(((f32[1024,1024]{1,0:T(8,128)}), f32[128,1024]{1,0:T(8,128)}) %reduce-scatter.24.cloned.1.call-update) | async-done | bytes 524304 | tf_op jit(solution)/shard_map/reduce_scatter | solution.py:357
  3700.3 39.8 %reduce-scatter.22.cloned.1.call-done = f32[256,128]{1,0:T(8,128)} async-done(((f32[256,1024]{1,0:T(8,128)}), f32[256,128]{1,0:T(8,128)}) %reduce-scatter.22.cloned.1.call-update) | async-done | bytes 131088 | tf_op jit(solution)/shard_map/reduce_scatter | solution.py:356
  3740.1 39.8 %reduce-scatter.20.cloned.1.call-done = f32[128,256]{1,0:T(8,128)} async-done(((f32[1024,256]{1,0:T(8,128)}), f32[128,256]{1,0:T(8,128)}) %reduce-scatter.20.cloned.1.call-update) | async-done | bytes 131088 | tf_op jit(solution)/shard_map/reduce_scatter | solution.py:355
  3779.9 39.7 %reduce-scatter.18.cloned.1.call-done = f32[128,256]{1,0:T(8,128)} async-done(((f32[1024,256]{1,0:T(8,128)}), f32[128,256]{1,0:T(8,128)}) %reduce-scatter.18.cloned.1.call-update) | async-done | bytes 131088 | tf_op jit(solution)/shard_map/reduce_scatter | solution.py:354
  (243 shorter events, 163.4 us)
Async XLA Ops:
  8.0 26.9 copy-start.48
  8.0 27.1 copy-start.43
  8.0 25.9 copy-start.14
  8.0 88.0 %copy-start.26 = (bf16[128,256]{1,0:T(8,128)(2,1)S(1)}, bf16[128,256]{1,0:T(8,128)(2,1)}, u32[]{:S(2)}) copy-start(bf16[128,256]{1,0:T(8,128)(2,1)} %param.23) | copy-start | bytes 196612
  8.1 97.0 %copy-start.27 = (bf16[128,256]{1,0:T(8,128)(2,1)S(1)}, bf16[128,256]{1,0:T(8,128)(2,1)}, u32[]{:S(2)}) copy-start(bf16[128,256]{1,0:T(8,128)(2,1)} %param.24) | copy-start | bytes 196612
  8.1 106.8 %copy-start.28 = (bf16[256,128]{1,0:T(8,128)(2,1)S(1)}, bf16[256,128]{1,0:T(8,128)(2,1)}, u32[]{:S(2)}) copy-start(bf16[256,128]{1,0:T(8,128)(2,1)} %param.25) | copy-start | bytes 196612
  8.1 116.1 %all-gather.13.cloned.1.call-start = ((), (), s32[]{:S(2)}) async-start(), calls=%async_computation.9 | async-start | bytes 5242880 | tf_op jit(solution)/shard_map/all_gather | solution.py:247
  9.9 20.9 copy-start.29
  11.9 18.9 copy-start.31
  33.9 1501.1 %reduce-scatter.10.cloned.1.call-start = ((), (), s32[]{:S(2)}) async-start(), calls=%async_computation.10 | async-start | bytes 5242880 | tf_op jit(solution)/shard_map/reduce_scatter | solution.py:258
  34.0 977.6 %copy-start.15 = (s32[2,4,32,64]{3,2,1,0:T(8,128)}, s32[2,4,32,64]{3,2,1,0:T(8,128)S(1)}, u32[]{:S(2)}) copy-start(s32[2,4,32,64]{3,2,1,0:T(8,128)S(1)} %eq.13) | copy-start | bytes 196612
  105.1 319.3 %copy-start.13 = (bf16[1024,256]{1,0:T(8,128)(2,1)}, bf16[1024,256]{1,0:T(8,128)(2,1)S(1)}, u32[]{:S(2)}) copy-start(bf16[1024,256]{1,0:T(8,128)(2,1)S(1)} %all_gather.55) | copy-start | bytes 1572868
  124.1 887.6 %copy-start.21 = (s32[2,4,32,128]{3,2,1,0:T(8,128)}, s32[2,4,32,128]{3,2,1,0:T(8,128)S(1)}, u32[]{:S(2)}) copy-start(s32[2,4,32,128]{3,2,1,0:T(8,128)S(1)} %get-tuple-element.33) | copy-start | bytes 393220
  124.1 887.6 %copy-start.35 = (pred[2,4,32,128]{3,2,1,0:T(8,128)(4,1)}, pred[2,4,32,128]{3,2,1,0:T(8,128)(4,1)S(1)}, u32[]{:S(2)}) copy-start(pred[2,4,32,128]{3,2,1,0:T(8,128)(4,1)S(1)} %get-tuple-element.32) | copy-start | bytes 98308
  124.1 887.6 %copy-start.33 = (pred[2,4,32,64]{3,2,1,0:T(8,128)(4,1)}, pred[2,4,32,64]{3,2,1,0:T(8,128)(4,1)S(1)}, u32[]{:S(2)}) copy-start(pred[2,4,32,64]{3,2,1,0:T(8,128)(4,1)S(1)} %broadcast_compare_fusion.1) | copy-start | bytes 49156
  428.3 295.7 %copy-start.3 = (bf16[1,2048,2,128]{3,1,2,0:T(8,128)(2,1)}, bf16[1,2048,2,128]{3,1,2,0:T(8,128)(2,1)S(1)}, u32[]{:S(2)}) copy-start(bf16[1,2048,2,128]{3,1,2,0:T(8,128)(2,1)S(1)} %copy.52) | copy-start | bytes 3145732
  429.6 288.4 %copy-start.17 = (f32[2,2048]{1,0:T(2,128)}, f32[2,2048]{1,0:T(2,128)S(1)}, u32[]{:S(2)}) copy-start(f32[2,2048]{1,0:T(2,128)S(1)} %get-tuple-element.43) | copy-start | bytes 49156
  718.9 292.8 %copy-start.19 = (bf16[1,2,4,1,64,128]{5,4,3,2,1,0:T(8,128)(2,1)}, bf16[1,2,4,1,64,128]{5,4,3,2,1,0:T(8,128)(2,1)S(1)}, u32[]{:S(2)}) copy-start(bf16[1,2,4,1,64,128]{5,4,3,2,1,0:T(8,128)(2,1)S(1)} %slice.112) | copy-start | bytes 393220
  1454.3 20.4 copy-start.8
  1457.6 86.1 %copy-start.46 = (bf16[128]{0:T(256)(128)(2,1)S(1)}, bf16[128]{0:T(256)(128)(2,1)}, u32[]{:S(2)}) copy-start(bf16[128]{0:T(256)(128)(2,1)} %param.27) | copy-start | bytes 772
  1457.6 94.8 %all-gather.17.cloned.1.call-start = ((), (), s32[]{:S(2)}) async-start(), calls=%async_computation.12 | async-start | bytes 2359296 | tf_op jit(solution)/shard_map/all_gather | solution.py:234
  1458.2 162.0 %all-gather.15.cloned.1.call-start = ((), (), s32[]{:S(2)}) async-start(), calls=%async_computation.11 | async-start | bytes 5242880 | tf_op jit(solution)/shard_map/all_gather | solution.py:268
  1537.1 294.9 %copy-start.1 = (f32[512,1024]{1,0:T(8,128)}, f32[512,1024]{1,0:T(8,128)S(1)}, u32[]{:S(2)}) copy-start(f32[512,1024]{1,0:T(8,128)S(1)} %get-tuple-element.31) | copy-start | bytes 6291460
  1538.9 109.7 %all-gather.19.cloned.1.call-start = ((), (), s32[]{:S(2)}) async-start(), calls=%async_computation.13 | async-start | bytes 2359296 | tf_op jit(solution)/shard_map/all_gather | solution.py:235
  1539.5 192.0 %all-gather.21.cloned.1.call-start = ((), (), s32[]{:S(2)}) async-start(), calls=%async_computation.15 | async-start | bytes 5242880 | tf_op jit(solution)/shard_map/all_gather | solution.py:308
  1543.6 285.7 %reduce-scatter.14.cloned.1.call-start = ((), (), s32[]{:S(2)}) async-start(), calls=%async_computation.16 | async-start | bytes 5242880 | tf_op jit(solution)/shard_map/reduce_scatter | solution.py:315
  1552.4 179.1 %copy-start.41 = (f32[8,1,128]{2,1,0:T(1,128)}, f32[8,1,128]{2,1,0:T(1,128)S(1)}, u32[]{:S(2)}) copy-start(f32[8,1,128]{2,1,0:T(1,128)S(1)} %convert_element_type.197) | copy-start | bytes 12292
  1731.5 16.0 copy-start.50
  1753.9 163.7 %all-gather.23.cloned.1.call-start = ((), (), s32[]{:S(2)}) async-start(), calls=%async_computation.17 | async-start | bytes 5242880 | tf_op jit(solution)/shard_map/all_gather | solution.py:325
  1836.3 89.4 %copy-start.7 = (f32[2,2048,128]{2,1,0:T(8,128)S(1)}, f32[2,2048,128]{2,1,0:T(8,128)}, u32[]{:S(2)}) copy-start(f32[2,2048,128]{2,1,0:T(8,128)} %copy-done.6) | copy-start | bytes 6291460
  1836.4 1672.0 %reduce-scatter.16.cloned.1.call-start = ((), (), s32[]{:S(2)}) async-start(), calls=%async_computation.18 | async-start | bytes 5242880 | tf_op jit(solution)/shard_map/reduce_scatter | solution.py:346
  2379.0 13.8 copy-start.22
  2379.0 13.9 copy-start.34
  2379.0 13.9 copy-start.36
  3432.7 156.3 %reduce-scatter.12.cloned.1.call-start = ((), (), s32[]{:S(2)}) async-start(), calls=%async_computation.14 | async-start | bytes 5242880 | tf_op jit(solution)/shard_map/reduce_scatter | solution.py:275
  3444.6 200.1 %reduce-scatter.26.cloned.1.call-start = ((), (), s32[]{:S(2)}) async-start(), calls=%async_computation.23 | async-start | bytes 4718592 | tf_op jit(solution)/shard_map/reduce_scatter | solution.py:359
  3457.3 243.1 %reduce-scatter.24.cloned.1.call-start = ((), (), s32[]{:S(2)}) async-start(), calls=%async_computation.22 | async-start | bytes 4718592 | tf_op jit(solution)/shard_map/reduce_scatter | solution.py:357
  3467.7 272.4 %reduce-scatter.22.cloned.1.call-start = ((), (), s32[]{:S(2)}) async-start(), calls=%async_computation.21 | async-start | bytes 1179648 | tf_op jit(solution)/shard_map/reduce_scatter | solution.py:356
  3472.2 19.8 copy-start.40
  3472.2 36.1 copy-start.2
  3472.3 36.1 copy-start.24
  3472.3 36.1 copy-start.30
  3472.3 36.1 copy-start.32
  3472.3 307.6 %reduce-scatter.20.cloned.1.call-start = ((), (), s32[]{:S(2)}) async-start(), calls=%async_computation.20 | async-start | bytes 1179648 | tf_op jit(solution)/shard_map/reduce_scatter | solution.py:355
  3477.3 33.2 copy-start.37
  3477.3 33.2 copy-start.38
  3477.3 33.2 copy-start.39
  3477.3 342.2 %reduce-scatter.18.cloned.1.call-start = ((), (), s32[]{:S(2)}) async-start(), calls=%async_computation.19 | async-start | bytes 1179648 | tf_op jit(solution)/shard_map/reduce_scatter | solution.py:354
  (20 other events, 143.6 us)
Sparse Core Ops, SparseCore 0:
  34.0 81.0 all-gather.12
  1457.7 77.2 reduce-scatter.9
  1754.0 75.2 reduce-scatter.13
  3432.8 75.5 reduce-scatter.15
  3510.6 78.3 reduce-scatter.11
  3592.8 51.8 reduce-scatter.25
  3649.0 51.3 reduce-scatter.23
  3704.1 35.9 reduce-scatter.21
  3743.9 35.9 reduce-scatter.19
  3783.5 36.0 reduce-scatter.17
Sparse Core Ops, SparseCore 1:
  1460.1 28.2 all-gather.16
  1539.0 81.1 all-gather.14
  1622.0 26.5 all-gather.18
  1650.9 80.6 all-gather.20
  1836.4 81.1 all-gather.22
where the time goes:
time: 3840 us; the launch traced here: 3830 us
  local copies, waits for them, and re-layouts  2570 us (67%)
  waiting for transfers between devices  644 us (17%)
  matrix products  360 us (9%)
  blocking collectives  140 us (4%)
  other arithmetic  89.3 us (2%)
    gather x14, local copies, waits for them, and re-layouts, sorted_rows(): source_rows[index_list]  2460 us
    dot_general x1, matrix products, attend_back(): jnp.einsum('hrnck,hrncd->hrnkd', grad_scores, query_sorted, preferred_ele...  111 us
    dot_general x1, matrix products, attend_back(): jnp.einsum('hrnck,hrnkd->hrncd', grad_scores, key_window, preferred_eleme...  107 us
    all_gather x1, waiting for transfers between devices, on_device(): lax.all_gather(cot_second.astype(jnp.bfloat16), 'tp', axis=0, tiled=True)  82.9 us
    all_gather x1, waiting for transfers between devices, on_device(): lax.all_gather(grad_in_first.astype(jnp.bfloat16), 'tp', axis=0, tiled=True)  81.1 us
  transfers between devices with their start and end apart: 15, of which 13 were waited for; matrix products, arithmetic and copies ran while one was open for 4% of the time, Pallas kernels for 0%

commit v1 on v0

--- a/solution.py
+++ b/solution.py
@@ -1,14 +1,19 @@
+import functools
+
 import jax
 import jax.numpy as jnp
 from jax import lax
+from jax.experimental import pallas as pl
+from jax.experimental.pallas import tpu as pltpu
 from jax.sharding import PartitionSpec as P
 
 HEAD_DIM = 128
 BLOCK = 64
 
 
-NEG_SELF = -100000.0
-NEG_MASK = -1000000000.0
+SCORE_SCALE = HEAD_DIM ** (-0.5) * 1.4426950408889634
+FLOOR = -1e30
+ALONE = 1e30
 
 
 def normalize(row_values):
@@ -40,152 +45,230 @@
     )
 
 
-def sorted_rows(source, index_all):
-    return jax.vmap(jax.vmap(lambda source_rows, index_list: source_rows[index_list]))(
-        source, index_all
-    )
-
-
-def invert(sort_order):
-    length = sort_order.shape[-1]
-    ranks = jnp.broadcast_to(jnp.arange(length, dtype=jnp.int32), sort_order.shape)
-    return jax.vmap(
-        jax.vmap(
-            lambda index_list, rank_list: jnp.zeros((length,), jnp.int32)
-            .at[index_list]
-            .set(rank_list)
-        )
-    )(sort_order, ranks)
-
-
-def head_major(packed, heads_here):
-    return packed.reshape(packed.shape[0], heads_here, -1).transpose(1, 0, 2)
-
-
-def to_rows(grads_head):
-    return grads_head.transpose(1, 0, 2).reshape(grads_head.shape[1], -1)
-
-
-def windows(blocks):
-    return jnp.concatenate([jnp.roll(blocks, 1, axis=-3), blocks], axis=-2)
-
-
-def unwindow(grad_window):
-    return grad_window[..., BLOCK:, :] + jnp.roll(grad_window[..., :BLOCK, :], -1, axis=-3)
-
-
-def arrange(shared, values_in, sort_order, prefix):
+def bucket_rows(sort_order):
     heads_here, rounds, length = sort_order.shape
     block_count = length // BLOCK
-    queries = head_major(shared, heads_here)
-    query_f = queries.astype(jnp.float32)
-    inv_norm = lax.rsqrt(jnp.mean(query_f * query_f, axis=-1, keepdims=True) + 1e-06)
-    key_rows = (query_f * inv_norm).astype(jnp.bfloat16)
-    values = head_major(values_in, heads_here)
-
-    def spread_sorted(source):
-        widened = jnp.broadcast_to(source[:, None], (heads_here, rounds) + source.shape[1:])
-        return sorted_rows(widened, sort_order).reshape(heads_here, rounds, block_count, BLOCK, -1)
-
-    query_sorted = spread_sorted(queries)
-    key_window = windows(spread_sorted(key_rows))
-    value_window = windows(spread_sorted(values))
-    query_pos = sort_order.reshape(heads_here, rounds, block_count, BLOCK)
-    key_pos = windows(query_pos[..., None])[..., 0]
-    query_at = query_pos[..., :, None]
-    key_at = key_pos[..., None, :]
-    allowed = (key_at < query_at) | (query_at < prefix) & (key_at < prefix)
-    same_token = key_at == query_at
-    raw_scores = jnp.einsum(
-        "hrncd,hrnkd->hrnck", query_sorted, key_window, preferred_element_type=jnp.float32
-    ) * HEAD_DIM ** (-0.5)
-    scores = jnp.where(same_token, NEG_SELF, jnp.where(allowed, raw_scores, NEG_MASK))
-    return (query_f, inv_norm, query_sorted, key_window, value_window, allowed, same_token, scores)
-
-
-def attend(shared, values_in, sort_order, prefix):
-    heads_here, rounds, length = sort_order.shape
-    query_f, inv_norm, query_sorted, key_window, value_window, allowed, same_token, scores = (
-        arrange(shared, values_in, sort_order, prefix)
-    )
-    row_peak = jnp.max(scores, axis=-1, keepdims=True)
-    round_lse = row_peak[..., 0] + jnp.log(jnp.sum(jnp.exp(scores - row_peak), axis=-1))
-    attn_probs = jnp.exp(scores - round_lse[..., None]).astype(jnp.bfloat16)
-    round_out = jnp.einsum(
-        "hrnck,hrnkd->hrncd", attn_probs, value_window, preferred_element_type=jnp.float32
-    )
-    inverse = invert(sort_order)
-    round_out = sorted_rows(round_out.reshape(heads_here, rounds, length, -1), inverse)
-    lse_tokens = sorted_rows(round_lse.reshape(heads_here, rounds, length, 1), inverse)[..., 0]
-    round_peak = jnp.max(lse_tokens, axis=1, keepdims=True)
-    total_lse = round_peak + jnp.log(
-        jnp.sum(jnp.exp(lse_tokens - round_peak), axis=1, keepdims=True)
-    )
-    weight = jnp.exp(lse_tokens - total_lse)
-    merged = jnp.sum(weight[..., None] * round_out, axis=1)
-    return (to_rows(merged).astype(jnp.bfloat16), round_out, weight, round_lse)
-
-
-def attend_back(shared, values_in, sort_order, prefix, round_out, weight, round_lse, grad_packed):
-    heads_here, rounds, length = sort_order.shape
-    block_count = length // BLOCK
-    query_f, inv_norm, query_sorted, key_window, value_window, allowed, same_token, scores = (
-        arrange(shared, values_in, sort_order, prefix)
-    )
-    probs_full = jnp.exp(scores - round_lse[..., None])
-    grad_merged = head_major(grad_packed, heads_here).astype(jnp.float32)
-    merged = jnp.sum(weight[..., None] * round_out, axis=1)
-    grad_lse = weight * jnp.sum(grad_merged[:, None] * (round_out - merged[:, None]), axis=-1)
-    grad_round = (weight[..., None] * grad_merged[:, None]).astype(jnp.bfloat16)
-    grad_round = sorted_rows(grad_round, sort_order).reshape(
-        heads_here, rounds, block_count, BLOCK, -1
-    )
-    grad_lse = sorted_rows(grad_lse[..., None], sort_order).reshape(
-        heads_here, rounds, block_count, BLOCK, 1
-    )
-    grad_probs = jnp.einsum(
-        "hrncd,hrnkd->hrnck", grad_round, value_window, preferred_element_type=jnp.float32
-    )
-    inner_sum = jnp.sum(probs_full * grad_probs, axis=-1, keepdims=True)
-    live = allowed & jnp.logical_not(same_token)
-    grad_scores = jnp.where(live, probs_full * (grad_probs - inner_sum + grad_lse), 0.0).astype(
-        jnp.bfloat16
-    )
-    factor = HEAD_DIM ** (-0.5)
-    grad_query = (
-        jnp.einsum(
-            "hrnck,hrnkd->hrncd", grad_scores, key_window, preferred_element_type=jnp.float32
+    slot_block = (jnp.arange(length, dtype=jnp.int32) // BLOCK).astype(jnp.bfloat16)
+    high = (
+        (sort_order // 128)[:, :, None, :]
+        == jnp.arange(length // 128, dtype=jnp.int32)[None, None, :, None]
+    )
+    low = (sort_order % 128)[..., None] == jnp.arange(128, dtype=jnp.int32)
+    high = jnp.where(high, slot_block, jnp.bfloat16(0))
+    bucket = jnp.einsum(
+        "hras,hrsb->hrab", high, low.astype(jnp.bfloat16), preferred_element_type=jnp.float32
+    )
+    bucket = bucket.reshape(heads_here, rounds, length).astype(jnp.int32)
+    bucket = bucket.transpose(0, 2, 1)[..., None]
+    lanes = jnp.arange(block_count, dtype=jnp.int32)
+    own = lanes == bucket
+    before = lanes == (bucket + block_count - 1) % block_count
+    shape = (heads_here, length, rounds * block_count)
+    seen_by = (own | before).astype(jnp.bfloat16).reshape(shape)
+    return seen_by, own.astype(jnp.bfloat16).reshape(shape)
+
+
+def dot_nt(left, right):
+    return lax.dot_general(
+        left, right, (((1,), (1,)), ((), ())), preferred_element_type=jnp.float32
+    )
+
+
+def unit_rows(rows):
+    inv_norm = lax.rsqrt(jnp.mean(rows * rows, axis=-1, keepdims=True) + 1e-06)
+    return rows * inv_norm, inv_norm
+
+
+def attend_kernel(
+    tile, prefix_ref, q_ref, v_ref, a_ref, b_ref, low_ref, full_ref, lse_ref, key_ref
+):
+    step = pl.program_id(1)
+    prefix = prefix_ref[0]
+
+    @pl.when(step == 0)
+    def _():
+        key_ref[...] = unit_rows(q_ref[...].astype(jnp.float32))[0].astype(jnp.bfloat16)
+
+    own = pl.ds(pl.multiple_of(step * tile, tile), tile)
+    query = q_ref[own, :]
+    seen = a_ref[0, own, :]
+
+    def visit(part, carry, masked):
+        peak, total, acc = carry
+        keys = pl.ds(pl.multiple_of(part * tile, tile), tile)
+        scores = dot_nt(query, key_ref[keys, :]) * SCORE_SCALE
+        count = dot_nt(seen, b_ref[0, keys, :])
+        if masked:
+            row = step * tile + lax.broadcasted_iota(jnp.int32, (tile, tile), 0)
+            col = part * tile + lax.broadcasted_iota(jnp.int32, (tile, tile), 1)
+            allowed = (col < row) | ((row < prefix) & (col < prefix) & (row != col))
+            count = jnp.where(allowed, count, 0.0)
+        scores = jnp.where(count > 0.5, scores, FLOOR)
+        peak_now = jnp.maximum(peak, jnp.max(scores, axis=1, keepdims=True))
+        probs = count * jnp.exp2(scores - peak_now)
+        shrink = jnp.exp2(peak - peak_now)
+        total = total * shrink + jnp.sum(probs, axis=1, keepdims=True)
+        acc = acc * shrink + jnp.dot(
+            probs.astype(jnp.bfloat16), v_ref[keys, :], preferred_element_type=jnp.float32
         )
-        * factor
-    )
-    grad_keywin = (
-        jnp.einsum(
-            "hrnck,hrncd->hrnkd", grad_scores, query_sorted, preferred_element_type=jnp.float32
+        return peak_now, total, acc
+
+    carry = (
+        jnp.full((tile, 1), FLOOR, jnp.float32),
+        jnp.zeros((tile, 1), jnp.float32),
+        jnp.zeros((tile, HEAD_DIM), jnp.float32),
+    )
+    carry = lax.fori_loop(0, step, lambda part, c: visit(part, c, False), carry)
+    ahead = jnp.where(step * tile < prefix, (prefix + tile - 1) // tile, 0)
+    carry = lax.fori_loop(
+        step, jnp.maximum(step + 1, ahead), lambda part, c: visit(part, c, True), carry
+    )
+    peak, total, acc = carry
+    alone = total == 0.0
+    merged = jnp.where(
+        alone, v_ref[own, :].astype(jnp.float32), acc / jnp.where(alone, 1.0, total)
+    )
+    low_ref[...] = merged.astype(jnp.bfloat16)
+    full_ref[...] = merged
+    lse = jnp.where(alone, ALONE, peak + jnp.log2(jnp.where(alone, 1.0, total)))
+    lse_ref[0] = jnp.broadcast_to(lse, (tile, 128)).T[:8]
+
+
+def attend(shared, values, seen_by, own_block, prefix):
+    length, width = shared.shape
+    heads_here = width // HEAD_DIM
+    tile = min(512, length)
+    whole = lambda h, i: (0, h)
+    hot = pl.BlockSpec((1, length, 128), lambda h, i: (h, 0, 0))
+    return pl.pallas_call(
+        functools.partial(attend_kernel, tile),
+        grid=(heads_here, length // tile),
+        in_specs=[
+            pl.BlockSpec(memory_space=pltpu.SMEM),
+            pl.BlockSpec((length, HEAD_DIM), whole),
+            pl.BlockSpec((length, HEAD_DIM), whole),
+            hot,
+            hot,
+        ],
+        out_specs=[
+            pl.BlockSpec((tile, HEAD_DIM), lambda h, i: (i, h)),
+            pl.BlockSpec((tile, HEAD_DIM), lambda h, i: (i, h)),
+            pl.BlockSpec((1, 8, tile), lambda h, i: (h, 0, i)),
+        ],
+        out_shape=[
+            jax.ShapeDtypeStruct((length, width), jnp.bfloat16),
+            jax.ShapeDtypeStruct((length, width), jnp.float32),
+            jax.ShapeDtypeStruct((heads_here, 8, length), jnp.float32),
+        ],
+        scratch_shapes=[pltpu.VMEM((length, HEAD_DIM), jnp.bfloat16)],
+        compiler_params=pltpu.CompilerParams(vmem_limit_bytes=48 * 2**20),
+    )(prefix, shared, values, seen_by, own_block)
+
+
+def attend_back_kernel(
+    tile,
+    prefix_ref,
+    q_ref,
+    v_ref,
+    a_ref,
+    b_ref,
+    full_ref,
+    lse_ref,
+    g_ref,
+    gs_ref,
+    gv_ref,
+    key_ref,
+    dq_ref,
+    dk_ref,
+    dv_ref,
+):
+    step = pl.program_id(1)
+    prefix = prefix_ref[0]
+
+    @pl.when(step == 0)
+    def _():
+        key_ref[...] = unit_rows(q_ref[...].astype(jnp.float32))[0].astype(jnp.bfloat16)
+        dk_ref[...] = jnp.zeros_like(dk_ref)
+        dv_ref[...] = jnp.zeros_like(dv_ref)
+        dq_ref[...] = jnp.zeros_like(dq_ref)
+
+    own = pl.ds(pl.multiple_of(step * tile, tile), tile)
+    query = q_ref[own, :]
+    seen = a_ref[0, own, :]
+    grad = g_ref[own, :]
+    delta = jnp.sum((grad.astype(jnp.float32) * full_ref[...]).T, axis=0, keepdims=True)
+    lse = lse_ref[0, 0:1, :]
+    alone = jnp.where(lse == ALONE, 1.0, 0.0)
+
+    def visit(part, masked):
+        keys = pl.ds(pl.multiple_of(part * tile, tile), tile)
+        key = key_ref[keys, :]
+        scores = dot_nt(key, query) * SCORE_SCALE
+        count = dot_nt(b_ref[0, keys, :], seen)
+        if masked:
+            col = part * tile + lax.broadcasted_iota(jnp.int32, (tile, tile), 0)
+            row = step * tile + lax.broadcasted_iota(jnp.int32, (tile, tile), 1)
+            same = row == col
+            allowed = (col < row) | ((row < prefix) & (col < prefix) & (row != col))
+            count = jnp.where(allowed, count, 0.0)
+        probs = count * jnp.exp2(jnp.minimum(scores - lse, 0.0))
+        grad_scores = probs * (dot_nt(v_ref[keys, :], grad) - delta)
+        if masked:
+            probs = jnp.where(same, alone, probs)
+        grad_scores = grad_scores.astype(jnp.bfloat16)
+        dv_ref[keys, :] += jnp.dot(
+            probs.astype(jnp.bfloat16), grad, preferred_element_type=jnp.float32
         )
-        * factor
-    )
-    grad_valwin = jnp.einsum(
-        "hrnck,hrncd->hrnkd",
-        probs_full.astype(jnp.bfloat16),
-        grad_round,
-        preferred_element_type=jnp.float32,
-    )
-    inverse = invert(sort_order)
-
-    def gather_back(grad_blocks):
-        return jnp.sum(
-            sorted_rows(grad_blocks.reshape(heads_here, rounds, length, -1), inverse), axis=1
-        )
-
-    grad_direct = gather_back(grad_query)
-    grad_keys = gather_back(unwindow(grad_keywin))
-    grad_values = gather_back(unwindow(grad_valwin))
-    grad_total = (
-        grad_direct
-        + inv_norm * grad_keys
-        - query_f * inv_norm**3 * jnp.mean(grad_keys * query_f, axis=-1, keepdims=True)
-    )
-    return (to_rows(grad_total).astype(jnp.bfloat16), to_rows(grad_values).astype(jnp.bfloat16))
+        dk_ref[keys, :] += jnp.dot(grad_scores, query, preferred_element_type=jnp.float32)
+        dq_ref[own, :] += cross(grad_scores, key)
+
+    @pl.loop(0, step)
+    def _(part):
+        visit(part, False)
+
+    ahead = jnp.where(step * tile < prefix, (prefix + tile - 1) // tile, 0)
+
+    @pl.loop(step, jnp.maximum(step + 1, ahead))
+    def _(part):
+        visit(part, True)
+
+    @pl.when(step == pl.num_programs(1) - 1)
+    def _():
+        rows = q_ref[...].astype(jnp.float32)
+        _, inv_norm = unit_rows(rows)
+        factor = HEAD_DIM ** (-0.5)
+        grad_keys = dk_ref[...] * factor
+        inner = jnp.mean(grad_keys * rows, axis=-1, keepdims=True)
+        total = dq_ref[...] * factor + inv_norm * grad_keys - rows * (inv_norm**3 * inner)
+        gs_ref[...] = total.astype(jnp.bfloat16)
+        gv_ref[...] = dv_ref[...].astype(jnp.bfloat16)
+
+
+def attend_back(shared, values, seen_by, own_block, prefix, full, lse, grad_packed):
+    length, width = shared.shape
+    heads_here = width // HEAD_DIM
+    tile = min(512, length)
+    whole = pl.BlockSpec((length, HEAD_DIM), lambda h, i: (0, h))
+    hot = pl.BlockSpec((1, length, 128), lambda h, i: (h, 0, 0))
+    return pl.pallas_call(
+        functools.partial(attend_back_kernel, tile),
+        grid=(heads_here, length // tile),
+        in_specs=[
+            pl.BlockSpec(memory_space=pltpu.SMEM),
+            whole,
+            whole,
+            hot,
+            hot,
+            pl.BlockSpec((tile, HEAD_DIM), lambda h, i: (i, h)),
+            pl.BlockSpec((1, 8, tile), lambda h, i: (h, 0, i)),
+            whole,
+        ],
+        out_specs=[whole, whole],
+        out_shape=[jax.ShapeDtypeStruct((length, width), jnp.bfloat16)] * 2,
+        scratch_shapes=[pltpu.VMEM((length, HEAD_DIM), jnp.bfloat16)]
+        + [pltpu.VMEM((length, HEAD_DIM), jnp.float32)] * 3,
+        compiler_params=pltpu.CompilerParams(vmem_limit_bytes=48 * 2**20),
+    )(prefix, shared, values, seen_by, own_block, full, lse, grad_packed)
 
 
 def cross(left, right):
@@ -213,8 +296,6 @@
     gain_two,
     shift_two,
 ):
-    seq_count = hash_order.shape[0]
-    length = hash_order.shape[3]
     (
         full_shared,
         full_value,
@@ -249,12 +330,8 @@
         jnp.bfloat16
     )
     values = jnp.dot(first_all, full_value, preferred_element_type=jnp.float32).astype(jnp.bfloat16)
-    shared_seq = shared.reshape(seq_count, length, -1)
-    values_seq = values.reshape(seq_count, length, -1)
-    packed, round_out, weight, round_lse = jax.vmap(attend)(
-        shared_seq, values_seq, hash_order, prefix_len
-    )
-    merged_all = packed.reshape(seq_count * length, -1)
+    seen_by, own_block = bucket_rows(hash_order[0])
+    merged_all, merged_full, lse = attend(shared, values, seen_by, own_block, prefix_len)
     out_first = in_first + lax.psum_scatter(
         jnp.dot(merged_all, full_out, preferred_element_type=jnp.float32).astype(jnp.bfloat16),
         "tp",
@@ -327,18 +404,9 @@
         jnp.bfloat16
     )
     grad_weight_out = cross(merged_all, grad_branch)
-    grad_shared, grad_value = jax.vmap(attend_back)(
-        shared_seq,
-        values_seq,
-        hash_order,
-        prefix_len,
-        round_out,
-        weight,
-        round_lse,
-        grad_merged.reshape(seq_count, length, -1),
-    )
-    grad_shared = grad_shared.reshape(seq_count * length, -1)
-    grad_value = grad_value.reshape(seq_count * length, -1)
+    grad_shared, grad_value = attend_back(
+        shared, values, seen_by, own_block, prefix_len, merged_full, lse, grad_merged
+    )
     grad_weight_shared = cross(first_all, grad_shared)
     grad_weight_value = cross(first_all, grad_value)
     part_shared = jnp.dot(grad_shared, back_shared.T, preferred_element_type=jnp.float32)

time: 3840 us -> 1050 us (0.27)
  local copies, waits for them, and re-layouts: 2570 us -> 16.5 us
  matrix products: 360 us -> 97.6 us
  other arithmetic: 89.3 us -> 28.1 us
  Pallas kernels: 0 us -> 54.1 us
    gather x14 -> x0, local copies, waits for them, and re-layouts: 2460 us -> none  [sorted_rows(): source_rows[index_list]]
    dot_general x6 -> x1, matrix products: 262 us -> 2.34 us  [bucket_rows(): jnp.einsum('hras,hrsb->hrab', high, low.astype(jnp.bfloat16), preferred_e...]
    unnamed x121 -> x73, local copies, waits for them, and re-layouts: 73.6 us -> 10.7 us
    pallas_call x0 -> x2, Pallas kernels: none -> 54.1 us  [the longest x1 29.3 us: attend_back(): pl.pallas_call(functools.partial(attend_back_kernel, tile), grid=(heads_h...]
    all_gather x1, waiting for transfers between devices: 0.02 us -> 40.1 us  [on_device(): first_all = lax.all_gather(first_low, 'tp', axis=0, tiled=True)]
  transfers between devices with their start and end apart: 15 -> 15, of which waited for: 13 -> 13; matrix products, arithmetic and copies ran while one was open for 4% -> 8% of each run, Pallas kernels for 0% -> 0%
where the time goes in v1:
time: 1050 us; the launch traced here: 1040 us
  waiting for transfers between devices  678 us (65%)
  blocking collectives  148 us (14%)
  matrix products  97.6 us (9%)
  Pallas kernels  54.1 us (5%)
  other arithmetic  28.1 us (3%)
  between operations  18 us (2%)
  local copies, waits for them, and re-layouts  16.5 us (2%)
    all_gather x1, waiting for transfers between devices, on_device(): lax.all_gather(cot_second.astype(jnp.bfloat16), 'tp', axis=0, tiled=True)  82.3 us
    all_gather x1, waiting for transfers between devices, on_device(): lax.all_gather(grad_in_first.astype(jnp.bfloat16), 'tp', axis=0, tiled=True)  81.1 us
    reduce_scatter x1, waiting for transfers between devices, on_device(): lax.psum_scatter(jnp.dot(grad_pre, back_up.T, preferred_element_type=jnp....  75.2 us
    all_gather x1, waiting for transfers between devices, on_device(): second_all = lax.all_gather(second_low, 'tp', axis=0, tiled=True)  67.8 us
    unnamed x2, blocking collectives  58.6 us
    reduce_scatter x1, waiting for transfers between devices, on_device(): lax.psum_scatter(jnp.dot(merged_all, full_out, preferred_element_type=jnp...  57.6 us
    reduce_scatter x1, waiting for transfers between devices, on_device(): lax.psum_scatter(grad_weight_up, 'fsdp', scatter_dimension=0, tiled=True)  55.7 us
    reduce_scatter x1, waiting for transfers between devices, on_device(): lax.psum_scatter(grad_weight_down, 'fsdp', scatter_dimension=1, tiled=True)  50.7 us
  transfers between devices with their start and end apart: 15, of which 13 were waited for; matrix products, arithmetic and copies ran while one was open for 8% of the time, Pallas kernels for 0%

profile of v1, /device:TPU:0, one launch (start us, length us, event | category | flops | bytes accessed | tf_op | source)
XLA Modules:
  0.0 1041.8 jit_solution(15206571852816984015)
XLA Ops:
  12.0 10.2 all-gather
  22.2 8.7 all-gather.1
  33.2 2.3 fusion.25
  39.3 2.1 copy.36
  41.4 10.2 all_gather.55
  51.6 10.7 %all_gather.56 = bf16[1024,256]{1,0:T(8,128)(2,1)} all-gather(bf16[128,256]{1,0:T(8,128)(2,1)S(1)} %copy-done.20), channel_id=1, replica_groups=mesh['fsdp'=8,'tp'=4] {'fsdp'}, dimensions={0}, use_global_device_ids=true | all-gather | bytes 589824 | tf_op jit(solution)/shard_map/all_gather | solution.py:313
  62.3 10.3 all_gather.57
  73.4 40.1 %all-gather.13.cloned.1.call-done = bf16[2048,1024]{1,0:T(8,128)(2,1)} async-done(((bf16[512,1024]{1,0:T(8,128)(2,1)}), bf16[2048,1024]{1,0:T(8,128)(2,1)}) %all-gather.13.cloned.1.call-update) | async-done | bytes 4194320 | tf_op jit(solution)/shard_map/all_gather | solution.py:328
  113.5 3.7 convolution_convert_fusion.4.v_ref
  118.6 24.8 %shard_map.280 = (bf16[2048,256]{1,0:T(8,128)(2,1)S(1)}, f32[2048,256]{1,0:T(8,128)}, f32[2,8,2048]{2,1,0:T(8,128)S(1)}) custom-call(s32[1]{0:T(128)S(6)} %copy.38.prefix_ref, bf16[2048,256]{1,0:T(8,128)(2,1)S(1)} %convolution_convert_fusion.5.q_ref, bf16[2048,256]{1,0:T(8,128)(2,1)S(1)} %convolution_convert_fusion.4.v_ref, ...), custom_call_target="tpu_custom_call" | custom-call | tf_op jit(solution)/shard_map/pallas_call | solution.py:143
  144.3 3.2 convolution_convert_fusion
  148.2 10.8 %all-gather.2 = bf16[8,1,128]{2,1,0:T(2,128)(2,1)S(1)} all-gather(bf16[1,1,128]{2,1,0:T(2,128)(2,1)S(1)} %bitcast.86), channel_id=1, replica_groups=mesh['fsdp'=8,'tp'=4] {'fsdp'}, dimensions={0}, use_global_device_ids=true | all-gather | bytes 2304 | tf_op jit(solution)/shard_map/all_gather | solution.py:320
  159.1 7.5 all-gather.3
  166.6 57.6 %reduce-scatter.10.cloned.1.call-done = bf16[512,1024]{1,0:T(8,128)(2,1)} async-done(((bf16[2048,1024]{1,0:T(8,128)(2,1)}), bf16[512,1024]{1,0:T(8,128)(2,1)}) %reduce-scatter.10.cloned.1.call-update) | async-done | bytes 1048592 | tf_op jit(solution)/shard_map/reduce_scatter | solution.py:335
  224.2 2.1 fusion.42
  229.7 3.6 fusion.44
  233.4 9.1 all-gather.4
  242.5 67.8 %all-gather.15.cloned.1.call-done = bf16[2048,1024]{1,0:T(8,128)(2,1)} async-done(((bf16[512,1024]{1,0:T(8,128)(2,1)}), bf16[2048,1024]{1,0:T(8,128)(2,1)}) %all-gather.15.cloned.1.call-update) | async-done | bytes 4194320 | tf_op jit(solution)/shard_map/all_gather | solution.py:345
  310.3 10.6 %fusion.45 = f32[2048,1024]{1,0:T(8,128)} fusion(bf16[2048,1024]{1,0:T(8,128)(2,1)} %all-gather.15.cloned.1.call-done, bf16[1024,1024]{1,0:T(8,128)(2,1)} %all-gather.17.cloned.1.call-done), kind=kOutput, calls=%fused_computation.95 | convolution fusion | flops 4294967296 | bytes 14680064 | tf_op jit(solution)/shard_map/dot_general | solution.py:346
  320.9 17.9 %all-gather.19.cloned.1.call-done = bf16[1024,1024]{1,0:T(8,128)(2,1)} async-done(((bf16[1024,128]{1,0:T(8,128)(2,1)}), bf16[1024,1024]{1,0:T(8,128)(2,1)}) %all-gather.19.cloned.1.call-update) | async-done | bytes 2097168 | tf_op jit(solution)/shard_map/all_gather | solution.py:316
  338.8 82.3 %all-gather.21.cloned.1.call-done = bf16[2048,1024]{1,0:T(8,128)(2,1)} async-done(((bf16[512,1024]{1,0:T(8,128)(2,1)}), bf16[2048,1024]{1,0:T(8,128)(2,1)}) %all-gather.21.cloned.1.call-update) | async-done | bytes 4194320 | tf_op jit(solution)/shard_map/all_gather | solution.py:385
  421.1 13.3 %convert_reduce_fusion = (f32[1024]{0:T(1024)S(1)}, bf16[2048,1024]{1,0:T(8,128)(2,1)S(1)}) fusion(f32[2048,1024]{1,0:T(8,128)} %fusion.45, f32[1024]{0:T(1024)S(1)} %bitcast.81, bf16[2048,1024]{1,0:T(8,128)(2,1)} %all-gather.21.cloned.1.call-done, bf16[1024,1024]{1,0:T(8,128)(2,1)} %all-gather.19.cloned.1.call-done), kind=kOutput, calls=%fused_computation.9 | convolution fusion | flops 4341103616 | bytes 18882560 | tf_op jit(solution)/shard_map/dot_general | solution.py:386
  434.4 2.0 copy-done.32
  436.4 6.3 convolution_convert_fusion.1
  442.9 75.2 %reduce-scatter.14.cloned.1.call-done = bf16[512,1024]{1,0:T(8,128)(2,1)} async-done(((bf16[2048,1024]{1,0:T(8,128)(2,1)}), bf16[512,1024]{1,0:T(8,128)(2,1)}) %reduce-scatter.14.cloned.1.call-update) | async-done | bytes 1048592 | tf_op jit(solution)/shard_map/reduce_scatter | solution.py:392
  518.1 3.0 fusion.23
  521.1 4.3 fusion.40
  525.5 81.1 %all-gather.23.cloned.1.call-done = bf16[2048,1024]{1,0:T(8,128)(2,1)} async-done(((bf16[512,1024]{1,0:T(8,128)(2,1)}), bf16[2048,1024]{1,0:T(8,128)(2,1)}) %all-gather.23.cloned.1.call-update) | async-done | bytes 4194320 | tf_op jit(solution)/shard_map/all_gather | solution.py:402
  606.6 4.6 convolution_convert_fusion.3.g_ref
  611.2 29.3 %shard_map.281 = (bf16[2048,256]{1,0:T(8,128)(2,1)S(1)}, bf16[2048,256]{1,0:T(8,128)(2,1)S(1)}) custom-call(s32[1]{0:T(128)S(6)} %copy.38.prefix_ref, bf16[2048,256]{1,0:T(8,128)(2,1)S(1)} %copy-done.2, bf16[2048,256]{1,0:T(8,128)(2,1)S(1)} %convolution_convert_fusion.4.v_ref, bf16[2,2048,128]{2,1,0:T(8,128)(2,1)S(1)} %or_convert_fusion.a_ref, ...), custom_call_target="tpu_custom_call" | custom-call | tf_op jit(solution)/shard_map/pallas_call | solution.py:253
  641.9 3.4 add_convert_fusion
  646.9 11.1 %convolution_convert_fusion.2 = bf16[2048,1024]{1,0:T(8,128)(2,1)} fusion(bf16[1024,1024]{1,0:T(8,128)(2,1)S(1)} %copy-done.29, f32[2048,1024]{1,0:T(8,128)} %fusion.45, f32[1024]{0:T(1024)S(1)} %bitcast.82), kind=kOutput, calls=%fused_computation.17 | convolution fusion | flops 4318035968 | bytes 14684160 | tf_op jit(solution)/shard_map/dot_general | solution.py:353
  658.1 12.7 %fusion.39 = f32[1024,1024]{1,0:T(8,128)} fusion(bf16[2048,1024]{1,0:T(8,128)(2,1)} %all-gather.21.cloned.1.call-done, f32[2048,1024]{1,0:T(8,128)} %fusion.45, f32[1024]{0:T(1024)S(1)} %bitcast.83), kind=kOutput, calls=%fused_computation.90 | convolution fusion | flops 4315938816 | bytes 16781312 | tf_op jit(solution)/shard_map/dot_general | solution.py:275
  671.2 10.1 fusion.50
  682.5 4.4 fusion.49
  687.0 4.5 fusion.48
  691.7 4.7 fusion.47
  697.0 12.1 %all-gather.5 = bf16[8,1,128]{2,1,0:T(2,128)(2,1)S(1)} all-gather(bf16[1,1,128]{2,1,0:T(2,128)(2,1)S(1)} %bitcast.89), channel_id=1, replica_groups=mesh['fsdp'=8,'tp'=4] {'fsdp'}, dimensions={0}, use_global_device_ids=true | all-gather | bytes 2304 | tf_op jit(solution)/shard_map/all_gather | solution.py:322
  709.8 14.0 %all-reduce = f32[1024]{0:T(1024)S(1)} all-reduce(f32[1024]{0:T(1024)S(1)} %get-tuple-element.50), channel_id=10, replica_groups=mesh['fsdp'=8,'tp'=4] {'fsdp'}, use_global_device_ids=true, to_apply=%region_17.18.clone | all-reduce | flops 1024 | bytes 8192
  724.3 2.2 fusion.24
  726.5 44.7 %all-reduce.6 = (f32[1024]{0:T(1024)S(1)}, f32[1024]{0:T(1024)S(1)}, f32[1024]{0:T(1024)S(1)}, f32[1024]{0:T(1024)S(1)}, f32[1024]{0:T(1024)S(1)}) all-reduce(f32[1024]{0:T(1024)S(1)} %get-tuple-element.44, f32[1024]{0:T(1024)S(1)} %get-tuple-element.27, ...), channel_id=12, replica_groups=mesh['fsdp'=8,'tp'=4] {'fsdp','tp'}, use_global_device_ids=true, to_apply=%region_20.21.clone | all-reduce | flops 5120 | bytes 40960
  774.1 29.2 %reduce-scatter.12.cloned.1.call-done = bf16[512,1024]{1,0:T(8,128)(2,1)} async-done(((bf16[2048,1024]{1,0:T(8,128)(2,1)}), bf16[512,1024]{1,0:T(8,128)(2,1)}) %reduce-scatter.12.cloned.1.call-update) | async-done | bytes 1048592 | tf_op jit(solution)/shard_map/reduce_scatter | solution.py:352
  803.2 5.0 fusion.17
  808.2 50.7 %reduce-scatter.26.cloned.1.call-done = f32[1024,128]{1,0:T(8,128)} async-done(((f32[1024,1024]{1,0:T(8,128)}), f32[1024,128]{1,0:T(8,128)}) %reduce-scatter.26.cloned.1.call-update) | async-done | bytes 524304 | tf_op jit(solution)/shard_map/reduce_scatter | solution.py:427
  858.9 55.7 %reduce-scatter.24.cloned.1.call-done = f32[128,1024]{1,0:T(8,128)} async-done(((f32[1024,1024]{1,0:T(8,128)}), f32[128,1024]{1,0:T(8,128)}) %reduce-scatter.24.cloned.1.call-update) | async-done | bytes 524304 | tf_op jit(solution)/shard_map/reduce_scatter | solution.py:425
  914.6 39.8 %reduce-scatter.22.cloned.1.call-done = f32[256,128]{1,0:T(8,128)} async-done(((f32[256,1024]{1,0:T(8,128)}), f32[256,128]{1,0:T(8,128)}) %reduce-scatter.22.cloned.1.call-update) | async-done | bytes 131088 | tf_op jit(solution)/shard_map/reduce_scatter | solution.py:424
  954.3 39.8 %reduce-scatter.20.cloned.1.call-done = f32[128,256]{1,0:T(8,128)} async-done(((f32[1024,256]{1,0:T(8,128)}), f32[128,256]{1,0:T(8,128)}) %reduce-scatter.20.cloned.1.call-update) | async-done | bytes 131088 | tf_op jit(solution)/shard_map/reduce_scatter | solution.py:423
  994.1 39.6 %reduce-scatter.18.cloned.1.call-done = f32[128,256]{1,0:T(8,128)} async-done(((f32[1024,256]{1,0:T(8,128)}), f32[128,256]{1,0:T(8,128)}) %reduce-scatter.18.cloned.1.call-update) | async-done | bytes 131088 | tf_op jit(solution)/shard_map/reduce_scatter | solution.py:422
  (135 shorter events, 25.5 us)
Async XLA Ops:
  8.0 22.9 %copy-start.11 = (f32[512,1024]{1,0:T(8,128)S(1)}, f32[512,1024]{1,0:T(8,128)}, u32[]{:S(2)}) copy-start(f32[512,1024]{1,0:T(8,128)} %param.18) | copy-start | bytes 6291460
  8.0 3.9 copy-start.22
  8.0 14.2 %copy-start.23 = (bf16[128]{0:T(256)(128)(2,1)S(1)}, bf16[128]{0:T(256)(128)(2,1)}, u32[]{:S(2)}) copy-start(bf16[128]{0:T(256)(128)(2,1)} %param.31) | copy-start | bytes 772
  8.0 25.1 %copy-start.18 = (s32[1,2,4,2048]{3,2,1,0:T(4,128)S(1)}, s32[1,2,4,2048]{3,2,1,0:T(4,128)}, u32[]{:S(2)}) copy-start(s32[1,2,4,2048]{3,2,1,0:T(4,128)} %param.21) | copy-start | bytes 196612
  8.1 105.4 %all-gather.13.cloned.1.call-start = ((), (), s32[]{:S(2)}) async-start(), calls=%async_computation.9 | async-start | bytes 5242880 | tf_op jit(solution)/shard_map/all_gather | solution.py:328
  32.3 191.9 %reduce-scatter.10.cloned.1.call-start = ((), (), s32[]{:S(2)}) async-start(), calls=%async_computation.10 | async-start | bytes 5242880 | tf_op jit(solution)/shard_map/reduce_scatter | solution.py:335
  37.7 3.7 copy-start.19
  37.7 13.9 %copy-start.20 = (bf16[128,256]{1,0:T(8,128)(2,1)S(1)}, bf16[128,256]{1,0:T(8,128)(2,1)}, u32[]{:S(2)}) copy-start(bf16[128,256]{1,0:T(8,128)(2,1)} %param.24) | copy-start | bytes 196612
  37.7 24.6 %copy-start.21 = (bf16[256,128]{1,0:T(8,128)(2,1)S(1)}, bf16[256,128]{1,0:T(8,128)(2,1)}, u32[]{:S(2)}) copy-start(bf16[256,128]{1,0:T(8,128)(2,1)} %param.25) | copy-start | bytes 196612
  41.4 31.6 %copy-start.13 = (s32[2,2048,128]{2,1,0:T(8,128)S(1)}, s32[2,2048,128]{2,1,0:T(8,128)}, u32[]{:S(2)}) copy-start(s32[2,2048,128]{2,1,0:T(8,128)} %copy.37) | copy-start | bytes 6291460
  73.0 45.5 %copy-start = (bf16[2,2048,128]{2,1,0:T(8,128)(2,1)}, bf16[2,2048,128]{2,1,0:T(8,128)(2,1)S(1)}, u32[]{:S(2)}) copy-start(bf16[2,2048,128]{2,1,0:T(8,128)(2,1)S(1)} %get-tuple-element.42.b_ref) | copy-start | bytes 3145732
  113.5 3.7 copy-start.15
  113.5 3.8 copy-start.28
  117.3 27.1 %copy-start.17 = (bf16[256,1024]{1,0:T(8,128)(2,1)S(1)}, bf16[256,1024]{1,0:T(8,128)(2,1)}, u32[]{:S(2)}) copy-start(bf16[256,1024]{1,0:T(8,128)(2,1)} %all_gather.57) | copy-start | bytes 1572868
  118.5 24.8 %copy-start.1 = (bf16[2048,256]{1,0:T(8,128)(2,1)}, bf16[2048,256]{1,0:T(8,128)(2,1)S(1)}, u32[]{:S(2)}) copy-start(bf16[2048,256]{1,0:T(8,128)(2,1)S(1)} %convolution_convert_fusion.5.q_ref) | copy-start | bytes 3145732
  143.4 1.0 copy-start.3
  147.6 0.7 copy-start.24
  147.6 11.5 %copy-start.25 = (bf16[128]{0:T(256)(128)(2,1)S(1)}, bf16[128]{0:T(256)(128)(2,1)}, u32[]{:S(2)}) copy-start(bf16[128]{0:T(256)(128)(2,1)} %param.33) | copy-start | bytes 772
  147.6 94.9 %all-gather.17.cloned.1.call-start = ((), (), s32[]{:S(2)}) async-start(), calls=%async_computation.12 | async-start | bytes 2359296 | tf_op jit(solution)/shard_map/all_gather | solution.py:315
  148.2 162.1 %all-gather.15.cloned.1.call-start = ((), (), s32[]{:S(2)}) async-start(), calls=%async_computation.11 | async-start | bytes 5242880 | tf_op jit(solution)/shard_map/all_gather | solution.py:345
  226.4 1.3 copy-start.9
  227.7 5.7 copy-start.26
  229.1 109.7 %all-gather.19.cloned.1.call-start = ((), (), s32[]{:S(2)}) async-start(), calls=%async_computation.13 | async-start | bytes 2359296 | tf_op jit(solution)/shard_map/all_gather | solution.py:316
  229.7 191.4 %all-gather.21.cloned.1.call-start = ((), (), s32[]{:S(2)}) async-start(), calls=%async_computation.15 | async-start | bytes 5242880 | tf_op jit(solution)/shard_map/all_gather | solution.py:385
  233.3 284.8 %reduce-scatter.14.cloned.1.call-start = ((), (), s32[]{:S(2)}) async-start(), calls=%async_computation.16 | async-start | bytes 5242880 | tf_op jit(solution)/shard_map/reduce_scatter | solution.py:392
  421.1 15.3 %copy-start.30 = (bf16[1024,1024]{1,0:T(8,128)(2,1)S(1)}, bf16[1024,1024]{1,0:T(8,128)(2,1)}, u32[]{:S(2)}) copy-start(bf16[1024,1024]{1,0:T(8,128)(2,1)} %all-gather.17.cloned.1.call-done) | copy-start | bytes 6291460
  434.4 2.0 copy-start.32
  442.7 164.0 %all-gather.23.cloned.1.call-start = ((), (), s32[]{:S(2)}) async-start(), calls=%async_computation.17 | async-start | bytes 5242880 | tf_op jit(solution)/shard_map/all_gather | solution.py:402
  518.1 3.0 copy-start.10
  525.4 85.8 %copy-start.2 = (bf16[2048,256]{1,0:T(8,128)(2,1)S(1)}, bf16[2048,256]{1,0:T(8,128)(2,1)}, u32[]{:S(2)}) copy-start(bf16[2048,256]{1,0:T(8,128)(2,1)} %copy-done.1) | copy-start | bytes 3145732
  525.4 198.9 %reduce-scatter.16.cloned.1.call-start = ((), (), s32[]{:S(2)}) async-start(), calls=%async_computation.18 | async-start | bytes 5242880 | tf_op jit(solution)/shard_map/reduce_scatter | solution.py:414
  611.2 29.3 %copy-start.16 = (bf16[1024,256]{1,0:T(8,128)(2,1)S(1)}, bf16[1024,256]{1,0:T(8,128)(2,1)}, u32[]{:S(2)}) copy-start(bf16[1024,256]{1,0:T(8,128)(2,1)} %all_gather.55) | copy-start | bytes 1572868
  640.5 1.3 copy-start.5
  640.5 1.3 copy-start.7
  640.5 1.4 copy-start.14
  645.3 1.6 copy-start.29
  645.3 157.9 %reduce-scatter.12.cloned.1.call-start = ((), (), s32[]{:S(2)}) async-start(), calls=%async_computation.14 | async-start | bytes 5242880 | tf_op jit(solution)/shard_map/reduce_scatter | solution.py:352
  658.0 200.8 %reduce-scatter.26.cloned.1.call-start = ((), (), s32[]{:S(2)}) async-start(), calls=%async_computation.23 | async-start | bytes 4718592 | tf_op jit(solution)/shard_map/reduce_scatter | solution.py:427
  670.9 243.7 %reduce-scatter.24.cloned.1.call-start = ((), (), s32[]{:S(2)}) async-start(), calls=%async_computation.22 | async-start | bytes 4718592 | tf_op jit(solution)/shard_map/reduce_scatter | solution.py:425
  681.3 1.2 copy-start.4
  681.3 5.7 copy-start.8
  681.3 273.0 %reduce-scatter.22.cloned.1.call-start = ((), (), s32[]{:S(2)}) async-start(), calls=%async_computation.21 | async-start | bytes 1179648 | tf_op jit(solution)/shard_map/reduce_scatter | solution.py:424
  687.0 4.7 copy-start.6
  687.0 307.2 %reduce-scatter.20.cloned.1.call-start = ((), (), s32[]{:S(2)}) async-start(), calls=%async_computation.20 | async-start | bytes 1179648 | tf_op jit(solution)/shard_map/reduce_scatter | solution.py:423
  691.6 4.8 copy-start.31
  691.6 5.4 copy-start.27
  691.6 32.7 %copy-start.12 = (f32[512,1024]{1,0:T(8,128)S(1)}, f32[512,1024]{1,0:T(8,128)}, u32[]{:S(2)}) copy-start(f32[512,1024]{1,0:T(8,128)} %param.18) | copy-start | bytes 6291460
  691.6 342.2 %reduce-scatter.18.cloned.1.call-start = ((), (), s32[]{:S(2)}) async-start(), calls=%async_computation.19 | async-start | bytes 1179648 | tf_op jit(solution)/shard_map/reduce_scatter | solution.py:422
Sparse Core Ops, SparseCore 0:
  32.4 81.0 all-gather.12
  147.7 76.4 reduce-scatter.9
  442.8 75.2 reduce-scatter.13
  645.5 77.1 reduce-scatter.15
  724.9 78.3 reduce-scatter.11
  807.0 51.8 reduce-scatter.25
  863.2 51.3 reduce-scatter.23
  918.3 35.9 reduce-scatter.21
  958.1 35.9 reduce-scatter.19
  997.7 35.9 reduce-scatter.17
Sparse Core Ops, SparseCore 1:
  150.1 27.4 all-gather.16
  229.2 81.1 all-gather.14
  312.2 26.5 all-gather.18
  340.4 80.6 all-gather.20
  525.5 81.1 all-gather.22

commit v2 on v1

--- a/solution.py
+++ b/solution.py
@@ -296,159 +296,108 @@
     gain_two,
     shift_two,
 ):
-    (
-        full_shared,
-        full_value,
-        full_out,
-        full_up,
-        full_down,
-        full_bias,
-        gain_a,
-        shift_a,
-        gain_b,
-        shift_b,
-        bias_last,
-    ) = (
-        lax.all_gather(weight_shared, "fsdp", axis=0, tiled=True),
-        lax.all_gather(weight_value, "fsdp", axis=0, tiled=True),
-        lax.all_gather(weight_out, "fsdp", axis=1, tiled=True),
-        lax.all_gather(weight_up, "fsdp", axis=0, tiled=True),
-        lax.all_gather(weight_down, "fsdp", axis=1, tiled=True),
-        lax.all_gather(bias_up, "fsdp", axis=0, tiled=True),
-        lax.all_gather(gain_one, "fsdp", axis=0, tiled=True),
-        lax.all_gather(shift_one, "fsdp", axis=0, tiled=True),
-        lax.all_gather(gain_two, "fsdp", axis=0, tiled=True),
-        lax.all_gather(shift_two, "fsdp", axis=0, tiled=True),
-        lax.all_gather(bias_down, "fsdp", axis=0, tiled=True),
-    )
+    rows, model = in_first.shape
+    split = weight_shared.shape[0]
+    heads_wide = weight_shared.shape[1]
+    hidden_wide = weight_up.shape[1]
+    groups = lax.axis_size("tp")
+    everyone = ("tp", "fsdp")
+
+    def collect(shard):
+        whole = lax.all_gather(shard, everyone, axis=0, tiled=True)
+        return whole.reshape(groups, -1, shard.shape[1])
+
+    small = jnp.stack([gain_one, shift_one, gain_two, shift_two, bias_down, bias_up])
+    small = lax.all_gather(small, everyone, axis=0, tiled=False).astype(jnp.float32)
+    small = small.reshape(groups, -1, 6, split)
+    gain_a, shift_a, gain_b, shift_b, bias_last = (
+        small[0, :, which].reshape(model) for which in range(5)
+    )
+    full_bias = small[:, :, 5].reshape(groups, 1, hidden_wide)
+    full_pair = collect(jnp.concatenate([weight_shared, weight_value], axis=1))
+    full_out = collect(weight_out.T)
+    full_up = collect(weight_up)
+    full_down = collect(weight_down.T)
+
+    def dots(spec, left, right):
+        return jnp.einsum(spec, left, right, preferred_element_type=jnp.float32)
+
+    def exchange(parts):
+        return lax.all_to_all(parts, "tp", 0, 0, tiled=True)
+
+    seen_by, own_block = bucket_rows(hash_order[0])
     norm_one, factor_one = normalize(in_second)
-    first_low = (norm_one * gain_a.astype(jnp.float32) + shift_a.astype(jnp.float32)).astype(
-        jnp.bfloat16
-    )
-    first_all = lax.all_gather(first_low, "tp", axis=0, tiled=True)
-    shared = jnp.dot(first_all, full_shared, preferred_element_type=jnp.float32).astype(
-        jnp.bfloat16
-    )
-    values = jnp.dot(first_all, full_value, preferred_element_type=jnp.float32).astype(jnp.bfloat16)
-    seen_by, own_block = bucket_rows(hash_order[0])
-    merged_all, merged_full, lse = attend(shared, values, seen_by, own_block, prefix_len)
-    out_first = in_first + lax.psum_scatter(
-        jnp.dot(merged_all, full_out, preferred_element_type=jnp.float32).astype(jnp.bfloat16),
-        "tp",
-        scatter_dimension=0,
-        tiled=True,
-    ).astype(jnp.float32)
+    first_low = (norm_one * gain_a + shift_a).astype(jnp.bfloat16)
+    pair = dots("rd,tdc->trc", first_low, full_pair).astype(jnp.bfloat16)
+    pair = exchange(pair).reshape(groups * rows, 2 * heads_wide)
+    shared, values = pair[:, :heads_wide], pair[:, heads_wide:]
+    merged_low, merged_full, lse = attend(shared, values, seen_by, own_block, prefix_len)
+    merged = exchange(merged_low.reshape(groups, rows, heads_wide))
+    out_first = in_first + dots("trc,tdc->rd", merged, full_out)
     norm_two, factor_two = normalize(out_first)
-    second_low = (norm_two * gain_b.astype(jnp.float32) + shift_b.astype(jnp.float32)).astype(
-        jnp.bfloat16
-    )
-    second_all = lax.all_gather(second_low, "tp", axis=0, tiled=True)
-    pre_act = jnp.dot(second_all, full_up, preferred_element_type=jnp.float32) + full_bias.astype(
-        jnp.float32
-    )
+    second_low = (norm_two * gain_b + shift_b).astype(jnp.bfloat16)
+    pre_act = dots("rd,tdh->trh", second_low, full_up) + full_bias
     hidden = gelu_tanh(pre_act).astype(jnp.bfloat16)
-    out_second = (
-        in_second
-        + lax.psum_scatter(
-            jnp.dot(hidden, full_down, preferred_element_type=jnp.float32).astype(jnp.bfloat16),
-            "tp",
-            scatter_dimension=0,
-            tiled=True,
-        ).astype(jnp.float32)
-        + bias_last.astype(jnp.float32)
-    )
-    (
-        back_shared,
-        back_value,
-        back_out,
-        back_up,
-        back_down,
-        back_bias,
-        gain_c,
-        shift_c,
-        gain_d,
-        shift_d,
-        bias_again,
-    ) = (
-        lax.all_gather(weight_shared, "fsdp", axis=0, tiled=True),
-        lax.all_gather(weight_value, "fsdp", axis=0, tiled=True),
-        lax.all_gather(weight_out, "fsdp", axis=1, tiled=True),
-        lax.all_gather(weight_up, "fsdp", axis=0, tiled=True),
-        lax.all_gather(weight_down, "fsdp", axis=1, tiled=True),
-        lax.all_gather(bias_up, "fsdp", axis=0, tiled=True),
-        lax.all_gather(gain_one, "fsdp", axis=0, tiled=True),
-        lax.all_gather(shift_one, "fsdp", axis=0, tiled=True),
-        lax.all_gather(gain_two, "fsdp", axis=0, tiled=True),
-        lax.all_gather(shift_two, "fsdp", axis=0, tiled=True),
-        lax.all_gather(bias_down, "fsdp", axis=0, tiled=True),
-    )
-    grad_up_all = lax.all_gather(cot_second.astype(jnp.bfloat16), "tp", axis=0, tiled=True)
-    grad_hidden = jnp.dot(grad_up_all, back_down.T, preferred_element_type=jnp.float32)
+    out_second = in_second + dots("trh,tdh->rd", hidden, full_down) + bias_last
+    grad_up = cot_second.astype(jnp.bfloat16)
+    grad_hidden = dots("rd,tdh->trh", grad_up, full_down)
     grad_pre = (grad_hidden * gelu_slope(pre_act)).astype(jnp.bfloat16)
-    grad_weight_down = cross(hidden, grad_up_all)
-    grad_weight_up = cross(second_all, grad_pre)
-    grad_bias_up = jnp.sum(grad_pre, axis=0, dtype=jnp.float32)
-    grad_bias_down = jnp.sum(cot_second, axis=0)
-    grad_second = lax.psum_scatter(
-        jnp.dot(grad_pre, back_up.T, preferred_element_type=jnp.float32).astype(jnp.bfloat16),
-        "tp",
-        scatter_dimension=0,
-        tiled=True,
-    ).astype(jnp.float32)
+    grad_second = dots("trh,tdh->rd", grad_pre, full_up)
     part_first, grad_gain_two, grad_shift_two = norm_backward(
-        grad_second, norm_two, factor_two, gain_d.astype(jnp.float32)
+        grad_second, norm_two, factor_two, gain_b
     )
     grad_in_first = cot_first + part_first
-    grad_branch = lax.all_gather(grad_in_first.astype(jnp.bfloat16), "tp", axis=0, tiled=True)
-    grad_merged = jnp.dot(grad_branch, back_out.T, preferred_element_type=jnp.float32).astype(
-        jnp.bfloat16
-    )
-    grad_weight_out = cross(merged_all, grad_branch)
+    grad_branch = grad_in_first.astype(jnp.bfloat16)
+
+    def total(partial):
+        flat = partial.astype(jnp.bfloat16).reshape(-1, partial.shape[-1])
+        return lax.psum_scatter(flat, everyone, scatter_dimension=0, tiled=True).astype(
+            jnp.float32
+        )
+
+    summed_down = total(dots("rd,trh->tdh", grad_up, hidden)).T
+    summed_up = total(dots("rd,trh->tdh", second_low, grad_pre))
+    grad_merged = dots("rd,tdc->trc", grad_branch, full_out).astype(jnp.bfloat16)
+    grad_merged = exchange(grad_merged).reshape(groups * rows, heads_wide)
+    summed_out = total(dots("rd,trc->tdc", grad_branch, merged)).T
     grad_shared, grad_value = attend_back(
         shared, values, seen_by, own_block, prefix_len, merged_full, lse, grad_merged
     )
-    grad_weight_shared = cross(first_all, grad_shared)
-    grad_weight_value = cross(first_all, grad_value)
-    part_shared = jnp.dot(grad_shared, back_shared.T, preferred_element_type=jnp.float32)
-    part_value = jnp.dot(grad_value, back_value.T, preferred_element_type=jnp.float32)
-    grad_first = lax.psum_scatter(
-        (part_shared + part_value).astype(jnp.bfloat16), "tp", scatter_dimension=0, tiled=True
-    ).astype(jnp.float32)
+    grad_pair = jnp.concatenate([grad_shared, grad_value], axis=1)
+    grad_pair = exchange(grad_pair.reshape(groups, rows, 2 * heads_wide))
+    summed_pair = total(dots("rd,trc->tdc", first_low, grad_pair))
+    grad_first = dots("trc,tdc->rd", grad_pair, full_pair)
     part_second, grad_gain_one, grad_shift_one = norm_backward(
-        grad_first, norm_one, factor_one, gain_c.astype(jnp.float32)
+        grad_first, norm_one, factor_one, gain_a
     )
     grad_in_second = cot_second + part_second
-    summed_shared, summed_value, summed_out, summed_up, summed_bias, summed_down = (
-        lax.psum_scatter(grad_weight_shared, "fsdp", scatter_dimension=0, tiled=True),
-        lax.psum_scatter(grad_weight_value, "fsdp", scatter_dimension=0, tiled=True),
-        lax.psum_scatter(grad_weight_out, "fsdp", scatter_dimension=1, tiled=True),
-        lax.psum_scatter(grad_weight_up, "fsdp", scatter_dimension=0, tiled=True),
-        lax.psum_scatter(grad_bias_up, "fsdp", scatter_dimension=0, tiled=True),
-        lax.psum_scatter(grad_weight_down, "fsdp", scatter_dimension=1, tiled=True),
-    )
-    norm_gain_a, norm_shift_a, norm_gain_b, norm_shift_b, norm_bias = (
-        lax.psum_scatter(grad_gain_one, ("fsdp", "tp"), scatter_dimension=0, tiled=True),
-        lax.psum_scatter(grad_shift_one, ("fsdp", "tp"), scatter_dimension=0, tiled=True),
-        lax.psum_scatter(grad_gain_two, ("fsdp", "tp"), scatter_dimension=0, tiled=True),
-        lax.psum_scatter(grad_shift_two, ("fsdp", "tp"), scatter_dimension=0, tiled=True),
-        lax.psum_scatter(grad_bias_down, ("fsdp", "tp"), scatter_dimension=0, tiled=True),
-    )
+    grad_bias_up = jnp.sum(grad_pre, axis=1, dtype=jnp.float32)
+    vectors = [
+        jnp.sum(cot_second, axis=0),
+        grad_gain_one,
+        grad_shift_one,
+        grad_gain_two,
+        grad_shift_two,
+    ]
+    piece = split // groups
+    vectors = [v.reshape(-1, groups, piece).transpose(1, 0, 2) for v in vectors]
+    vectors = jnp.concatenate([grad_bias_up.reshape(groups, -1, split)] + vectors, axis=2)
+    vectors = lax.psum_scatter(
+        vectors.reshape(-1, split + 5 * piece), everyone, scatter_dimension=0, tiled=True
+    )[0]
+    tails = [vectors[split + which * piece : split + (which + 1) * piece] for which in range(5)]
     return (
         out_first,
         out_second,
         grad_in_first,
         grad_in_second,
-        summed_shared,
-        summed_value,
+        summed_pair[:, :heads_wide],
+        summed_pair[:, heads_wide:],
         summed_out,
         summed_up,
-        summed_bias,
+        vectors[:split],
         summed_down,
-        norm_bias,
-        norm_gain_a,
-        norm_shift_a,
-        norm_gain_b,
-        norm_shift_b,
+        *tails,
     )
 
 

time: 1050 us -> 995 us (0.948)
  waiting for transfers between devices: 678 us -> 588 us
  local copies, waits for them, and re-layouts: 16.5 us -> 54.4 us
  other arithmetic: 28.1 us -> 11.6 us
  blocking collectives: 148 us -> 135 us
  matrix products: 97.6 us -> 110 us
  starting transfers between devices: 1.26 us -> 13.2 us
    reduce_scatter x9 -> x3, waiting for transfers between devices: 388 us -> 221 us  [total(): lax.psum_scatter(flat, everyone, scatter_dimension=0, tiled=True)]
    all_gather x6 -> x4, waiting for transfers between devices: 289 us -> 129 us  [collect(): whole = lax.all_gather(shard, everyone, axis=0, tiled=True)]
    unnamed x15 -> x9, waiting for transfers between devices: 1.25 us -> 147 us
    all_to_all x0 -> x3, waiting for transfers between devices: none -> 90.9 us  [exchange(): return lax.all_to_all(parts, 'tp', 0, 0, tiled=True)]
    all_to_all x0 -> x1, blocking collectives: none -> 52.4 us  [exchange(): return lax.all_to_all(parts, 'tp', 0, 0, tiled=True)]
    all_gather x9 -> x1, blocking collectives: 89.7 us -> 43.4 us  [on_device(): lax.all_gather(small, everyone, axis=0, tiled=False).astype(jnp.float32)]
    unnamed x2 -> x1, blocking collectives: 58.6 us -> 38.8 us
    all_gather x0 -> x2, local copies, waits for them, and re-layouts: none -> 16.2 us  [collect(): whole = lax.all_gather(shard, everyone, axis=0, tiled=True)]
  transfers between devices with their start and end apart: 15 -> 11, of which waited for: 13 -> 9; matrix products, arithmetic and copies ran while one was open for 8% -> 12% of each run, Pallas kernels for 0% -> 6%
where the time goes in v2:
time: 995 us; the launch traced here: 986 us
  waiting for transfers between devices  588 us (59%)
  blocking collectives  135 us (14%)
  matrix products  110 us (11%)
  Pallas kernels  58.9 us (6%)
  local copies, waits for them, and re-layouts  54.4 us (5%)
  between operations  15.6 us (2%)
  starting transfers between devices  13.2 us (1%)
  other arithmetic  11.6 us (1%)
    reduce_scatter x3, waiting for transfers between devices, total(): lax.psum_scatter(flat, everyone, scatter_dimension=0, tiled=True)  221 us
    unnamed x9, waiting for transfers between devices  147 us
    all_gather x4, waiting for transfers between devices, collect(): whole = lax.all_gather(shard, everyone, axis=0, tiled=True)  129 us
    dot_general x12, matrix products, dots(): return jnp.einsum(spec, left, right, preferred_element_type=jnp.float32)  107 us
    all_to_all x3, waiting for transfers between devices, exchange(): return lax.all_to_all(parts, 'tp', 0, 0, tiled=True)  90.9 us
    all_to_all x1, blocking collectives, exchange(): return lax.all_to_all(parts, 'tp', 0, 0, tiled=True)  52.4 us
    all_gather x1, blocking collectives, on_device(): lax.all_gather(small, everyone, axis=0, tiled=False).astype(jnp.float32)  43.4 us
    unnamed x1, blocking collectives  38.8 us
  transfers between devices with their start and end apart: 11, of which 9 were waited for; matrix products, arithmetic and copies ran while one was open for 12% of the time, Pallas kernels for 6%

profile of v2, /device:TPU:0, one launch (start us, length us, event | category | flops | bytes accessed | tf_op | source)
XLA Modules:
  0.0 985.6 jit_solution(16708903916980193399)
XLA Ops:
  7.3 1.7 pad_maximum_fusion.1
  11.1 1.8 reduce_sum.126
  12.9 43.4 %all-gather.1 = bf16[32,6,128]{2,1,0:T(8,128)(2,1)S(1)} all-gather(bf16[1,6,128]{2,1,0:T(8,128)(2,1)S(1)} %bitcast.227), channel_id=2, replica_groups=mesh['fsdp'=8,'tp'=4] {'tp','fsdp'}, dimensions={0}, use_global_device_ids=true | all-gather | bytes 50688 | tf_op jit(solution)/shard_map/all_gather | solution.py:311
  56.7 19.5 %all-gather.7.cloned.1.call-done = bf16[4096,512]{1,0:T(8,128)(2,1)} async-done(((bf16[128,512]{1,0:T(8,128)(2,1)}), bf16[4096,512]{1,0:T(8,128)(2,1)}) %all-gather.7.cloned.1.call-update) | async-done | bytes 4194320 | tf_op jit(solution)/shard_map/all_gather | solution.py:307
  76.3 6.1 convert_bitcast_fusion.2
  82.4 4.6 all-to-all-start
  87.8 2.3 fusion.15
  90.2 1.6 eq.80
  91.7 1.9 copy.78
  93.8 1.6 eq.83
  95.4 2.9 copy.79
  98.7 1.5 copy-done.8
  100.6 43.2 %all-to-all-done = bf16[4,512,512]{1,2,0:T(8,128)(2,1)} async-done(((bf16[4,512,512]{1,2,0:T(8,128)(2,1)}), bf16[4,512,512]{1,2,0:T(8,128)(2,1)}, u32[]{:S(2)}, u32[]{:S(2)}) %all-to-all-start) | async-done | bytes 2097184 | tf_op jit(solution)/shard_map/all_to_all | solution.py:326
  143.8 4.1 copy.77
  147.9 1.7 fusion.46
  149.6 26.9 %shard_map.280 = (bf16[2048,256]{1,0:T(8,128)(2,1)S(1)}, f32[2048,256]{1,0:T(8,128)}, f32[2,8,2048]{2,1,0:T(8,128)S(1)}) custom-call(s32[1]{0:T(128)S(6)} %copy.115.prefix_ref, bf16[2048,256]{1,0:T(8,128)(2,1)S(1)} %get-tuple-element.83.q_ref, bf16[2048,256]{1,0:T(8,128)(2,1)S(1)} %get-tuple-element.82.v_ref, ...), custom_call_target="tpu_custom_call" | custom-call | tf_op jit(solution)/shard_map/pallas_call | solution.py:143
  177.5 3.8 all-to-all-start.1
  181.4 4.1 copy.80
  185.5 28.8 %all-to-all-done.1 = bf16[4,512,256]{2,1,0:T(8,128)(2,1)S(1)} async-done(((bf16[4,512,256]{2,1,0:T(8,128)(2,1)}), bf16[4,512,256]{2,1,0:T(8,128)(2,1)S(1)}, u32[]{:S(2)}, u32[]{:S(2)}) %all-to-all-start.1) | async-done | bytes 1048608 | tf_op jit(solution)/shard_map/all_to_all | solution.py:326
  214.3 3.6 fusion.49
  219.6 27.4 %all-gather.11.cloned.1.call-done = bf16[4096,1024]{1,0:T(8,128)(2,1)} async-done(((bf16[128,1024]{1,0:T(8,128)(2,1)}), bf16[4096,1024]{1,0:T(8,128)(2,1)}) %all-gather.11.cloned.1.call-update) | async-done | bytes 8388624 | tf_op jit(solution)/shard_map/all_gather | solution.py:307
  246.9 11.9 %fusion.40 = f32[512,4,1024]{2,0,1:T(8,128)} fusion(bf16[4,1024,1024]{2,1,0:T(8,128)(2,1)} %bitcast.239, f32[512,1024]{1,0:T(8,128)} %copy-done.6, f32[1024]{0:T(1024)S(1)} %bitcast.229, f32[1024]{0:T(1024)S(1)} %bitcast.220, f32[512]{0:T(512)S(1)} %add_rsqrt_fusion, f32[512]{0:T(512)S(1)} %broadcast_multiply_fusion.4), kind=kOutput, calls=%fused_computation.112 | convolution fusion | flops 4297588736 | bytes 18886656 | tf_op jit(solution)/shard_map/rd,tdh->trh/dot_general | solution.py:323
  258.8 81.7 %all-gather.13.cloned.1.call-done = bf16[4096,1024]{0,1:T(8,128)(2,1)} async-done(((bf16[128,1024]{0,1:T(8,128)(2,1)}), bf16[4096,1024]{0,1:T(8,128)(2,1)}) %all-gather.13.cloned.1.call-update) | async-done | bytes 8388624 | tf_op jit(solution)/shard_map/all_gather | solution.py:307
  340.5 12.0 %copy.81 = bf16[4096,1024]{1,0:T(8,128)(2,1)} copy(bf16[4096,1024]{0,1:T(8,128)(2,1)} %all-gather.13.cloned.1.call-done) | data formatting | bytes 16777216 | tf_op jit(solution)/shard_map/all_gather | solution.py:307
  352.5 12.9 %convert_reduce_fusion = (f32[4,1024]{1,0:T(4,128)S(1)}, bf16[4,512,1024]{2,1,0:T(8,128)(2,1)S(1)}) fusion(f32[512,4,1024]{2,0,1:T(8,128)} %fusion.40, f32[4,1024]{1,0:T(4,128)S(1)} %bitcast.224, bf16[4,1024,1024]{2,1,0:T(8,128)(2,1)} %bitcast.193, f32[512,1024]{1,0:T(8,128)} %param.20), kind=kOutput, calls=%fused_computation.10 | convolution fusion | flops 4341624832 | bytes 23101440 | tf_op jit(solution)/shard_map/rd,tdh->trh/dot_general | solution.py:323
  365.5 20.1 %fusion.10 = (f32[1024]{0:T(1024)S(1)}, f32[512]{0:T(512)S(1)}, f32[512]{0:T(512)S(1)}, f32[1024]{0:T(1024)S(1)}, f32[512,1024,1]{1,0,2:T(8,128)S(1)}) fusion(f32[512,1024]{1,0:T(8,128)S(1)} %copy-done.7, f32[512]{0:T(512)S(1)} %add_rsqrt_fusion, f32[512]{0:T(512)S(1)} %broadcast_multiply_fusion.4, f32[1024]{0:T(1024)S(1)} %bitcast.221, ...), kind=kOutput, calls=%fused_computation.26 | convolution fusion | flops 4299682816 | bytes 16797696 | tf_op jit(solution)/shard_map/trh,tdh->rd/dot_general | solution.py:323
  386.4 1.3 copy-done.10
  387.7 2.2 fusion.14
  389.9 4.3 all-to-all-start.2
  394.2 4.2 convert_bitcast_fusion.1
  398.4 3.9 copy.85
  402.4 18.9 %all-to-all-done.2 = bf16[4,512,256]{2,1,0:T(8,128)(2,1)} async-done(((bf16[4,512,256]{2,1,0:T(8,128)(2,1)}), bf16[4,512,256]{2,1,0:T(8,128)(2,1)}, u32[]{:S(2)}, u32[]{:S(2)}) %all-to-all-start.2) | async-done | bytes 1048608 | tf_op jit(solution)/shard_map/all_to_all | solution.py:326
  421.4 32.0 %shard_map.281 = (bf16[2048,256]{1,0:T(8,128)(2,1)S(1)}, bf16[2048,256]{1,0:T(8,128)(2,1)S(1)}) custom-call(s32[1]{0:T(128)S(6)} %copy.115.prefix_ref, bf16[2048,256]{1,0:T(8,128)(2,1)S(1)} %copy-done.2, bf16[2048,256]{1,0:T(8,128)(2,1)S(1)} %get-tuple-element.82.v_ref, bf16[2,2048,128]{2,1,0:T(8,128)(2,1)S(1)} %or_convert_fusion.a_ref, ...), custom_call_target="tpu_custom_call" | custom-call | tf_op jit(solution)/shard_map/pallas_call | solution.py:253
  453.5 52.4 %all_to_all.20 = bf16[4,512,512]{2,1,0:T(8,128)(2,1)S(1)} all-to-all(bf16[4,512,512]{2,1,0:T(8,128)(2,1)S(1)} %bitcast.199), channel_id=1, replica_groups=mesh['fsdp'=8,'tp'=4] {'tp'}, dimensions={0} | all-to-all | bytes 4194304 | tf_op jit(solution)/shard_map/all_to_all | solution.py:326
  506.0 1.3 copy-done.11
  507.3 4.5 convert_bitcast_fusion
  511.8 6.2 copy.83
  518.1 12.4 %convolution_convert_fusion = bf16[4,1024,1024]{1,2,0:T(8,128)(2,1)} fusion(f32[512,1024]{1,0:T(8,128)} %param.20, f32[512,4,1024]{2,0,1:T(8,128)} %fusion.40, f32[4,1024]{1,0:T(4,128)S(1)} %bitcast.225), kind=kOutput, calls=%fused_computation.14 | convolution fusion | flops 4320657408 | bytes 18890752 | tf_op jit(solution)/shard_map/rd,trh->tdh/dot_general | solution.py:323
  530.7 11.2 %convolution_convert_fusion.1 = bf16[4,1024,1024]{1,2,0:T(8,128)(2,1)} fusion(bf16[4,512,1024]{2,1,0:T(8,128)(2,1)} %copy-done.22, f32[512,1024]{1,0:T(8,128)} %copy-done.6, f32[1024]{0:T(1024)S(1)} %bitcast.230, f32[1024]{0:T(1024)S(1)} %bitcast.223, f32[512]{0:T(512)S(1)} %add_rsqrt_fusion, f32[512]{0:T(512)S(1)} %broadcast_multiply_fusion.4), kind=kOutput, calls=%fused_computation.15 | convolution fusion | flops 4301783040 | bytes 14692352 | tf_op jit(solution)/shard_map/rd,trh->tdh/dot_general | solution.py:323
  543.3 12.6 %fusion.11 = f32[512,1024]{1,0:T(8,128)} fusion(f32[512,1024]{1,0:T(8,128)S(1)} %copy-done.5, bf16[4,1024,1024]{2,1,0:T(8,128)(2,1)} %bitcast.194, f32[1024]{0:T(1024)S(1)} %bitcast.228, f32[512,4,1024]{2,0,1:T(8,128)} %fusion.40, f32[4,1024]{1,0:T(4,128)S(1)} %bitcast.226), kind=kOutput, calls=%fused_computation.28 | convolution fusion | flops 4316987392 | bytes 20992000 | tf_op jit(solution)/shard_map/trh,tdh->rd/dot_general | solution.py:323
  557.5 5.8 fusion.9
  563.3 2.1 fusion.45
  565.8 38.8 %all-reduce = f32[32,288]{1,0:T(8,128)S(1)} all-reduce(f32[32,288]{1,0:T(8,128)S(1)} %concatenate.30), channel_id=6, replica_groups=mesh['fsdp'=8,'tp'=4] {'tp','fsdp'}, use_global_device_ids=true, to_apply=%region_17.18.clone | all-reduce | flops 9216 | bytes 73728
  607.0 75.8 %reduce-scatter.7.cloned.1.call-done = bf16[128,512]{1,0:T(8,128)(2,1)} async-done(((bf16[4096,512]{1,0:T(8,128)(2,1)}), bf16[128,512]{1,0:T(8,128)(2,1)}) %reduce-scatter.7.cloned.1.call-update) | async-done | bytes 131088 | tf_op jit(solution)/shard_map/reduce_scatter | solution.py:354
  682.7 1.6 fusion.47
  684.3 145.3 %reduce-scatter.13.cloned.1.call-done = bf16[128,1024]{1,0:T(8,128)(2,1)} async-done(((bf16[4096,1024]{1,0:T(8,128)(2,1)}), bf16[128,1024]{1,0:T(8,128)(2,1)}) %reduce-scatter.13.cloned.1.call-update) | async-done | bytes 262160
  831.6 145.0 %reduce-scatter.11.cloned.1.call-done = bf16[128,1024]{1,0:T(8,128)(2,1)} async-done(((bf16[4096,1024]{1,0:T(8,128)(2,1)}), bf16[128,1024]{1,0:T(8,128)(2,1)}) %reduce-scatter.11.cloned.1.call-update) | async-done | bytes 262160 | tf_op jit(solution)/shard_map/reduce_scatter | solution.py:354
  976.5 1.8 convert_element_type.106
  (103 shorter events, 15.4 us)
Async XLA Ops:
  7.2 49.1 %copy-start.4 = (f32[512,1024]{1,0:T(8,128)S(1)}, f32[512,1024]{1,0:T(8,128)}, u32[]{:S(2)}) copy-start(f32[512,1024]{1,0:T(8,128)} %param.18) | copy-start | bytes 6291460
  7.2 5.6 copy-start.15
  7.2 5.6 copy-start.16
  7.2 5.6 copy-start.17
  7.2 5.6 copy-start.18
  7.2 5.6 copy-start.19
  7.2 5.6 copy-start.20
  7.3 69.0 %all-gather.7.cloned.1.call-start = ((), (), s32[]{:S(2)}) async-start(), calls=%async_computation.8 | async-start | bytes 4325376 | tf_op jit(solution)/shard_map/all_gather | solution.py:307
  9.0 172.4 %all-gather.9.cloned.1.call-start = ((), (), s32[]{:S(2)}) async-start(), calls=%async_computation.9 | async-start | bytes 2162688 | tf_op jit(solution)/shard_map/all_gather | solution.py:307
  9.7 237.2 %all-gather.11.cloned.1.call-start = ((), (), s32[]{:S(2)}) async-start(), calls=%async_computation.10 | async-start | bytes 8650752 | tf_op jit(solution)/shard_map/all_gather | solution.py:307
  10.5 330.0 %all-gather.13.cloned.1.call-start = ((), (), s32[]{:S(2)}) async-start(), calls=%async_computation.11 | async-start | bytes 8650752 | tf_op jit(solution)/shard_map/all_gather | solution.py:307
  82.4 5.3 copy-start.14
  82.4 61.4 %all-to-all-start = ((bf16[4,512,512]{1,2,0:T(8,128)(2,1)}), bf16[4,512,512]{1,2,0:T(8,128)(2,1)}, u32[]{:S(2)}, u32[]{:S(2)}) async-start(bf16[4,512,512]{1,2,0:T(8,128)(2,1)} %convert_bitcast_fusion.2), calls=%async_computation | async-start | bytes 4194304 | tf_op jit(solution)/shard_map/all_to_all | solution.py:326
  98.2 2.0 copy-start.8
  98.6 51.0 %copy-start = (bf16[2,2048,128]{2,1,0:T(8,128)(2,1)}, bf16[2,2048,128]{2,1,0:T(8,128)(2,1)S(1)}, u32[]{:S(2)}) copy-start(bf16[2,2048,128]{2,1,0:T(8,128)(2,1)S(1)} %get-tuple-element.78.b_ref) | copy-start | bytes 3145732
  149.6 26.9 %copy-start.1 = (bf16[2048,256]{1,0:T(8,128)(2,1)}, bf16[2048,256]{1,0:T(8,128)(2,1)S(1)}, u32[]{:S(2)}) copy-start(bf16[2048,256]{1,0:T(8,128)(2,1)S(1)} %get-tuple-element.83.q_ref) | copy-start | bytes 3145732
  176.5 1.0 copy-start.3
  177.5 36.8 %all-to-all-start.1 = ((bf16[4,512,256]{2,1,0:T(8,128)(2,1)}), bf16[4,512,256]{2,1,0:T(8,128)(2,1)S(1)}, u32[]{:S(2)}, u32[]{:S(2)}) async-start(bf16[4,512,256]{2,1,0:T(8,128)(2,1)} %bitcast.191), calls=%async_computation.1 | async-start | bytes 2097152 | tf_op jit(solution)/shard_map/all_to_all | solution.py:326
  217.9 1.3 copy-start.6
  352.5 12.9 %copy-start.7 = (f32[512,1024]{1,0:T(8,128)S(1)}, f32[512,1024]{1,0:T(8,128)}, u32[]{:S(2)}) copy-start(f32[512,1024]{1,0:T(8,128)} %copy-done.6) | copy-start | bytes 6291460
  365.5 20.1 %copy-start.22 = (bf16[4,512,1024]{2,1,0:T(8,128)(2,1)}, bf16[4,512,1024]{2,1,0:T(8,128)(2,1)S(1)}, u32[]{:S(2)}) copy-start(bf16[4,512,1024]{2,1,0:T(8,128)(2,1)S(1)} %get-tuple-element.103) | copy-start | bytes 12582916
  365.5 20.1 %copy-start.9 = (f32[512,1024]{1,0:T(8,128)S(1)}, f32[512,1024]{1,0:T(8,128)}, u32[]{:S(2)}) copy-start(f32[512,1024]{1,0:T(8,128)} %param.19) | copy-start | bytes 6291460
  385.6 2.0 copy-start.12
  386.4 1.3 copy-start.10
  389.9 31.5 %all-to-all-start.2 = ((bf16[4,512,256]{2,1,0:T(8,128)(2,1)}), bf16[4,512,256]{2,1,0:T(8,128)(2,1)}, u32[]{:S(2)}, u32[]{:S(2)}) async-start(bf16[4,512,256]{2,1,0:T(8,128)(2,1)} %fusion.14), calls=%async_computation.2 | async-start | bytes 2097152 | tf_op jit(solution)/shard_map/all_to_all | solution.py:326
  394.2 161.7 %reduce-scatter.9.cloned.1.call-start = ((), (), s32[]{:S(2)}) async-start(), calls=%async_computation.13 | async-start | bytes 2162688 | tf_op jit(solution)/shard_map/reduce_scatter | solution.py:354
  402.4 19.0 %copy-start.2 = (bf16[2048,256]{1,0:T(8,128)(2,1)S(1)}, bf16[2048,256]{1,0:T(8,128)(2,1)}, u32[]{:S(2)}) copy-start(bf16[2048,256]{1,0:T(8,128)(2,1)} %copy-done.1) | copy-start | bytes 3145732
  402.4 280.3 %reduce-scatter.7.cloned.1.call-start = ((), (), s32[]{:S(2)}) async-start(), calls=%async_computation.12 | async-start | bytes 4325376 | tf_op jit(solution)/shard_map/reduce_scatter | solution.py:354
  453.5 53.8 %copy-start.5 = (f32[512,1024]{1,0:T(8,128)S(1)}, f32[512,1024]{1,0:T(8,128)}, u32[]{:S(2)}) copy-start(f32[512,1024]{1,0:T(8,128)} %param.18) | copy-start | bytes 6291460
  506.0 1.3 copy-start.11
  518.0 311.6 %reduce-scatter.13.cloned.1.call-start = ((), (), s32[]{:S(2)}) async-start(), calls=%async_computation.15 | async-start | bytes 8650752
  530.5 446.1 %reduce-scatter.11.cloned.1.call-start = ((), (), s32[]{:S(2)}) async-start(), calls=%async_computation.14 | async-start | bytes 8650752 | tf_op jit(solution)/shard_map/reduce_scatter | solution.py:354
  541.9 0.7 copy-start.21
  557.5 5.8 copy-start.13
Sparse Core Ops, SparseCore 0:
  11.5 64.6 all-gather.6
  79.1 74.2 all-gather.8
  156.2 90.6 all-gather.10
  249.6 90.8 all-gather.12
  402.5 140.6 reduce-scatter.8
  545.4 137.2 reduce-scatter.6
  685.1 144.4 reduce-scatter.12
  832.0 144.5 reduce-scatter.10

commit v3 on v2

--- a/solution.py
+++ b/solution.py
@@ -1,4 +1,5 @@
 import functools
+import math
 
 import jax
 import jax.numpy as jnp
@@ -271,6 +272,218 @@
     )(prefix, shared, values, seen_by, own_block, full, lse, grad_packed)
 
 
+MESH = pl.DeviceIdType.MESH
+
+
+def bit_of(index, which):
+    return lax.rem(lax.div(index, 2**which), 2)
+
+
+def across(index, which):
+    return index + (1 - 2 * bit_of(index, which)) * 2**which
+
+
+def mirrored(index, steps):
+    return sum(((index >> k) & 1) << (steps - 1 - k) for k in range(steps))
+
+
+def add_rows(out, left, right, lead, rows):
+    tall = 32 if rows % 32 == 0 else (16 if rows % 16 == 0 else rows)
+    parts = rows // tall
+
+    @pl.loop(0, math.prod(lead) * parts)
+    def _(flat):
+        here = pl.ds(pl.multiple_of(lax.rem(flat, parts) * tall, tall), tall)
+        flat = lax.div(flat, parts)
+        index = []
+        for size in reversed(lead):
+            index.insert(0, lax.rem(flat, size))
+            flat = lax.div(flat, size)
+        summed = left[(*index, here)].astype(jnp.float32) + right[(*index, here)].astype(
+            jnp.float32
+        )
+        out[(*index, here)] = summed.astype(out.dtype)
+
+
+class Summed:
+    @staticmethod
+    def scratch(groups, peers, rows, cols, dtype):
+        count, half = peers // 2, groups // 2
+        steps = count.bit_length() - 1
+        shapes = []
+        for _ in range(2):
+            shapes += [pltpu.VMEM((half, count, rows, cols), dtype)] * 2
+            shapes += [pltpu.VMEM((half, count >> (k + 1), rows, cols), dtype) for k in range(steps)]
+        shapes += [pltpu.VMEM((groups, rows, cols), dtype)] * 2
+        copies = 2 * count + 2 * steps + groups
+        shapes += [pltpu.SemaphoreType.DMA((copies,))] * 2
+        shapes.append(pltpu.SemaphoreType.DMA((2 * count,)))
+        return shapes
+
+    def __init__(self, groups, source, out, scratch):
+        scratch = list(scratch)
+        self.groups, self.half, self.source, self.out = groups, groups // 2, source, out
+        self.own, self.landings = [], []
+        self.count = scratch[0].shape[1]
+        self.steps = self.count.bit_length() - 1
+        for _ in range(2):
+            self.own.append(scratch.pop(0))
+            self.landings.append([scratch.pop(0) for _ in range(1 + self.steps)])
+        self.packed, self.arrived, self.send, self.recv, self.local = scratch
+        self.rows = self.packed.shape[1]
+        self.f, self.t = lax.axis_index("fsdp"), lax.axis_index("tp")
+        self.waiting = {}
+
+    def remote(self, name, slot, source, target, device):
+        copy = pltpu.make_async_remote_copy(
+            src_ref=source,
+            dst_ref=target,
+            send_sem=self.send.at[slot],
+            recv_sem=self.recv.at[slot],
+            device_id=device,
+            device_id_type=MESH,
+        )
+        copy.start()
+        self.waiting.setdefault(name, []).append(copy)
+
+    def settle(self, name):
+        for copy in self.waiting.pop(name):
+            copy.wait()
+
+    def place(self, side, block):
+        return block if side == 0 else mirrored(block, self.steps)
+
+    def begin(self):
+        core = bit_of(self.f, 0)
+        for block in range(self.count):
+            for side in range(2):
+                part = pl.ds(side * self.half, self.half)
+                place = self.place(side, block)
+                slot = side * self.count + block
+                self.remote(
+                    "core",
+                    slot,
+                    self.source.at[part, 2 * block + 1 - core],
+                    self.landings[side][0].at[:, place],
+                    {"fsdp": across(self.f, 0)},
+                )
+                copy = pltpu.make_async_copy(
+                    self.source.at[part, 2 * block + core],
+                    self.own[side].at[:, place],
+                    self.local.at[slot],
+                )
+                copy.start()
+                self.waiting.setdefault("core", []).append(copy)
+
+    def core_step(self):
+        self.settle("core")
+        for side in range(2):
+            own = self.own[side]
+            add_rows(own, own, self.landings[side][0], own.shape[:2], self.rows)
+        self.current = list(self.own)
+
+    def along(self, side, step):
+        return 1 + (self.steps - 1 - step if side == 0 else step)
+
+    def send_step(self, step):
+        for side in range(2):
+            which = self.along(side, step)
+            left = self.count >> (step + 1)
+            gone = (1 - bit_of(self.f, which)) * left
+            self.remote(
+                step,
+                2 * self.count + 2 * step + side,
+                self.current[side].at[:, pl.ds(gone, left)],
+                self.landings[side][1 + step],
+                {"fsdp": across(self.f, which)},
+            )
+
+    def add_step(self, step):
+        self.settle(step)
+        left = self.count >> (step + 1)
+        for side in range(2):
+            kept = bit_of(self.f, self.along(side, step)) * left
+            kept = self.current[side].at[:, pl.ds(kept, left)]
+            landed = self.landings[side][1 + step]
+            if left > 1:
+                add_rows(landed, kept, landed, landed.shape[:2], self.rows)
+            else:
+                out = self.packed.at[pl.ds(side * self.half, self.half)]
+                add_rows(out, kept.at[:, 0], landed.at[:, 0], (self.half,), self.rows)
+            self.current[side] = landed
+
+    def send_groups(self):
+        for ahead in range(1, self.groups):
+            target = lax.rem(self.t + ahead, self.groups)
+            self.remote(
+                "groups",
+                2 * self.count + 2 * self.steps + ahead,
+                self.packed.at[target],
+                self.arrived.at[ahead],
+                {"tp": target},
+            )
+
+    def finish(self):
+        self.settle("groups")
+        rows = self.rows
+        tall = 16 if rows % 16 == 0 else rows
+
+        @pl.loop(0, rows // tall)
+        def _(part):
+            here = pl.ds(pl.multiple_of(part * tall, tall), tall)
+            total = self.packed[self.t, here].astype(jnp.float32)
+            for ahead in range(1, self.groups):
+                total += self.arrived[ahead, here].astype(jnp.float32)
+            self.out[here] = total
+
+
+def greet(groups, peers):
+    f, t = lax.axis_index("fsdp"), lax.axis_index("tp")
+    partners = [{"fsdp": across(f, which)} for which in range(peers.bit_length() - 1)]
+    partners += [{"tp": lax.rem(t + ahead, groups)} for ahead in range(1, groups)]
+    barrier = pltpu.get_barrier_semaphore()
+    for partner in partners:
+        pl.semaphore_signal(barrier, inc=1, device_id=partner, device_id_type=MESH)
+    pl.semaphore_wait(barrier, len(partners))
+
+
+def sum_kernel(groups, peers, count, per, *refs):
+    sources, outs, scratch = refs[:count], refs[count : 2 * count], refs[2 * count :]
+    arrays = [
+        Summed(groups, sources[k], outs[k], scratch[k * per : (k + 1) * per]) for k in range(count)
+    ]
+    greet(groups, peers)
+    for array in arrays:
+        array.begin()
+    for array in arrays:
+        array.core_step()
+        array.send_step(0)
+    for step in range(arrays[0].steps):
+        for array in arrays:
+            array.add_step(step)
+            if step + 1 < array.steps:
+                array.send_step(step + 1)
+            else:
+                array.send_groups()
+    for array in arrays:
+        array.finish()
+
+
+def sum_everywhere(groups, peers, arrays):
+    blocks = [a.reshape(groups, peers, -1, a.shape[-1]) for a in arrays]
+    scratch = [Summed.scratch(groups, peers, *b.shape[2:], b.dtype) for b in blocks]
+    return pl.pallas_call(
+        functools.partial(sum_kernel, groups, peers, len(blocks), len(scratch[0])),
+        in_specs=[pl.BlockSpec(memory_space=pl.ANY)] * len(blocks),
+        out_specs=[pl.BlockSpec(memory_space=pltpu.VMEM)] * len(blocks),
+        out_shape=[jax.ShapeDtypeStruct(b.shape[2:], jnp.float32) for b in blocks],
+        scratch_shapes=sum(scratch, []),
+        compiler_params=pltpu.CompilerParams(
+            collective_id=1, has_side_effects=True, vmem_limit_bytes=56 * 2**20
+        ),
+    )(*blocks)
+
+
 def cross(left, right):
     return lax.dot_general(
         left, right, (((0,), (0,)), ((), ())), preferred_element_type=jnp.float32
@@ -349,23 +562,17 @@
     grad_in_first = cot_first + part_first
     grad_branch = grad_in_first.astype(jnp.bfloat16)
 
-    def total(partial):
-        flat = partial.astype(jnp.bfloat16).reshape(-1, partial.shape[-1])
-        return lax.psum_scatter(flat, everyone, scatter_dimension=0, tiled=True).astype(
-            jnp.float32
-        )
-
-    summed_down = total(dots("rd,trh->tdh", grad_up, hidden)).T
-    summed_up = total(dots("rd,trh->tdh", second_low, grad_pre))
+    partial_down = dots("rd,trh->tdh", grad_up, hidden).astype(jnp.bfloat16)
+    partial_up = dots("rd,trh->tdh", second_low, grad_pre).astype(jnp.bfloat16)
     grad_merged = dots("rd,tdc->trc", grad_branch, full_out).astype(jnp.bfloat16)
     grad_merged = exchange(grad_merged).reshape(groups * rows, heads_wide)
-    summed_out = total(dots("rd,trc->tdc", grad_branch, merged)).T
+    partial_out = dots("rd,trc->tdc", grad_branch, merged).astype(jnp.bfloat16)
     grad_shared, grad_value = attend_back(
         shared, values, seen_by, own_block, prefix_len, merged_full, lse, grad_merged
     )
     grad_pair = jnp.concatenate([grad_shared, grad_value], axis=1)
     grad_pair = exchange(grad_pair.reshape(groups, rows, 2 * heads_wide))
-    summed_pair = total(dots("rd,trc->tdc", first_low, grad_pair))
+    partial_pair = dots("rd,trc->tdc", first_low, grad_pair).astype(jnp.bfloat16)
     grad_first = dots("trc,tdc->rd", grad_pair, full_pair)
     part_second, grad_gain_one, grad_shift_one = norm_backward(
         grad_first, norm_one, factor_one, gain_a
@@ -382,9 +589,13 @@
     piece = split // groups
     vectors = [v.reshape(-1, groups, piece).transpose(1, 0, 2) for v in vectors]
     vectors = jnp.concatenate([grad_bias_up.reshape(groups, -1, split)] + vectors, axis=2)
-    vectors = lax.psum_scatter(
-        vectors.reshape(-1, split + 5 * piece), everyone, scatter_dimension=0, tiled=True
-    )[0]
+    wide = vectors.shape[2]
+    vectors = jnp.pad(vectors, ((0, 0), (0, 0), (0, -wide % 1024)))
+    vectors = vectors.reshape(groups, -1, 8, vectors.shape[2] // 8)
+    summed_down, summed_up, summed_pair, summed_out, vectors = sum_everywhere(
+        groups, vectors.shape[1], [partial_down, partial_up, partial_pair, partial_out, vectors]
+    )
+    vectors = vectors.reshape(-1)
     tails = [vectors[split + which * piece : split + (which + 1) * piece] for which in range(5)]
     return (
         out_first,
@@ -393,10 +604,10 @@
         grad_in_second,
         summed_pair[:, :heads_wide],
         summed_pair[:, heads_wide:],
-        summed_out,
+        summed_out.T,
         summed_up,
         vectors[:split],
-        summed_down,
+        summed_down.T,
         *tails,
     )
 

time: 995 us -> 705 us (0.71)
  waiting for transfers between devices: 588 us -> 236 us
  Pallas kernels: 58.9 us -> 210 us
  blocking collectives: 135 us -> 43.4 us
    reduce_scatter x3 -> x0, waiting for transfers between devices: 221 us -> none  [total(): lax.psum_scatter(flat, everyone, scatter_dimension=0, tiled=True)]
    pallas_call x0 -> x1, Pallas kernels: none -> 156 us  [sum_everywhere(): pl.pallas_call(functools.partial(sum_kernel, groups, peers, len(blocks),...]
    unnamed x9 -> x4, waiting for transfers between devices: 147 us -> 1.91 us
    all_to_all x1 -> x0, blocking collectives: 52.4 us -> none  [exchange(): return lax.all_to_all(parts, 'tp', 0, 0, tiled=True)]
    unnamed x1 -> x0, blocking collectives: 38.8 us -> none
    all_to_all x3 -> x4, waiting for transfers between devices: 90.9 us -> 109 us  [exchange(): return lax.all_to_all(parts, 'tp', 0, 0, tiled=True)]
  transfers between devices with their start and end apart: 11 -> 8, of which waited for: 9 -> 7; matrix products, arithmetic and copies ran while one was open for 12% -> 13% of each run, Pallas kernels for 6% -> 4%
where the time goes in v3:
time: 705 us; the launch traced here: 695 us
  waiting for transfers between devices  236 us (33%)
  Pallas kernels  210 us (30%)
  matrix products  110 us (16%)
  local copies, waits for them, and re-layouts  53 us (8%)
  blocking collectives  43.4 us (6%)
  starting transfers between devices  17.5 us (2%)
  between operations  15.3 us (2%)
  other arithmetic  9.69 us (1%)
    pallas_call x1, Pallas kernels, sum_everywhere(): pl.pallas_call(functools.partial(sum_kernel, groups, peers, len(blocks),...  156 us
    all_gather x4, waiting for transfers between devices, collect(): whole = lax.all_gather(shard, everyone, axis=0, tiled=True)  126 us
    all_to_all x4, waiting for transfers between devices, exchange(): return lax.all_to_all(parts, 'tp', 0, 0, tiled=True)  109 us
    dot_general x12, matrix products, dots(): return jnp.einsum(spec, left, right, preferred_element_type=jnp.float32)  107 us
    all_gather x1, blocking collectives, on_device(): lax.all_gather(small, everyone, axis=0, tiled=False).astype(jnp.float32)  43.4 us
    pallas_call x1, Pallas kernels, attend_back(): pl.pallas_call(functools.partial(attend_back_kernel, tile), grid=(heads_h...  29.3 us
    pallas_call x1, Pallas kernels, attend(): pl.pallas_call(functools.partial(attend_kernel, tile), grid=(heads_here,...  24.8 us
    all_to_all x4, starting transfers between devices, exchange(): return lax.all_to_all(parts, 'tp', 0, 0, tiled=True)  17.3 us
  transfers between devices with their start and end apart: 8, of which 7 were waited for; matrix products, arithmetic and copies ran while one was open for 13% of the time, Pallas kernels for 4%

profile of v3, /device:TPU:0, one launch (start us, length us, event | category | flops | bytes accessed | tf_op | source)
XLA Modules:
  0.0 695.2 jit_solution(7819294479303886782)
XLA Ops:
  7.3 1.7 pad_maximum_fusion.1
  11.1 1.8 reduce_sum.126
  12.9 43.4 %all-gather.1 = bf16[32,6,128]{2,1,0:T(8,128)(2,1)S(1)} all-gather(bf16[1,6,128]{2,1,0:T(8,128)(2,1)S(1)} %bitcast.212), channel_id=2, replica_groups=mesh['fsdp'=8,'tp'=4] {'tp','fsdp'}, dimensions={0}, use_global_device_ids=true | all-gather | bytes 50688 | tf_op jit(solution)/shard_map/all_gather | solution.py:524
  56.7 19.5 %all-gather.7.cloned.1.call-done = bf16[4096,512]{1,0:T(8,128)(2,1)} async-done(((bf16[128,512]{1,0:T(8,128)(2,1)}), bf16[4096,512]{1,0:T(8,128)(2,1)}) %all-gather.7.cloned.1.call-update) | async-done | bytes 4194320 | tf_op jit(solution)/shard_map/all_gather | solution.py:520
  76.3 6.1 convert_bitcast_fusion.2
  82.4 4.6 all-to-all-start
  87.9 2.3 fusion.15
  90.5 1.8 copy.68
  92.4 1.6 eq.80
  93.9 1.9 copy.67
  96.3 1.5 copy-done.8
  98.2 45.6 %all-to-all-done = bf16[4,512,512]{1,2,0:T(8,128)(2,1)} async-done(((bf16[4,512,512]{1,2,0:T(8,128)(2,1)}), bf16[4,512,512]{1,2,0:T(8,128)(2,1)}, u32[]{:S(2)}, u32[]{:S(2)}) %all-to-all-start) | async-done | bytes 2097184 | tf_op jit(solution)/shard_map/all_to_all | solution.py:539
  143.8 4.1 copy.66
  147.9 1.7 fusion.46
  149.6 24.8 %shard_map.280 = (bf16[2048,256]{1,0:T(8,128)(2,1)S(1)}, f32[2048,256]{1,0:T(8,128)}, f32[2,8,2048]{2,1,0:T(8,128)S(1)}) custom-call(s32[1]{0:T(128)S(6)} %copy.101.prefix_ref, bf16[2048,256]{1,0:T(8,128)(2,1)S(1)} %get-tuple-element.93.q_ref, bf16[2048,256]{1,0:T(8,128)(2,1)S(1)} %get-tuple-element.92.v_ref, ...), custom_call_target="tpu_custom_call" | custom-call | tf_op jit(solution)/shard_map/pallas_call | solution.py:144
  175.4 3.8 all-to-all-start.1
  179.3 4.1 copy.69
  183.4 33.0 %all-to-all-done.1 = bf16[4,512,256]{2,1,0:T(8,128)(2,1)S(1)} async-done(((bf16[4,512,256]{2,1,0:T(8,128)(2,1)}), bf16[4,512,256]{2,1,0:T(8,128)(2,1)S(1)}, u32[]{:S(2)}, u32[]{:S(2)}) %all-to-all-start.1) | async-done | bytes 1048608 | tf_op jit(solution)/shard_map/all_to_all | solution.py:539
  216.3 3.8 fusion.50
  220.2 1.3 copy-done.6
  221.9 24.2 %all-gather.11.cloned.1.call-done = bf16[4096,1024]{1,0:T(8,128)(2,1)} async-done(((bf16[128,1024]{1,0:T(8,128)(2,1)}), bf16[4096,1024]{1,0:T(8,128)(2,1)}) %all-gather.11.cloned.1.call-update) | async-done | bytes 8388624 | tf_op jit(solution)/shard_map/all_gather | solution.py:520
  246.1 11.9 %fusion.40 = f32[512,4,1024]{2,0,1:T(8,128)} fusion(bf16[4,1024,1024]{2,1,0:T(8,128)(2,1)} %bitcast.225, f32[512,1024]{1,0:T(8,128)} %copy-done.6, f32[1024]{0:T(1024)S(1)} %bitcast.216, f32[1024]{0:T(1024)S(1)} %bitcast.204, f32[512]{0:T(512)S(1)} %add_rsqrt_fusion, f32[512]{0:T(512)S(1)} %broadcast_multiply_fusion.4), kind=kOutput, calls=%fused_computation.103 | convolution fusion | flops 4297588736 | bytes 18886656 | tf_op jit(solution)/shard_map/rd,tdh->trh/dot_general | solution.py:536
  258.0 81.8 %all-gather.13.cloned.1.call-done = bf16[4096,1024]{0,1:T(8,128)(2,1)} async-done(((bf16[128,1024]{0,1:T(8,128)(2,1)}), bf16[4096,1024]{0,1:T(8,128)(2,1)}) %all-gather.13.cloned.1.call-update) | async-done | bytes 8388624 | tf_op jit(solution)/shard_map/all_gather | solution.py:520
  339.7 11.9 %copy.70 = bf16[4096,1024]{1,0:T(8,128)(2,1)} copy(bf16[4096,1024]{0,1:T(8,128)(2,1)} %all-gather.13.cloned.1.call-done) | data formatting | bytes 16777216 | tf_op jit(solution)/shard_map/all_gather | solution.py:520
  351.7 12.9 %convert_reduce_fusion = (f32[4,1024]{1,0:T(4,128)S(1)}, bf16[4,512,1024]{2,1,0:T(8,128)(2,1)S(1)}) fusion(f32[512,4,1024]{2,0,1:T(8,128)} %fusion.40, f32[4,1024]{1,0:T(4,128)S(1)} %bitcast.208, bf16[4,1024,1024]{2,1,0:T(8,128)(2,1)} %bitcast.178, f32[512,1024]{1,0:T(8,128)} %param.20), kind=kOutput, calls=%fused_computation.10 | convolution fusion | flops 4341624832 | bytes 23101440 | tf_op jit(solution)/shard_map/rd,tdh->trh/dot_general | solution.py:536
  364.6 18.3 %fusion.10 = (f32[1024]{0:T(1024)S(1)}, f32[512]{0:T(512)S(1)}, f32[512]{0:T(512)S(1)}, f32[1024]{0:T(1024)S(1)}, f32[512,1024,1]{1,0,2:T(8,128)S(1)}) fusion(f32[512,1024]{1,0:T(8,128)S(1)} %copy-done.7, f32[512]{0:T(512)S(1)} %add_rsqrt_fusion, f32[512]{0:T(512)S(1)} %broadcast_multiply_fusion.4, f32[1024]{0:T(1024)S(1)} %bitcast.205, ...), kind=kOutput, calls=%fused_computation.26 | convolution fusion | flops 4299682816 | bytes 16797696 | tf_op jit(solution)/shard_map/trh,tdh->rd/dot_general | solution.py:536
  383.7 1.3 copy-done.10
  385.0 2.2 fusion.14
  387.2 4.3 all-to-all-start.2
  391.6 4.2 convert_bitcast_fusion.1
  395.8 3.9 copy.76
  399.8 12.4 %convolution_convert_fusion.1 = bf16[4,1024,1024]{1,2,0:T(8,128)(2,1)} fusion(f32[512,1024]{1,0:T(8,128)} %param.20, f32[512,4,1024]{2,0,1:T(8,128)} %fusion.40, f32[4,1024]{1,0:T(4,128)S(1)} %bitcast.209), kind=kOutput, calls=%fused_computation.15 | convolution fusion | flops 4320657408 | bytes 18890752 | tf_op jit(solution)/shard_map/rd,trh->tdh/dot_general | solution.py:536
  412.2 5.8 all-to-all-done.2
  418.0 29.3 %shard_map.281 = (bf16[2048,256]{1,0:T(8,128)(2,1)S(1)}, bf16[2048,256]{1,0:T(8,128)(2,1)S(1)}) custom-call(s32[1]{0:T(128)S(6)} %copy.101.prefix_ref, bf16[2048,256]{1,0:T(8,128)(2,1)S(1)} %copy-done.2, bf16[2048,256]{1,0:T(8,128)(2,1)S(1)} %get-tuple-element.92.v_ref, bf16[2,2048,128]{2,1,0:T(8,128)(2,1)S(1)} %or_convert_fusion.a_ref, ...), custom_call_target="tpu_custom_call" | custom-call | tf_op jit(solution)/shard_map/pallas_call | solution.py:254
  447.2 1.5 pad_maximum_fusion
  448.7 4.7 all-to-all-start.3
  453.4 11.3 %convolution_convert_fusion = bf16[4,1024,1024]{1,2,0:T(8,128)(2,1)} fusion(bf16[4,512,1024]{2,1,0:T(8,128)(2,1)} %copy-done.21, f32[512,1024]{1,0:T(8,128)} %copy-done.6, f32[1024]{0:T(1024)S(1)} %bitcast.217, f32[1024]{0:T(1024)S(1)} %bitcast.207, f32[512]{0:T(512)S(1)} %add_rsqrt_fusion, f32[512]{0:T(512)S(1)} %broadcast_multiply_fusion.4), kind=kOutput, calls=%fused_computation.14 | convolution fusion | flops 4301783040 | bytes 14692352 | tf_op jit(solution)/shard_map/rd,trh->tdh/dot_general | solution.py:536
  464.7 12.5 %fusion.11 = f32[512,1024]{1,0:T(8,128)} fusion(f32[512,1024]{1,0:T(8,128)S(1)} %copy-done.5, bf16[4,1024,1024]{2,1,0:T(8,128)(2,1)} %bitcast.179, f32[1024]{0:T(1024)S(1)} %bitcast.215, f32[512,4,1024]{2,0,1:T(8,128)} %fusion.40, f32[4,1024]{1,0:T(4,128)S(1)} %bitcast.210), kind=kOutput, calls=%fused_computation.28 | convolution fusion | flops 4316987392 | bytes 20992000 | tf_op jit(solution)/shard_map/trh,tdh->rd/dot_general | solution.py:536
  477.2 24.6 %all-to-all-done.3 = bf16[4,512,512]{2,1,0:T(8,128)(2,1)} async-done(((bf16[4,512,512]{2,1,0:T(8,128)(2,1)}), bf16[4,512,512]{2,1,0:T(8,128)(2,1)}, u32[]{:S(2)}, u32[]{:S(2)}) %all-to-all-start.3) | async-done | bytes 2097184 | tf_op jit(solution)/shard_map/all_to_all | solution.py:539
  501.8 5.8 fusion.9
  507.6 2.3 fusion.45
  511.0 6.0 convert_bitcast_fusion
  517.0 6.2 copy.74
  523.2 156.1 %shard_map.282 = (f32[128,1024]{1,0:T(8,128)}, f32[128,1024]{1,0:T(8,128)}, f32[128,512]{1,0:T(8,128)}, f32[128,256]{1,0:T(8,128)}, f32[8,128]{1,0:T(8,128)}) custom-call(bf16[4,8,128,1024]{3,2,1,0:T(8,128)(2,1)} %bitcast.183, bf16[4,8,128,1024]{3,2,1,0:T(8,128)(2,1)} %bitcast.184, bf16[4,8,128,512]{3,2,1,0:T(8,128)(2,1)} %bitcast.177, ...), custom_call_target="tpu_custom_call" | custom-call | tf_op jit(solution)/shard_map/pallas_call | solution.py:475
  679.3 1.7 copy.82
  681.0 1.7 fusion.47
  683.9 1.5 fusion.49
  685.4 2.0 copy.83
  (90 shorter events, 9.2 us)
Async XLA Ops:
  7.2 49.1 %copy-start.4 = (f32[512,1024]{1,0:T(8,128)S(1)}, f32[512,1024]{1,0:T(8,128)}, u32[]{:S(2)}) copy-start(f32[512,1024]{1,0:T(8,128)} %param.18) | copy-start | bytes 6291460
  7.2 5.6 copy-start.18
  7.2 5.6 copy-start.17
  7.2 5.6 copy-start.16
  7.2 5.6 copy-start.15
  7.2 5.6 copy-start.19
  7.2 5.6 copy-start.20
  7.3 69.0 %all-gather.7.cloned.1.call-start = ((), (), s32[]{:S(2)}) async-start(), calls=%async_computation.4 | async-start | bytes 4325376 | tf_op jit(solution)/shard_map/all_gather | solution.py:520
  9.0 170.3 %all-gather.9.cloned.1.call-start = ((), (), s32[]{:S(2)}) async-start(), calls=%async_computation.5 | async-start | bytes 2162688 | tf_op jit(solution)/shard_map/all_gather | solution.py:520
  9.7 236.4 %all-gather.11.cloned.1.call-start = ((), (), s32[]{:S(2)}) async-start(), calls=%async_computation.6 | async-start | bytes 8650752 | tf_op jit(solution)/shard_map/all_gather | solution.py:520
  10.5 329.2 %all-gather.13.cloned.1.call-start = ((), (), s32[]{:S(2)}) async-start(), calls=%async_computation.7 | async-start | bytes 8650752 | tf_op jit(solution)/shard_map/all_gather | solution.py:520
  82.4 5.4 copy-start.14
  82.4 61.4 %all-to-all-start = ((bf16[4,512,512]{1,2,0:T(8,128)(2,1)}), bf16[4,512,512]{1,2,0:T(8,128)(2,1)}, u32[]{:S(2)}, u32[]{:S(2)}) async-start(bf16[4,512,512]{1,2,0:T(8,128)(2,1)} %convert_bitcast_fusion.2), calls=%async_computation | async-start | bytes 4194304 | tf_op jit(solution)/shard_map/all_to_all | solution.py:539
  95.8 2.0 copy-start.8
  96.3 53.4 %copy-start = (bf16[2,2048,128]{2,1,0:T(8,128)(2,1)}, bf16[2,2048,128]{2,1,0:T(8,128)(2,1)S(1)}, u32[]{:S(2)}) copy-start(bf16[2,2048,128]{2,1,0:T(8,128)(2,1)S(1)} %get-tuple-element.88.b_ref) | copy-start | bytes 3145732
  149.6 24.8 %copy-start.1 = (bf16[2048,256]{1,0:T(8,128)(2,1)}, bf16[2048,256]{1,0:T(8,128)(2,1)S(1)}, u32[]{:S(2)}) copy-start(bf16[2048,256]{1,0:T(8,128)(2,1)S(1)} %get-tuple-element.93.q_ref) | copy-start | bytes 3145732
  174.4 1.0 copy-start.3
  175.4 41.0 %all-to-all-start.1 = ((bf16[4,512,256]{2,1,0:T(8,128)(2,1)}), bf16[4,512,256]{2,1,0:T(8,128)(2,1)S(1)}, u32[]{:S(2)}, u32[]{:S(2)}) async-start(bf16[4,512,256]{2,1,0:T(8,128)(2,1)} %bitcast.176), calls=%async_computation.1 | async-start | bytes 2097152 | tf_op jit(solution)/shard_map/all_to_all | solution.py:539
  220.2 1.3 copy-start.6
  351.7 12.9 %copy-start.7 = (f32[512,1024]{1,0:T(8,128)S(1)}, f32[512,1024]{1,0:T(8,128)}, u32[]{:S(2)}) copy-start(f32[512,1024]{1,0:T(8,128)} %copy-done.6) | copy-start | bytes 6291460
  364.6 18.3 %copy-start.21 = (bf16[4,512,1024]{2,1,0:T(8,128)(2,1)}, bf16[4,512,1024]{2,1,0:T(8,128)(2,1)S(1)}, u32[]{:S(2)}) copy-start(bf16[4,512,1024]{2,1,0:T(8,128)(2,1)S(1)} %get-tuple-element.112) | copy-start | bytes 12582916
  364.6 18.3 %copy-start.9 = (f32[512,1024]{1,0:T(8,128)S(1)}, f32[512,1024]{1,0:T(8,128)}, u32[]{:S(2)}) copy-start(f32[512,1024]{1,0:T(8,128)} %param.19) | copy-start | bytes 6291460
  382.9 2.0 copy-start.11
  383.6 1.3 copy-start.10
  387.2 30.8 %all-to-all-start.2 = ((bf16[4,512,256]{2,1,0:T(8,128)(2,1)}), bf16[4,512,256]{2,1,0:T(8,128)(2,1)}, u32[]{:S(2)}, u32[]{:S(2)}) async-start(bf16[4,512,256]{2,1,0:T(8,128)(2,1)} %fusion.14), calls=%async_computation.2 | async-start | bytes 2097152 | tf_op jit(solution)/shard_map/all_to_all | solution.py:539
  399.8 18.2 %copy-start.2 = (bf16[2048,256]{1,0:T(8,128)(2,1)S(1)}, bf16[2048,256]{1,0:T(8,128)(2,1)}, u32[]{:S(2)}) copy-start(bf16[2048,256]{1,0:T(8,128)(2,1)} %copy-done.1) | copy-start | bytes 3145732
  448.7 53.1 %all-to-all-start.3 = ((bf16[4,512,512]{2,1,0:T(8,128)(2,1)}), bf16[4,512,512]{2,1,0:T(8,128)(2,1)}, u32[]{:S(2)}, u32[]{:S(2)}) async-start(bf16[4,512,512]{2,1,0:T(8,128)(2,1)} %bitcast.38), calls=%async_computation.3 | async-start | bytes 4194304 | tf_op jit(solution)/shard_map/all_to_all | solution.py:539
  453.4 11.3 %copy-start.5 = (f32[512,1024]{1,0:T(8,128)S(1)}, f32[512,1024]{1,0:T(8,128)}, u32[]{:S(2)}) copy-start(f32[512,1024]{1,0:T(8,128)} %param.18) | copy-start | bytes 6291460
  501.8 5.8 copy-start.12
  679.3 8.1 %copy-start.13 = (f32[128,1024]{1,0:T(8,128)S(1)}, f32[128,1024]{1,0:T(8,128)}, u32[]{:S(2)}) copy-start(f32[128,1024]{1,0:T(8,128)} %get-tuple-element.138) | copy-start | bytes 1572868
Sparse Core Ops, SparseCore 0:
  11.5 64.6 all-gather.6
  79.1 74.2 all-gather.8
  156.2 89.8 all-gather.10
  248.8 90.8 all-gather.12

commit v4 on v3

--- a/solution.py
+++ b/solution.py
@@ -46,29 +46,6 @@
     )
 
 
-def bucket_rows(sort_order):
-    heads_here, rounds, length = sort_order.shape
-    block_count = length // BLOCK
-    slot_block = (jnp.arange(length, dtype=jnp.int32) // BLOCK).astype(jnp.bfloat16)
-    high = (
-        (sort_order // 128)[:, :, None, :]
-        == jnp.arange(length // 128, dtype=jnp.int32)[None, None, :, None]
-    )
-    low = (sort_order % 128)[..., None] == jnp.arange(128, dtype=jnp.int32)
-    high = jnp.where(high, slot_block, jnp.bfloat16(0))
-    bucket = jnp.einsum(
-        "hras,hrsb->hrab", high, low.astype(jnp.bfloat16), preferred_element_type=jnp.float32
-    )
-    bucket = bucket.reshape(heads_here, rounds, length).astype(jnp.int32)
-    bucket = bucket.transpose(0, 2, 1)[..., None]
-    lanes = jnp.arange(block_count, dtype=jnp.int32)
-    own = lanes == bucket
-    before = lanes == (bucket + block_count - 1) % block_count
-    shape = (heads_here, length, rounds * block_count)
-    seen_by = (own | before).astype(jnp.bfloat16).reshape(shape)
-    return seen_by, own.astype(jnp.bfloat16).reshape(shape)
-
-
 def dot_nt(left, right):
     return lax.dot_general(
         left, right, (((1,), (1,)), ((), ())), preferred_element_type=jnp.float32
@@ -78,92 +55,6 @@
 def unit_rows(rows):
     inv_norm = lax.rsqrt(jnp.mean(rows * rows, axis=-1, keepdims=True) + 1e-06)
     return rows * inv_norm, inv_norm
-
-
-def attend_kernel(
-    tile, prefix_ref, q_ref, v_ref, a_ref, b_ref, low_ref, full_ref, lse_ref, key_ref
-):
-    step = pl.program_id(1)
-    prefix = prefix_ref[0]
-
-    @pl.when(step == 0)
-    def _():
-        key_ref[...] = unit_rows(q_ref[...].astype(jnp.float32))[0].astype(jnp.bfloat16)
-
-    own = pl.ds(pl.multiple_of(step * tile, tile), tile)
-    query = q_ref[own, :]
-    seen = a_ref[0, own, :]
-
-    def visit(part, carry, masked):
-        peak, total, acc = carry
-        keys = pl.ds(pl.multiple_of(part * tile, tile), tile)
-        scores = dot_nt(query, key_ref[keys, :]) * SCORE_SCALE
-        count = dot_nt(seen, b_ref[0, keys, :])
-        if masked:
-            row = step * tile + lax.broadcasted_iota(jnp.int32, (tile, tile), 0)
-            col = part * tile + lax.broadcasted_iota(jnp.int32, (tile, tile), 1)
-            allowed = (col < row) | ((row < prefix) & (col < prefix) & (row != col))
-            count = jnp.where(allowed, count, 0.0)
-        scores = jnp.where(count > 0.5, scores, FLOOR)
-        peak_now = jnp.maximum(peak, jnp.max(scores, axis=1, keepdims=True))
-        probs = count * jnp.exp2(scores - peak_now)
-        shrink = jnp.exp2(peak - peak_now)
-        total = total * shrink + jnp.sum(probs, axis=1, keepdims=True)
-        acc = acc * shrink + jnp.dot(
-            probs.astype(jnp.bfloat16), v_ref[keys, :], preferred_element_type=jnp.float32
-        )
-        return peak_now, total, acc
-
-    carry = (
-        jnp.full((tile, 1), FLOOR, jnp.float32),
-        jnp.zeros((tile, 1), jnp.float32),
-        jnp.zeros((tile, HEAD_DIM), jnp.float32),
-    )
-    carry = lax.fori_loop(0, step, lambda part, c: visit(part, c, False), carry)
-    ahead = jnp.where(step * tile < prefix, (prefix + tile - 1) // tile, 0)
-    carry = lax.fori_loop(
-        step, jnp.maximum(step + 1, ahead), lambda part, c: visit(part, c, True), carry
-    )
-    peak, total, acc = carry
-    alone = total == 0.0
-    merged = jnp.where(
-        alone, v_ref[own, :].astype(jnp.float32), acc / jnp.where(alone, 1.0, total)
-    )
-    low_ref[...] = merged.astype(jnp.bfloat16)
-    full_ref[...] = merged
-    lse = jnp.where(alone, ALONE, peak + jnp.log2(jnp.where(alone, 1.0, total)))
-    lse_ref[0] = jnp.broadcast_to(lse, (tile, 128)).T[:8]
-
-
-def attend(shared, values, seen_by, own_block, prefix):
-    length, width = shared.shape
-    heads_here = width // HEAD_DIM
-    tile = min(512, length)
-    whole = lambda h, i: (0, h)
-    hot = pl.BlockSpec((1, length, 128), lambda h, i: (h, 0, 0))
-    return pl.pallas_call(
-        functools.partial(attend_kernel, tile),
-        grid=(heads_here, length // tile),
-        in_specs=[
-            pl.BlockSpec(memory_space=pltpu.SMEM),
-            pl.BlockSpec((length, HEAD_DIM), whole),
-            pl.BlockSpec((length, HEAD_DIM), whole),
-            hot,
-            hot,
-        ],
-        out_specs=[
-            pl.BlockSpec((tile, HEAD_DIM), lambda h, i: (i, h)),
-            pl.BlockSpec((tile, HEAD_DIM), lambda h, i: (i, h)),
-            pl.BlockSpec((1, 8, tile), lambda h, i: (h, 0, i)),
-        ],
-        out_shape=[
-            jax.ShapeDtypeStruct((length, width), jnp.bfloat16),
-            jax.ShapeDtypeStruct((length, width), jnp.float32),
-            jax.ShapeDtypeStruct((heads_here, 8, length), jnp.float32),
-        ],
-        scratch_shapes=[pltpu.VMEM((length, HEAD_DIM), jnp.bfloat16)],
-        compiler_params=pltpu.CompilerParams(vmem_limit_bytes=48 * 2**20),
-    )(prefix, shared, values, seen_by, own_block)
 
 
 def attend_back_kernel(
@@ -195,17 +86,17 @@
 
     own = pl.ds(pl.multiple_of(step * tile, tile), tile)
     query = q_ref[own, :]
-    seen = a_ref[0, own, :]
+    seen = a_ref[own, :]
     grad = g_ref[own, :]
     delta = jnp.sum((grad.astype(jnp.float32) * full_ref[...]).T, axis=0, keepdims=True)
-    lse = lse_ref[0, 0:1, :]
+    lse = lse_ref[0:1, :]
     alone = jnp.where(lse == ALONE, 1.0, 0.0)
 
     def visit(part, masked):
         keys = pl.ds(pl.multiple_of(part * tile, tile), tile)
         key = key_ref[keys, :]
         scores = dot_nt(key, query) * SCORE_SCALE
-        count = dot_nt(b_ref[0, keys, :], seen)
+        count = dot_nt(b_ref[keys, :], seen)
         if masked:
             col = part * tile + lax.broadcasted_iota(jnp.int32, (tile, tile), 0)
             row = step * tile + lax.broadcasted_iota(jnp.int32, (tile, tile), 1)
@@ -245,31 +136,29 @@
         gv_ref[...] = dv_ref[...].astype(jnp.bfloat16)
 
 
-def attend_back(shared, values, seen_by, own_block, prefix, full, lse, grad_packed):
-    length, width = shared.shape
-    heads_here = width // HEAD_DIM
-    tile = min(512, length)
-    whole = pl.BlockSpec((length, HEAD_DIM), lambda h, i: (0, h))
-    hot = pl.BlockSpec((1, length, 128), lambda h, i: (h, 0, 0))
+def attend_back(qv, seen_by, own_block, prefix, full, lse, grads):
+    heads, length, _ = full.shape
+    tile = lse.shape[-1]
+    whole = pl.BlockSpec((None, length, HEAD_DIM), lambda h, i: (h, 0, 0))
     return pl.pallas_call(
         functools.partial(attend_back_kernel, tile),
-        grid=(heads_here, length // tile),
+        grid=(heads, length // tile),
         in_specs=[
             pl.BlockSpec(memory_space=pltpu.SMEM),
             whole,
+            pl.BlockSpec((None, length, HEAD_DIM), lambda h, i: (h + heads, 0, 0)),
             whole,
-            hot,
-            hot,
-            pl.BlockSpec((tile, HEAD_DIM), lambda h, i: (i, h)),
-            pl.BlockSpec((1, 8, tile), lambda h, i: (h, 0, i)),
             whole,
+            pl.BlockSpec((None, tile, HEAD_DIM), lambda h, i: (h, i, 0)),
+            pl.BlockSpec((None, None, 8, tile), lambda h, i: (h, i, 0, 0)),
+            pl.BlockSpec((length, HEAD_DIM), lambda h, i: (0, h)),
         ],
-        out_specs=[whole, whole],
-        out_shape=[jax.ShapeDtypeStruct((length, width), jnp.bfloat16)] * 2,
+        out_specs=[pl.BlockSpec((length, HEAD_DIM), lambda h, i: (0, h))] * 2,
+        out_shape=[jax.ShapeDtypeStruct((length, heads * HEAD_DIM), jnp.bfloat16)] * 2,
         scratch_shapes=[pltpu.VMEM((length, HEAD_DIM), jnp.bfloat16)]
         + [pltpu.VMEM((length, HEAD_DIM), jnp.float32)] * 3,
         compiler_params=pltpu.CompilerParams(vmem_limit_bytes=48 * 2**20),
-    )(prefix, shared, values, seen_by, own_block, full, lse, grad_packed)
+    )(prefix, qv, qv, seen_by, own_block, full, lse, grads)
 
 
 MESH = pl.DeviceIdType.MESH
@@ -482,6 +371,411 @@
             collective_id=1, has_side_effects=True, vmem_limit_bytes=56 * 2**20
         ),
     )(*blocks)
+
+
+class Gathered:
+    @staticmethod
+    def scratch(groups, peers):
+        count = peers // 2
+        slots = groups + groups * (count - 1) + groups
+        return [pltpu.SemaphoreType.DMA((slots,))] * 2 + [pltpu.SemaphoreType.DMA((1,))]
+
+    def __init__(self, source, full, scratch, turn):
+        self.source, self.full, self.turn = source, full, turn
+        self.send, self.recv, self.local = scratch
+        self.groups, self.count = full.shape[:2]
+        self.steps = self.count.bit_length() - 1
+        self.f, self.t = lax.axis_index("fsdp"), lax.axis_index("tp")
+        self.place, self.core = lax.div(self.f, 2), lax.rem(self.f, 2)
+        self.copies, self.sent = {}, []
+
+    def remote(self, name, slot, source, target, device):
+        copy = pltpu.make_async_remote_copy(
+            src_ref=source,
+            dst_ref=target,
+            send_sem=self.send.at[slot],
+            recv_sem=self.recv.at[slot],
+            device_id=device,
+            device_id_type=MESH,
+        )
+        copy.start()
+        self.copies.setdefault(name, []).append(copy)
+        self.sent.append(copy)
+
+    def landed(self, name):
+        for copy in self.copies.pop(name):
+            copy.wait_recv()
+
+    def group(self, behind):
+        return lax.rem(self.t + self.groups - behind, self.groups)
+
+    def begin_local(self):
+        self.own = pltpu.make_async_copy(
+            self.source, self.full.at[self.t, self.place, self.core], self.local.at[0]
+        )
+        self.own.start()
+
+    def begin(self):
+        for ahead in range(1, self.groups):
+            self.remote(
+                ("z", ahead),
+                ahead,
+                self.source,
+                self.full.at[self.t, self.place, self.core],
+                {"tp": lax.rem(self.t + ahead, self.groups)},
+            )
+
+    def ready(self, behind, step):
+        if step > 0:
+            self.landed((behind, step - 1))
+        elif behind > 0:
+            self.landed(("z", behind))
+        else:
+            self.own.wait()
+
+    def spread(self, behind, step):
+        self.ready(behind, step)
+        low_first = (behind + self.turn) % 2 == 0
+        which = step if low_first else self.steps - 1 - step
+        many = 2**step
+        for j in range(many):
+            if low_first:
+                block = lax.div(self.place, many) * many + j
+            else:
+                rest = self.count // many
+                block = j * rest + lax.rem(self.place, rest)
+            here = self.full.at[self.group(behind), block, self.core]
+            slot = self.groups + behind * (self.count - 1) + many - 1 + j
+            self.remote((behind, step), slot, here, here, {"fsdp": across(self.f, 1 + which)})
+
+    def pair_up(self, behind):
+        self.ready(behind, self.steps)
+        here = self.full.at[self.group(behind), :, self.core]
+        slot = self.groups * self.count + behind
+        self.remote(("core", behind), slot, here, here, {"fsdp": across(self.f, 0)})
+
+    def complete(self, behind):
+        self.landed(("core", behind))
+
+    def finish(self):
+        for copy in self.sent:
+            copy.wait_send()
+
+
+def hot_rows(order_ref, seen_ref, own_ref, head):
+    rounds, length = order_ref.shape[1:]
+    blocks = length // BLOCK
+    high = lax.broadcasted_iota(jnp.int32, (length // 128, length), 0)
+    low = lax.broadcasted_iota(jnp.int32, (128, length), 0)
+    block = (lax.broadcasted_iota(jnp.int32, (1, length), 1) // BLOCK).astype(jnp.float32)
+    lane = lax.broadcasted_iota(jnp.int32, (128, rounds * blocks), 1)
+    slot_block = lax.rem(lane, blocks).astype(jnp.float32)
+    turn = lax.div(lane, blocks)
+    columns = []
+    for r in range(rounds):
+        token = order_ref[head, r : r + 1, :]
+        left = jnp.where(high == token // 128, block, 0.0).astype(jnp.bfloat16)
+        right = jnp.where(low == token % 128, 1.0, 0.0).astype(jnp.bfloat16)
+        columns.append(dot_nt(right, left))
+    for part in range(length // 128):
+        own = jnp.zeros((128, rounds * blocks), jnp.float32)
+        for r in range(rounds):
+            own = jnp.where(turn == r, columns[r][:, part : part + 1], own)
+        before = jnp.where(own == 0.0, blocks - 1.0, own - 1.0)
+        mine = jnp.where(own == slot_block, 1.0, 0.0)
+        rows = pl.ds(part * 128, 128)
+        own_ref[head, rows, :] = mine.astype(jnp.bfloat16)
+        seen_ref[head, rows, :] = jnp.where(before == slot_block, 1.0, mine).astype(jnp.bfloat16)
+
+
+def attend_rows(tile, step, prefix, query_ref, key_ref, value_ref, seen_ref, own_ref):
+    own = pl.ds(pl.multiple_of(step * tile, tile), tile)
+    query = query_ref[own, :]
+    seen = seen_ref[own, :]
+
+    def visit(part, carry, masked):
+        peak, total, acc = carry
+        keys = pl.ds(pl.multiple_of(part * tile, tile), tile)
+        scores = dot_nt(query, key_ref[keys, :]) * SCORE_SCALE
+        count = dot_nt(seen, own_ref[keys, :])
+        if masked:
+            row = step * tile + lax.broadcasted_iota(jnp.int32, (tile, tile), 0)
+            col = part * tile + lax.broadcasted_iota(jnp.int32, (tile, tile), 1)
+            allowed = (col < row) | ((row < prefix) & (col < prefix) & (row != col))
+            count = jnp.where(allowed, count, 0.0)
+        scores = jnp.where(count > 0.5, scores, FLOOR)
+        peak_now = jnp.maximum(peak, jnp.max(scores, axis=1, keepdims=True))
+        probs = count * jnp.exp2(scores - peak_now)
+        shrink = jnp.exp2(peak - peak_now)
+        total = total * shrink + jnp.sum(probs, axis=1, keepdims=True)
+        acc = acc * shrink + jnp.dot(
+            probs.astype(jnp.bfloat16), value_ref[keys, :], preferred_element_type=jnp.float32
+        )
+        return peak_now, total, acc
+
+    carry = (
+        jnp.full((tile, 1), FLOOR, jnp.float32),
+        jnp.zeros((tile, 1), jnp.float32),
+        jnp.zeros((tile, HEAD_DIM), jnp.float32),
+    )
+    carry = lax.fori_loop(0, step, lambda part, c: visit(part, c, False), carry)
+    length = query_ref.shape[0]
+    carry = lax.fori_loop(
+        step, last_part(step, tile, length), lambda part, c: visit(part, c, True), carry
+    )
+    peak, total, acc = carry
+    alone = total == 0.0
+    merged = jnp.where(
+        alone, value_ref[own, :].astype(jnp.float32), acc / jnp.where(alone, 1.0, total)
+    )
+    lse = jnp.where(alone, ALONE, peak + jnp.log2(jnp.where(alone, 1.0, total)))
+    return merged, jnp.broadcast_to(lse, (tile, 128)).T[:8]
+
+
+def last_part(step, tile, length):
+    ahead = length // 2 // tile
+    return jnp.where(step < ahead, ahead, step + 1)
+
+
+def forward_kernel(
+    groups,
+    peers,
+    prefix_ref,
+    order_ref,
+    x_ref,
+    small_ref,
+    pair_ref,
+    out_ref,
+    up_ref,
+    down_ref,
+    small_all,
+    pair_all,
+    out_all,
+    up_all,
+    down_all,
+    low_ref,
+    qv_ref,
+    seen_ref,
+    own_ref,
+    merged_ref,
+    full_ref,
+    lse_ref,
+    pair_hold,
+    leave_ref,
+    key_ref,
+    away_ref,
+    qv_send,
+    qv_recv,
+    merged_send,
+    merged_recv,
+    hold_sem,
+    *sems,
+):
+    tile, model = x_ref.shape
+    heads = order_ref.shape[0]
+    prefix = prefix_ref[0]
+    t = lax.axis_index("tp")
+    arrays = {}
+    turn = 0
+    for name, source, full in (
+        ("small", small_ref, small_all),
+        ("pair", pair_ref, pair_hold),
+        ("up", up_ref, up_all),
+        ("down", down_ref, down_all),
+        ("out", out_ref, out_all),
+    ):
+        arrays[name] = Gathered(source, full, sems[3 * turn : 3 * turn + 3], turn)
+        turn += 1
+    small, pair, up, down, out = (arrays[n] for n in ("small", "pair", "up", "down", "out"))
+    steps = small.steps
+
+    def waves(array, behinds):
+        for wave in range(len(behinds) + steps):
+            for place, behind in enumerate(behinds):
+                step = wave - place
+                if 0 <= step < steps:
+                    array.spread(behind, step)
+                elif step == steps:
+                    array.pair_up(behind)
+            yield
+
+    def drive(*lines):
+        lines = list(lines)
+        while lines:
+            for line in list(lines):
+                if next(line, "end") == "end":
+                    lines.remove(line)
+
+    every = list(range(groups))
+    for array in arrays.values():
+        array.begin_local()
+    greet(groups, peers)
+    small.begin()
+    pair.begin()
+    up.begin()
+    drive(waves(small, every), waves(pair, every[:1]))
+    for head in range(heads):
+        hot_rows(order_ref, seen_ref, own_ref, head)
+    drive(waves(pair, every[1:]))
+    for behind in every:
+        small.complete(behind)
+    gain_shift = jnp.concatenate(
+        [small_all[0, j // 2, j % 2].astype(jnp.float32)[:2] for j in range(peers)], axis=1
+    )
+
+    @pl.loop(0, tile // 64)
+    def _(part):
+        here = pl.ds(pl.multiple_of(part * 64, 64), 64)
+        norm, _ = normalize(x_ref[here, :])
+        low_ref[here, :] = (norm * gain_shift[0:1] + gain_shift[1:2]).astype(jnp.bfloat16)
+
+    drive(waves(up, every[:1]), waves(down, every[:1]), waves(out, every[:1]))
+    for behind in every:
+        pair.complete(behind)
+    hold = pltpu.make_async_copy(pair_hold, pair_all, hold_sem.at[0])
+    hold.start()
+    pieces = 2 * heads
+    moved = {}
+
+    def project(ahead):
+        target = lax.rem(t + ahead, groups)
+        weights = pair_hold[target].reshape(model, pieces * HEAD_DIM)
+        rows = jnp.dot(low_ref[...], weights, preferred_element_type=jnp.float32)
+        rows = rows.astype(jnp.bfloat16)
+        own = pl.ds(pl.multiple_of(t * tile, tile), tile)
+        for piece in range(pieces):
+            cut = rows[:, piece * HEAD_DIM : (piece + 1) * HEAD_DIM]
+            if ahead == 0:
+                qv_ref[piece, own, :] = cut
+            else:
+                leave_ref[ahead - 1, piece] = cut
+        return target
+
+    def send_piece(ahead, piece):
+        own = pl.ds(pl.multiple_of(t * tile, tile), tile)
+        slot = (ahead - 1) * pieces + piece
+        copy = pltpu.make_async_remote_copy(
+            src_ref=leave_ref.at[ahead - 1, piece],
+            dst_ref=qv_ref.at[piece, own],
+            send_sem=qv_send.at[slot],
+            recv_sem=qv_recv.at[slot],
+            device_id={"tp": lax.rem(t + ahead, groups)},
+            device_id_type=MESH,
+        )
+        copy.start()
+        moved[ahead, piece] = copy
+
+    for ahead in every[1:] + [0]:
+        project(ahead)
+        if ahead > 0:
+            send_piece(ahead, 0)
+            send_piece(ahead, heads)
+    for head in range(1, heads):
+        for ahead in every[1:]:
+            send_piece(ahead, head)
+            send_piece(ahead, heads + head)
+    rest = [waves(up, every[1:])]
+    drive(*rest)
+    sent = []
+    later = [waves(out, every[1:]), waves(down, every[1:])]
+    for head in range(heads):
+        for ahead in every[1:]:
+            moved[ahead, head].wait_recv()
+            moved[ahead, heads + head].wait_recv()
+        if head == 0:
+            out.begin()
+            down.begin()
+        key_ref[...] = unit_rows(qv_ref[head].astype(jnp.float32))[0].astype(jnp.bfloat16)
+        for ahead in every[1:] + [0]:
+            step = lax.rem(t + ahead, groups)
+            merged, lse = attend_rows(
+                tile,
+                step,
+                prefix,
+                qv_ref.at[head],
+                key_ref,
+                qv_ref.at[heads + head],
+                seen_ref.at[head],
+                own_ref.at[head],
+            )
+            rows = pl.ds(pl.multiple_of(step * tile, tile), tile)
+            full_ref[head, rows, :] = merged
+            lse_ref[head, step] = lse
+            low = merged.astype(jnp.bfloat16)
+            lanes = pl.ds(head * HEAD_DIM, HEAD_DIM)
+            if ahead == 0:
+                merged_ref[t, :, lanes] = low
+                continue
+            slot = head * groups + ahead
+            away_ref[slot] = low
+            copy = pltpu.make_async_remote_copy(
+                src_ref=away_ref.at[slot],
+                dst_ref=merged_ref.at[t, :, lanes],
+                send_sem=merged_send.at[slot],
+                recv_sem=merged_recv.at[slot],
+                device_id={"tp": step},
+                device_id_type=MESH,
+            )
+            copy.start()
+            sent.append(copy)
+            if head > 0:
+                for line in later:
+                    next(line, None)
+    drive(*later)
+    for copy in moved.values():
+        copy.wait_send()
+    for copy in sent:
+        copy.wait()
+    for array in (up, down, out):
+        for behind in every:
+            array.complete(behind)
+    for array in arrays.values():
+        array.finish()
+    hold.wait()
+
+
+def forward(groups, peers, prefix, order, x, small, pair, out, up, down):
+    tile, model = x.shape
+    heads, _, length = order.shape
+    assert length == groups * tile
+
+    def whole(shard):
+        return jax.ShapeDtypeStruct((groups, peers // 2, 2, *shard.shape), shard.dtype)
+
+    anywhere = pl.BlockSpec(memory_space=pl.ANY)
+    inside = pl.BlockSpec(memory_space=pltpu.VMEM)
+    low = jnp.bfloat16
+    exchanged = (groups - 1) * 2 * heads
+    return pl.pallas_call(
+        functools.partial(forward_kernel, groups, peers),
+        in_specs=[pl.BlockSpec(memory_space=pltpu.SMEM), inside, inside] + [anywhere] * 5,
+        out_specs=[inside] + [anywhere] * 4 + [inside] * 7,
+        out_shape=[whole(s) for s in (small, pair, out, up, down)]
+        + [
+            jax.ShapeDtypeStruct((tile, model), low),
+            jax.ShapeDtypeStruct((2 * heads, length, HEAD_DIM), low),
+            jax.ShapeDtypeStruct((heads, length, 128), low),
+            jax.ShapeDtypeStruct((heads, length, 128), low),
+            jax.ShapeDtypeStruct((groups, tile, heads * HEAD_DIM), low),
+            jax.ShapeDtypeStruct((heads, length, HEAD_DIM), jnp.float32),
+            jax.ShapeDtypeStruct((heads, groups, 8, tile), jnp.float32),
+        ],
+        scratch_shapes=[
+            pltpu.VMEM(whole(pair).shape, low),
+            pltpu.VMEM((groups - 1, 2 * heads, tile, HEAD_DIM), low),
+            pltpu.VMEM((length, HEAD_DIM), low),
+            pltpu.VMEM((heads * groups, tile, HEAD_DIM), low),
+            pltpu.SemaphoreType.DMA((exchanged,)),
+            pltpu.SemaphoreType.DMA((exchanged,)),
+            pltpu.SemaphoreType.DMA((heads * groups,)),
+            pltpu.SemaphoreType.DMA((heads * groups,)),
+            pltpu.SemaphoreType.DMA((1,)),
+        ]
+        + Gathered.scratch(groups, peers) * 5,
+        compiler_params=pltpu.CompilerParams(
+            collective_id=2, has_side_effects=True, vmem_limit_bytes=56 * 2**20
+        ),
+    )(prefix, order, x, small, pair, out, up, down)
 
 
 def cross(left, right):
@@ -516,21 +810,43 @@
     groups = lax.axis_size("tp")
     everyone = ("tp", "fsdp")
 
-    def collect(shard):
-        whole = lax.all_gather(shard, everyone, axis=0, tiled=True)
-        return whole.reshape(groups, -1, shard.shape[1])
-
+    peers = lax.axis_size("fsdp")
     small = jnp.stack([gain_one, shift_one, gain_two, shift_two, bias_down, bias_up])
-    small = lax.all_gather(small, everyone, axis=0, tiled=False).astype(jnp.float32)
-    small = small.reshape(groups, -1, 6, split)
+    small = jnp.pad(small, ((0, 10), (0, 0)))
+    pair_shard = jnp.concatenate([weight_shared, weight_value], axis=1)
+    (
+        small,
+        full_pair,
+        full_out,
+        full_up,
+        full_down,
+        first_low,
+        qv,
+        seen_by,
+        own_block,
+        merged,
+        merged_full,
+        lse,
+    ) = forward(
+        groups,
+        peers,
+        prefix_len,
+        hash_order[0],
+        in_second,
+        small,
+        pair_shard,
+        weight_out.T,
+        weight_up,
+        weight_down.T,
+    )
+    full_pair, full_out, full_up, full_down = (
+        a.reshape(groups, model, -1) for a in (full_pair, full_out, full_up, full_down)
+    )
+    small = small.reshape(groups, peers, 16, split).astype(jnp.float32)
     gain_a, shift_a, gain_b, shift_b, bias_last = (
         small[0, :, which].reshape(model) for which in range(5)
     )
     full_bias = small[:, :, 5].reshape(groups, 1, hidden_wide)
-    full_pair = collect(jnp.concatenate([weight_shared, weight_value], axis=1))
-    full_out = collect(weight_out.T)
-    full_up = collect(weight_up)
-    full_down = collect(weight_down.T)
 
     def dots(spec, left, right):
         return jnp.einsum(spec, left, right, preferred_element_type=jnp.float32)
@@ -538,14 +854,7 @@
     def exchange(parts):
         return lax.all_to_all(parts, "tp", 0, 0, tiled=True)
 
-    seen_by, own_block = bucket_rows(hash_order[0])
     norm_one, factor_one = normalize(in_second)
-    first_low = (norm_one * gain_a + shift_a).astype(jnp.bfloat16)
-    pair = dots("rd,tdc->trc", first_low, full_pair).astype(jnp.bfloat16)
-    pair = exchange(pair).reshape(groups * rows, 2 * heads_wide)
-    shared, values = pair[:, :heads_wide], pair[:, heads_wide:]
-    merged_low, merged_full, lse = attend(shared, values, seen_by, own_block, prefix_len)
-    merged = exchange(merged_low.reshape(groups, rows, heads_wide))
     out_first = in_first + dots("trc,tdc->rd", merged, full_out)
     norm_two, factor_two = normalize(out_first)
     second_low = (norm_two * gain_b + shift_b).astype(jnp.bfloat16)
@@ -568,7 +877,7 @@
     grad_merged = exchange(grad_merged).reshape(groups * rows, heads_wide)
     partial_out = dots("rd,trc->tdc", grad_branch, merged).astype(jnp.bfloat16)
     grad_shared, grad_value = attend_back(
-        shared, values, seen_by, own_block, prefix_len, merged_full, lse, grad_merged
+        qv, seen_by, own_block, prefix_len, merged_full, lse, grad_merged
     )
     grad_pair = jnp.concatenate([grad_shared, grad_value], axis=1)
     grad_pair = exchange(grad_pair.reshape(groups, rows, 2 * heads_wide))

time: 705 us -> 555 us (0.79)
  waiting for transfers between devices: 236 us -> 28.1 us
  Pallas kernels: 210 us -> 371 us
  blocking collectives: 43.4 us -> 0 us
  matrix products: 110 us -> 86.2 us
  local copies, waits for them, and re-layouts: 53 us -> 29.3 us
  between operations: 15.3 us -> 1.81 us
    pallas_call x2, Pallas kernels: 54.1 us -> 216 us  [the longest x1 184 us: forward(): pl.pallas_call(functools.partial(forward_kernel, groups, peers), in_specs...]
    all_gather x4 -> x0, waiting for transfers between devices: 126 us -> none  [collect(): whole = lax.all_gather(shard, everyone, axis=0, tiled=True)]
    all_to_all x4 -> x2, waiting for transfers between devices: 109 us -> 28.1 us  [exchange(): return lax.all_to_all(parts, 'tp', 0, 0, tiled=True)]
    all_gather x1 -> x0, blocking collectives: 43.4 us -> none  [on_device(): lax.all_gather(small, everyone, axis=0, tiled=False).astype(jnp.float32)]
    dot_general x12 -> x11, matrix products: 107 us -> 86.2 us  [dots(): return jnp.einsum(spec, left, right, preferred_element_type=jnp.float32)]
    all_gather x2 -> x0, local copies, waits for them, and re-layouts: 16 us -> none  [collect(): whole = lax.all_gather(shard, everyone, axis=0, tiled=True)]
    all_to_all x4 -> x2, starting transfers between devices: 17.3 us -> 22.6 us  [exchange(): return lax.all_to_all(parts, 'tp', 0, 0, tiled=True)]
  transfers between devices with their start and end apart: 8 -> 2, of which waited for: 7 -> 2; matrix products, arithmetic and copies ran while one was open for 13% -> 8% of each run, Pallas kernels for 4% -> 0%
where the time goes in v4:
time: 555 us; the launch traced here: 549 us
  Pallas kernels  371 us (67%)
  matrix products  86.2 us (16%)
  local copies, waits for them, and re-layouts  29.3 us (5%)
  waiting for transfers between devices  28.1 us (5%)
  starting transfers between devices  22.6 us (4%)
  other arithmetic  9.83 us (2%)
    pallas_call x1, Pallas kernels, forward(): pl.pallas_call(functools.partial(forward_kernel, groups, peers), in_specs...  184 us
    pallas_call x1, Pallas kernels, sum_everywhere(): pl.pallas_call(functools.partial(sum_kernel, groups, peers, len(blocks),...  156 us
    dot_general x11, matrix products, dots(): return jnp.einsum(spec, left, right, preferred_element_type=jnp.float32)  86.2 us
    pallas_call x1, Pallas kernels, attend_back(): pl.pallas_call(functools.partial(attend_back_kernel, tile), grid=(heads,...  31.8 us
    all_to_all x2, waiting for transfers between devices, exchange(): return lax.all_to_all(parts, 'tp', 0, 0, tiled=True)  28.1 us
    all_to_all x2, starting transfers between devices, exchange(): return lax.all_to_all(parts, 'tp', 0, 0, tiled=True)  22.6 us
  transfers between devices with their start and end apart: 2, of which 2 were waited for; matrix products, arithmetic and copies ran while one was open for 8% of the time, Pallas kernels for 0%

profile of v4, /device:TPU:0, one launch (start us, length us, event | category | flops | bytes accessed | tf_op | source)
XLA Modules:
  0.0 549.3 jit_solution(12366564998961740475)
XLA Ops:
  1.3 1.6 copy.44
  2.9 1.8 copy.45
  4.7 0.8 stack.27
  5.4 0.6 pad.8.small_ref
  6.0 1.5 pad_maximum_fusion.1.pair_ref
  7.6 183.9 %shard_map.280 = (bf16[4,4,2,16,128]{4,3,2,1,0:T(8,128)(2,1)}, bf16[4,4,2,128,512]{4,3,2,1,0:T(8,128)(2,1)}, bf16[4,4,2,128,256]{4,3,2,1,0:T(8,128)(2,1)}, bf16[...) custom-call(s32[1]{0:T(128)S(6)} %copy.78.prefix_ref, ...), custom_call_target="tpu_custom_call" | custom-call | tf_op jit(solution)/shard_map/pallas_call | solution.py:749
  191.4 0.9 fusion.28
  192.3 0.9 convert.1
  193.2 4.1 fusion.30
  197.3 0.3 multiply_reduce_fusion.3
  197.8 0.4 copy-done.11
  198.2 7.1 %fusion.24 = f32[4,1024,512]{1,2,0:T(8,128)} fusion(bf16[4,1024,1024]{2,1,0:T(8,128)(2,1)S(1)} %bitcast.183, f32[512,1024]{1,0:T(8,128)S(1)} %get-tuple-element.127, f32[1024]{0:T(1024)S(1)} %bitcast.170, f32[1024]{0:T(1024)S(1)} %bitcast.161, f32[512]{0:T(512)S(1)} %add_rsqrt_fusion.1, f32[512]{0:T(512)S(1)} %broadcast_multiply_fusion.5), kind=kOutput, calls=%fused_computation.66 | convolution fusion | flops 4297588736 | bytes 18886656 | tf_op jit(solution)/shard_map/rd,tdh->trh/dot_general | solution.py:852
  205.3 12.7 %convert_reduce_fusion = (f32[4,1024]{1,0:T(4,128)S(1)}, bf16[4,512,1024]{2,1,0:T(8,128)(2,1)}) fusion(f32[4,1024,512]{1,2,0:T(8,128)} %fusion.24, f32[4,1024]{1,0:T(4,128)S(1)} %bitcast.165, bf16[4,1024,1024]{2,1,0:T(8,128)(2,1)S(1)} %bitcast.182, f32[512,1024]{1,0:T(8,128)S(1)} %copy-done.8), kind=kOutput, calls=%fused_computation.10 | convolution fusion | flops 4341624832 | bytes 23101440 | tf_op jit(solution)/shard_map/rd,tdh->trh/dot_general | solution.py:852
  218.0 7.2 %fusion.8 = (f32[1024]{0:T(1024)S(1)}, f32[512]{0:T(512)S(1)}, f32[512]{0:T(512)S(1)}, f32[1024]{0:T(1024)S(1)}, f32[512,1024,1]{1,0,2:T(8,128)S(1)}) fusion(f32[512,1024]{1,0:T(8,128)S(1)} %get-tuple-element.127, f32[512]{0:T(512)S(1)} %add_rsqrt_fusion.1, f32[512]{0:T(512)S(1)} %broadcast_multiply_fusion.5, f32[1024]{0:T(1024)S(1)} %bitcast.162, ...), kind=kOutput, calls=%fused_computation.23 | convolution fusion | flops 4299682816 | bytes 16797696 | tf_op jit(solution)/shard_map/trh,tdh->rd/dot_general | solution.py:852
  225.2 0.7 multiply_add_fusion.2
  226.0 1.3 copy-done.7
  227.3 2.3 fusion.12
  229.6 18.0 %all-to-all-start = ((bf16[4,512,256]{1,2,0:T(8,128)(2,1)}), bf16[4,512,256]{1,2,0:T(8,128)(2,1)}, u32[]{:S(2)}, u32[]{:S(2)}) async-start(bf16[4,512,256]{1,2,0:T(8,128)(2,1)} %fusion.12), calls=%async_computation | async-start | bytes 2097152 | tf_op jit(solution)/shard_map/all_to_all | solution.py:855
  247.6 4.3 convert_bitcast_fusion.1
  251.9 0.2 reduce_sum.130
  252.1 0.3 multiply_reduce_fusion.1
  252.5 4.1 copy.53
  256.6 0.1 reshape.147
  256.7 0.1 reshape.148
  256.8 11.8 %convolution_convert_fusion.1 = bf16[4,1024,1024]{1,2,0:T(8,128)(2,1)} fusion(f32[512,1024]{1,0:T(8,128)S(1)} %copy-done.9, f32[4,1024,512]{1,2,0:T(8,128)} %fusion.24, f32[4,1024]{1,0:T(4,128)S(1)} %bitcast.166), kind=kOutput, calls=%fused_computation.13 | convolution fusion | flops 4320657408 | bytes 18890752 | tf_op jit(solution)/shard_map/rd,trh->tdh/dot_general | solution.py:852
  268.6 6.1 %all-to-all-done = bf16[4,512,256]{1,2,0:T(8,128)(2,1)} async-done(((bf16[4,512,256]{1,2,0:T(8,128)(2,1)}), bf16[4,512,256]{1,2,0:T(8,128)(2,1)}, u32[]{:S(2)}, u32[]{:S(2)}) %all-to-all-start) | async-done | bytes 1048608 | tf_op jit(solution)/shard_map/all_to_all | solution.py:855
  274.7 1.5 copy.47
  276.2 31.8 %shard_map.281 = (bf16[2048,256]{1,0:T(8,128)(2,1)S(1)}, bf16[2048,256]{1,0:T(8,128)(2,1)S(1)}) custom-call(s32[1]{0:T(128)S(6)} %copy.78.prefix_ref, bf16[4,2048,128]{2,1,0:T(8,128)(2,1)} %get-tuple-element.39.q_ref.v_ref, bf16[4,2048,128]{2,1,0:T(8,128)(2,1)} %get-tuple-element.39.q_ref.v_ref, bf16[2,2048,128]{2,1,0:T(8,128)(2,1)S(1)} %copy-done, ...), custom_call_target="tpu_custom_call" | custom-call | tf_op jit(solution)/shard_map/pallas_call | solution.py:143
  308.0 1.5 pad_maximum_fusion
  309.5 4.6 all-to-all-start.1
  314.1 11.3 %convolution_convert_fusion = bf16[4,1024,1024]{1,2,0:T(8,128)(2,1)} fusion(bf16[4,512,1024]{2,1,0:T(8,128)(2,1)} %get-tuple-element.108, f32[512,1024]{1,0:T(8,128)} %copy-done.5, f32[1024]{0:T(1024)S(1)} %bitcast.171, f32[1024]{0:T(1024)S(1)} %bitcast.164, f32[512]{0:T(512)S(1)} %add_rsqrt_fusion.1, f32[512]{0:T(512)S(1)} %broadcast_multiply_fusion.5), kind=kOutput, calls=%fused_computation.12 | convolution fusion | flops 4301783040 | bytes 14692352 | tf_op jit(solution)/shard_map/rd,trh->tdh/dot_general | solution.py:852
  325.4 12.5 %fusion.9 = f32[512,1024]{1,0:T(8,128)} fusion(f32[512,1024]{1,0:T(8,128)S(1)} %copy-done.4, bf16[4,1024,1024]{2,1,0:T(8,128)(2,1)} %bitcast.179, f32[1024]{0:T(1024)S(1)} %bitcast.169, f32[4,1024,512]{1,2,0:T(8,128)} %fusion.24, f32[4,1024]{1,0:T(4,128)S(1)} %bitcast.167), kind=kOutput, calls=%fused_computation.25 | convolution fusion | flops 4316987392 | bytes 20992000 | tf_op jit(solution)/shard_map/trh,tdh->rd/dot_general | solution.py:852
  337.9 22.0 %all-to-all-done.1 = bf16[4,512,512]{2,1,0:T(8,128)(2,1)} async-done(((bf16[4,512,512]{2,1,0:T(8,128)(2,1)}), bf16[4,512,512]{2,1,0:T(8,128)(2,1)}, u32[]{:S(2)}, u32[]{:S(2)}) %all-to-all-start.1) | async-done | bytes 2097184 | tf_op jit(solution)/shard_map/all_to_all | solution.py:855
  359.9 6.9 %fusion.7 = (f32[1024]{0:T(1024)S(1)}, f32[512]{0:T(512)S(1)}, f32[512]{0:T(512)S(1)}, f32[1024]{0:T(1024)S(1)}, f32[512,1024,1]{1,0,2:T(8,128)}) fusion(f32[512,1024]{1,0:T(8,128)S(1)} %copy-done.4, f32[512]{0:T(512)S(1)} %add_rsqrt_fusion, f32[512]{0:T(512)S(1)} %broadcast_multiply_fusion.2, f32[1024]{0:T(1024)S(1)} %bitcast.159, ...), kind=kOutput, calls=%fused_computation.19 | convolution fusion | flops 2152199168 | bytes 10506240 | tf_op jit(solution)/shard_map/trc,tdc->rd/dot_general | solution.py:852
  366.8 6.2 %convert_bitcast_fusion = bf16[4,1024,512]{1,2,0:T(8,128)(2,1)} fusion(bf16[4,512,512]{2,1,0:T(8,128)(2,1)} %all-to-all-done.1, bf16[512,1024]{1,0:T(8,128)(2,1)S(1)} %copy-done.13), kind=kOutput, calls=%fused_computation.14 | convolution fusion | flops 2149580800 | bytes 7340032 | tf_op jit(solution)/shard_map/rd,trc->tdc/dot_general | solution.py:852
  372.9 6.2 %copy.51 = bf16[4,1024,512]{2,1,0:T(8,128)(2,1)} copy(bf16[4,1024,512]{1,2,0:T(8,128)(2,1)} %convert_bitcast_fusion) | data formatting | bytes 8388608 | tf_op jit(solution)/shard_map/convert_element_type | solution.py:884
  379.1 4.3 fusion.26
  383.5 0.1 reshape.145
  383.6 0.1 reshape.146
  383.6 0.1 concatenate.11
  383.7 0.7 copy.74
  384.4 155.8 %shard_map.282 = (f32[128,1024]{1,0:T(8,128)}, f32[128,1024]{1,0:T(8,128)}, f32[128,512]{1,0:T(8,128)}, f32[128,256]{1,0:T(8,128)}, f32[8,128]{1,0:T(8,128)}) custom-call(bf16[4,8,128,1024]{3,2,1,0:T(8,128)(2,1)} %bitcast.142, bf16[4,8,128,1024]{3,2,1,0:T(8,128)(2,1)} %bitcast.143, bf16[4,8,128,512]{3,2,1,0:T(8,128)(2,1)} %bitcast.141, ...), custom_call_target="tpu_custom_call" | custom-call | tf_op jit(solution)/shard_map/pallas_call | solution.py:364
  540.2 1.7 fusion.27
  542.0 1.7 copy.59
  543.6 1.2 slice_bitcast_fusion
  544.8 2.0 copy.60
  546.8 1.4 fusion.29
  548.3 0.8 copy.79
  (50 shorter events, 0.3 us)
Async XLA Ops:
  193.2 5.0 copy-start.11
  197.3 27.9 %copy-start.5 = (f32[512,1024]{1,0:T(8,128)}, f32[512,1024]{1,0:T(8,128)S(1)}, u32[]{:S(2)}) copy-start(f32[512,1024]{1,0:T(8,128)S(1)} %get-tuple-element.127) | copy-start | bytes 6291460
  197.3 8.0 %slice-start = ((s8[8388608]{0:T(1024)(128)(4,1)}), s8[4194304]{0:T(1024)(128)(4,1)S(1)}, s32[]{:S(2)}) async-start(s8[8388608]{0:T(1024)(128)(4,1)} %bitcast.180), calls=%async_computation.2 | async-start | bytes 8388608
  198.2 7.1 %copy-start.8 = (f32[512,1024]{1,0:T(8,128)S(1)}, f32[512,1024]{1,0:T(8,128)}, u32[]{:S(2)}) copy-start(f32[512,1024]{1,0:T(8,128)} %param.20) | copy-start | bytes 6291460
  198.2 7.1 %slice-start.1 = ((s8[8388608]{0:T(1024)(128)(4,1)}), s8[4194304]{0:T(1024)(128)(4,1)S(1)}, s32[]{:S(2)}) async-start(s8[8388608]{0:T(1024)(128)(4,1)} %bitcast.180), calls=%async_computation.3 | async-start | bytes 8388608
  218.0 7.2 %copy-start.6 = (f32[512,1024]{1,0:T(8,128)S(1)}, f32[512,1024]{1,0:T(8,128)}, u32[]{:S(2)}) copy-start(f32[512,1024]{1,0:T(8,128)} %param.19) | copy-start | bytes 6291460
  225.2 2.1 copy-start.12
  226.0 1.3 copy-start.7
  229.6 18.0 %copy-start.14 = (bf16[4,512,256]{2,1,0:T(8,128)(2,1)S(1)}, bf16[4,512,256]{2,1,0:T(8,128)(2,1)}, u32[]{:S(2)}) copy-start(bf16[4,512,256]{2,1,0:T(8,128)(2,1)} %get-tuple-element.34) | copy-start | bytes 3145732
  229.6 45.1 %all-to-all-start = ((bf16[4,512,256]{1,2,0:T(8,128)(2,1)}), bf16[4,512,256]{1,2,0:T(8,128)(2,1)}, u32[]{:S(2)}, u32[]{:S(2)}) async-start(bf16[4,512,256]{1,2,0:T(8,128)(2,1)} %fusion.12), calls=%async_computation | async-start | bytes 2097152 | tf_op jit(solution)/shard_map/all_to_all | solution.py:855
  247.6 4.4 copy-start.3
  252.5 4.3 copy-start.9
  256.8 19.4 %copy-start.2 = (f32[2,4,8,512]{3,2,1,0:T(8,128)S(1)}, f32[2,4,8,512]{3,2,1,0:T(8,128)}, u32[]{:S(2)}) copy-start(f32[2,4,8,512]{3,2,1,0:T(8,128)} %get-tuple-element.43.lse_ref) | copy-start | bytes 393220
  268.5 7.6 %copy-start = (bf16[2,2048,128]{2,1,0:T(8,128)(2,1)S(1)}, bf16[2,2048,128]{2,1,0:T(8,128)(2,1)}, u32[]{:S(2)}) copy-start(bf16[2,2048,128]{2,1,0:T(8,128)(2,1)} %get-tuple-element.40.a_ref) | copy-start | bytes 3145732
  268.5 7.6 %copy-start.1 = (bf16[2,2048,128]{2,1,0:T(8,128)(2,1)S(1)}, bf16[2,2048,128]{2,1,0:T(8,128)(2,1)}, u32[]{:S(2)}) copy-start(bf16[2,2048,128]{2,1,0:T(8,128)(2,1)} %get-tuple-element.41.b_ref) | copy-start | bytes 3145732
  309.5 50.4 %all-to-all-start.1 = ((bf16[4,512,512]{2,1,0:T(8,128)(2,1)}), bf16[4,512,512]{2,1,0:T(8,128)(2,1)}, u32[]{:S(2)}, u32[]{:S(2)}) async-start(bf16[4,512,512]{2,1,0:T(8,128)(2,1)} %bitcast.27), calls=%async_computation.1 | async-start | bytes 4194304 | tf_op jit(solution)/shard_map/all_to_all | solution.py:855
  314.1 11.3 %copy-start.4 = (f32[512,1024]{1,0:T(8,128)S(1)}, f32[512,1024]{1,0:T(8,128)}, u32[]{:S(2)}) copy-start(f32[512,1024]{1,0:T(8,128)} %x_ref.1) | copy-start | bytes 6291460
  359.8 6.9 %copy-start.13 = (bf16[512,1024]{1,0:T(8,128)(2,1)S(1)}, bf16[512,1024]{1,0:T(8,128)(2,1)}, u32[]{:S(2)}) copy-start(bf16[512,1024]{1,0:T(8,128)(2,1)} %get-tuple-element.47) | copy-start | bytes 3145732
  540.2 8.1 %copy-start.10 = (f32[128,1024]{1,0:T(8,128)S(1)}, f32[128,1024]{1,0:T(8,128)}, u32[]{:S(2)}) copy-start(f32[128,1024]{1,0:T(8,128)} %get-tuple-element.134) | copy-start | bytes 1572868

commit v5 on v4

--- a/solution.py
+++ b/solution.py
@@ -55,110 +55,6 @@
 def unit_rows(rows):
     inv_norm = lax.rsqrt(jnp.mean(rows * rows, axis=-1, keepdims=True) + 1e-06)
     return rows * inv_norm, inv_norm
-
-
-def attend_back_kernel(
-    tile,
-    prefix_ref,
-    q_ref,
-    v_ref,
-    a_ref,
-    b_ref,
-    full_ref,
-    lse_ref,
-    g_ref,
-    gs_ref,
-    gv_ref,
-    key_ref,
-    dq_ref,
-    dk_ref,
-    dv_ref,
-):
-    step = pl.program_id(1)
-    prefix = prefix_ref[0]
-
-    @pl.when(step == 0)
-    def _():
-        key_ref[...] = unit_rows(q_ref[...].astype(jnp.float32))[0].astype(jnp.bfloat16)
-        dk_ref[...] = jnp.zeros_like(dk_ref)
-        dv_ref[...] = jnp.zeros_like(dv_ref)
-        dq_ref[...] = jnp.zeros_like(dq_ref)
-
-    own = pl.ds(pl.multiple_of(step * tile, tile), tile)
-    query = q_ref[own, :]
-    seen = a_ref[own, :]
-    grad = g_ref[own, :]
-    delta = jnp.sum((grad.astype(jnp.float32) * full_ref[...]).T, axis=0, keepdims=True)
-    lse = lse_ref[0:1, :]
-    alone = jnp.where(lse == ALONE, 1.0, 0.0)
-
-    def visit(part, masked):
-        keys = pl.ds(pl.multiple_of(part * tile, tile), tile)
-        key = key_ref[keys, :]
-        scores = dot_nt(key, query) * SCORE_SCALE
-        count = dot_nt(b_ref[keys, :], seen)
-        if masked:
-            col = part * tile + lax.broadcasted_iota(jnp.int32, (tile, tile), 0)
-            row = step * tile + lax.broadcasted_iota(jnp.int32, (tile, tile), 1)
-            same = row == col
-            allowed = (col < row) | ((row < prefix) & (col < prefix) & (row != col))
-            count = jnp.where(allowed, count, 0.0)
-        probs = count * jnp.exp2(jnp.minimum(scores - lse, 0.0))
-        grad_scores = probs * (dot_nt(v_ref[keys, :], grad) - delta)
-        if masked:
-            probs = jnp.where(same, alone, probs)
-        grad_scores = grad_scores.astype(jnp.bfloat16)
-        dv_ref[keys, :] += jnp.dot(
-            probs.astype(jnp.bfloat16), grad, preferred_element_type=jnp.float32
-        )
-        dk_ref[keys, :] += jnp.dot(grad_scores, query, preferred_element_type=jnp.float32)
-        dq_ref[own, :] += cross(grad_scores, key)
-
-    @pl.loop(0, step)
-    def _(part):
-        visit(part, False)
-
-    ahead = jnp.where(step * tile < prefix, (prefix + tile - 1) // tile, 0)
-
-    @pl.loop(step, jnp.maximum(step + 1, ahead))
-    def _(part):
-        visit(part, True)
-
-    @pl.when(step == pl.num_programs(1) - 1)
-    def _():
-        rows = q_ref[...].astype(jnp.float32)
-        _, inv_norm = unit_rows(rows)
-        factor = HEAD_DIM ** (-0.5)
-        grad_keys = dk_ref[...] * factor
-        inner = jnp.mean(grad_keys * rows, axis=-1, keepdims=True)
-        total = dq_ref[...] * factor + inv_norm * grad_keys - rows * (inv_norm**3 * inner)
-        gs_ref[...] = total.astype(jnp.bfloat16)
-        gv_ref[...] = dv_ref[...].astype(jnp.bfloat16)
-
-
-def attend_back(qv, seen_by, own_block, prefix, full, lse, grads):
-    heads, length, _ = full.shape
-    tile = lse.shape[-1]
-    whole = pl.BlockSpec((None, length, HEAD_DIM), lambda h, i: (h, 0, 0))
-    return pl.pallas_call(
-        functools.partial(attend_back_kernel, tile),
-        grid=(heads, length // tile),
-        in_specs=[
-            pl.BlockSpec(memory_space=pltpu.SMEM),
-            whole,
-            pl.BlockSpec((None, length, HEAD_DIM), lambda h, i: (h + heads, 0, 0)),
-            whole,
-            whole,
-            pl.BlockSpec((None, tile, HEAD_DIM), lambda h, i: (h, i, 0)),
-            pl.BlockSpec((None, None, 8, tile), lambda h, i: (h, i, 0, 0)),
-            pl.BlockSpec((length, HEAD_DIM), lambda h, i: (0, h)),
-        ],
-        out_specs=[pl.BlockSpec((length, HEAD_DIM), lambda h, i: (0, h))] * 2,
-        out_shape=[jax.ShapeDtypeStruct((length, heads * HEAD_DIM), jnp.bfloat16)] * 2,
-        scratch_shapes=[pltpu.VMEM((length, HEAD_DIM), jnp.bfloat16)]
-        + [pltpu.VMEM((length, HEAD_DIM), jnp.float32)] * 3,
-        compiler_params=pltpu.CompilerParams(vmem_limit_bytes=48 * 2**20),
-    )(prefix, qv, qv, seen_by, own_block, full, lse, grads)
 
 
 MESH = pl.DeviceIdType.MESH
@@ -196,32 +92,34 @@
 
 class Summed:
     @staticmethod
-    def scratch(groups, peers, rows, cols, dtype):
+    def scratch(groups, peers, rows, cols, dtype, inside):
         count, half = peers // 2, groups // 2
         steps = count.bit_length() - 1
         shapes = []
         for _ in range(2):
-            shapes += [pltpu.VMEM((half, count, rows, cols), dtype)] * 2
+            shapes.append(pltpu.VMEM((half, count, rows, cols), dtype))
             shapes += [pltpu.VMEM((half, count >> (k + 1), rows, cols), dtype) for k in range(steps)]
         shapes += [pltpu.VMEM((groups, rows, cols), dtype)] * 2
         copies = 2 * count + 2 * steps + groups
         shapes += [pltpu.SemaphoreType.DMA((copies,))] * 2
-        shapes.append(pltpu.SemaphoreType.DMA((2 * count,)))
+        if not inside:
+            shapes.append(pltpu.VMEM((2, half, rows, cols), dtype))
+            shapes.append(pltpu.SemaphoreType.DMA((2,)))
         return shapes
 
     def __init__(self, groups, source, out, scratch):
         scratch = list(scratch)
         self.groups, self.half, self.source, self.out = groups, groups // 2, source, out
-        self.own, self.landings = [], []
+        self.landings = []
         self.count = scratch[0].shape[1]
         self.steps = self.count.bit_length() - 1
         for _ in range(2):
-            self.own.append(scratch.pop(0))
             self.landings.append([scratch.pop(0) for _ in range(1 + self.steps)])
-        self.packed, self.arrived, self.send, self.recv, self.local = scratch
+        self.packed, self.arrived, self.send, self.recv = scratch[:4]
+        self.stage, self.local = scratch[4:] if len(scratch) > 4 else (None, None)
         self.rows = self.packed.shape[1]
         self.f, self.t = lax.axis_index("fsdp"), lax.axis_index("tp")
-        self.waiting = {}
+        self.waiting, self.loads = {}, {}
 
     def remote(self, name, slot, source, target, device):
         copy = pltpu.make_async_remote_copy(
@@ -239,37 +137,52 @@
         for copy in self.waiting.pop(name):
             copy.wait()
 
-    def place(self, side, block):
-        return block if side == 0 else mirrored(block, self.steps)
+    def mine(self, chunk):
+        block, side = chunk // 2, chunk % 2
+        return self.source.at[
+            pl.ds(side * self.half, self.half), 2 * block + bit_of(self.f, 0)
+        ]
+
+    def load(self, chunk):
+        if self.stage is None or chunk >= 2 * self.count:
+            return
+        copy = pltpu.make_async_copy(
+            self.mine(chunk), self.stage.at[chunk % 2], self.local.at[chunk % 2]
+        )
+        copy.start()
+        self.loads[chunk] = copy
+
+    def landing(self, chunk):
+        block, side = chunk // 2, chunk % 2
+        place = block if side == 0 else mirrored(block, self.steps)
+        return self.landings[side][0].at[:, place]
 
     def begin(self):
         core = bit_of(self.f, 0)
-        for block in range(self.count):
-            for side in range(2):
-                part = pl.ds(side * self.half, self.half)
-                place = self.place(side, block)
-                slot = side * self.count + block
-                self.remote(
-                    "core",
-                    slot,
-                    self.source.at[part, 2 * block + 1 - core],
-                    self.landings[side][0].at[:, place],
-                    {"fsdp": across(self.f, 0)},
-                )
-                copy = pltpu.make_async_copy(
-                    self.source.at[part, 2 * block + core],
-                    self.own[side].at[:, place],
-                    self.local.at[slot],
-                )
-                copy.start()
-                self.waiting.setdefault("core", []).append(copy)
+        for chunk in range(2 * self.count):
+            block, side = chunk // 2, chunk % 2
+            self.remote(
+                ("core", chunk),
+                chunk,
+                self.source.at[pl.ds(side * self.half, self.half), 2 * block + 1 - core],
+                self.landing(chunk),
+                {"fsdp": across(self.f, 0)},
+            )
+        self.load(0)
+        self.load(1)
 
     def core_step(self):
-        self.settle("core")
-        for side in range(2):
-            own = self.own[side]
-            add_rows(own, own, self.landings[side][0], own.shape[:2], self.rows)
-        self.current = list(self.own)
+        for chunk in range(2 * self.count):
+            self.settle(("core", chunk))
+            if self.stage is None:
+                own = self.mine(chunk)
+            else:
+                self.loads.pop(chunk).wait()
+                own = self.stage.at[chunk % 2]
+            landed = self.landing(chunk)
+            add_rows(landed, landed, own, (self.half,), self.rows)
+            self.load(chunk + 2)
+        self.current = [landings[0] for landings in self.landings]
 
     def along(self, side, step):
         return 1 + (self.steps - 1 - step if side == 0 else step)
@@ -325,6 +238,17 @@
                 total += self.arrived[ahead, here].astype(jnp.float32)
             self.out[here] = total
 
+    def start(self):
+        self.core_step()
+        self.send_step(0)
+
+    def follow(self, step):
+        self.add_step(step)
+        if step + 1 < self.steps:
+            self.send_step(step + 1)
+        else:
+            self.send_groups()
+
 
 def greet(groups, peers):
     f, t = lax.axis_index("fsdp"), lax.axis_index("tp")
@@ -334,43 +258,6 @@
     for partner in partners:
         pl.semaphore_signal(barrier, inc=1, device_id=partner, device_id_type=MESH)
     pl.semaphore_wait(barrier, len(partners))
-
-
-def sum_kernel(groups, peers, count, per, *refs):
-    sources, outs, scratch = refs[:count], refs[count : 2 * count], refs[2 * count :]
-    arrays = [
-        Summed(groups, sources[k], outs[k], scratch[k * per : (k + 1) * per]) for k in range(count)
-    ]
-    greet(groups, peers)
-    for array in arrays:
-        array.begin()
-    for array in arrays:
-        array.core_step()
-        array.send_step(0)
-    for step in range(arrays[0].steps):
-        for array in arrays:
-            array.add_step(step)
-            if step + 1 < array.steps:
-                array.send_step(step + 1)
-            else:
-                array.send_groups()
-    for array in arrays:
-        array.finish()
-
-
-def sum_everywhere(groups, peers, arrays):
-    blocks = [a.reshape(groups, peers, -1, a.shape[-1]) for a in arrays]
-    scratch = [Summed.scratch(groups, peers, *b.shape[2:], b.dtype) for b in blocks]
-    return pl.pallas_call(
-        functools.partial(sum_kernel, groups, peers, len(blocks), len(scratch[0])),
-        in_specs=[pl.BlockSpec(memory_space=pl.ANY)] * len(blocks),
-        out_specs=[pl.BlockSpec(memory_space=pltpu.VMEM)] * len(blocks),
-        out_shape=[jax.ShapeDtypeStruct(b.shape[2:], jnp.float32) for b in blocks],
-        scratch_shapes=sum(scratch, []),
-        compiler_params=pltpu.CompilerParams(
-            collective_id=1, has_side_effects=True, vmem_limit_bytes=56 * 2**20
-        ),
-    )(*blocks)
 
 
 class Gathered:
@@ -784,6 +671,343 @@
     )
 
 
+def attend_back_rows(
+    tile,
+    step,
+    prefix,
+    query_ref,
+    key_ref,
+    value_ref,
+    seen_ref,
+    own_ref,
+    full_ref,
+    lse,
+    grad_ref,
+    dq_ref,
+    dk_ref,
+    dv_ref,
+):
+    own = pl.ds(pl.multiple_of(step * tile, tile), tile)
+    query = query_ref[own, :]
+    seen = seen_ref[own, :]
+    grad = grad_ref[own, :]
+    delta = jnp.sum((grad.astype(jnp.float32) * full_ref[own, :]).T, axis=0, keepdims=True)
+    alone = jnp.where(lse == ALONE, 1.0, 0.0)
+
+    def visit(part, masked):
+        keys = pl.ds(pl.multiple_of(part * tile, tile), tile)
+        key = key_ref[keys, :]
+        scores = dot_nt(key, query) * SCORE_SCALE
+        count = dot_nt(own_ref[keys, :], seen)
+        if masked:
+            col = part * tile + lax.broadcasted_iota(jnp.int32, (tile, tile), 0)
+            row = step * tile + lax.broadcasted_iota(jnp.int32, (tile, tile), 1)
+            same = row == col
+            allowed = (col < row) | ((row < prefix) & (col < prefix) & (row != col))
+            count = jnp.where(allowed, count, 0.0)
+        probs = count * jnp.exp2(jnp.minimum(scores - lse, 0.0))
+        grad_scores = probs * (dot_nt(value_ref[keys, :], grad) - delta)
+        if masked:
+            probs = jnp.where(same, alone, probs)
+        grad_scores = grad_scores.astype(jnp.bfloat16)
+        dv_ref[keys, :] += jnp.dot(
+            probs.astype(jnp.bfloat16), grad, preferred_element_type=jnp.float32
+        )
+        dk_ref[keys, :] += jnp.dot(grad_scores, query, preferred_element_type=jnp.float32)
+        dq_ref[own, :] += cross(grad_scores, key)
+
+    @pl.loop(0, step)
+    def _(part):
+        visit(part, False)
+
+    @pl.loop(step, last_part(step, tile, query_ref.shape[0]))
+    def _(part):
+        visit(part, True)
+
+
+def backward_kernel(
+    groups,
+    peers,
+    prefix_ref,
+    gm_ref,
+    gain_ref,
+    vector_ref,
+    lse_ref,
+    qv_hbm,
+    seen_hbm,
+    own_hbm,
+    full_hbm,
+    low_hbm,
+    pair_hbm,
+    x_hbm,
+    cot_hbm,
+    down_ref,
+    up_ref,
+    out_ref,
+    gis_hbm,
+    down_sum,
+    up_sum,
+    out_sum,
+    pair_sum,
+    vector_sum,
+    qv_ref,
+    seen_ref,
+    own_ref,
+    full_ref,
+    low_ref,
+    pair_ref,
+    load_sem,
+    grad_ref,
+    gm_send,
+    gm_recv,
+    gm_local,
+    key_ref,
+    dq_ref,
+    dk_ref,
+    dv_ref,
+    leave_ref,
+    back_ref,
+    back_send,
+    back_recv,
+    turned_ref,
+    first_ref,
+    x_ref,
+    cot_ref,
+    gis_ref,
+    row_sem,
+    vector_own,
+    *scratch,
+):
+    tile, model = low_ref.shape
+    heads, length, _ = full_ref.shape
+    prefix = prefix_ref[0]
+    t = lax.axis_index("tp")
+    split = vector_own.shape[-1]
+    others = range(1, groups)
+    scratch = list(scratch)
+    arrays = []
+    for source, total, many in (
+        (down_ref, down_sum, 0),
+        (up_ref, up_sum, 0),
+        (out_ref, out_sum, 0),
+        (pair_ref, pair_sum, 2),
+        (vector_own, vector_sum, 2),
+    ):
+        steps = (peers // 2).bit_length() - 1
+        many = 2 * (1 + steps) + 6 - many
+        arrays.append(Summed(groups, source, total, [scratch.pop(0) for _ in range(many)]))
+    down, up, out, pair, vector = arrays
+    steps = down.steps
+    greet(groups, peers)
+    down.begin()
+    up.begin()
+    loads = []
+    for slot, (source, target) in enumerate(
+        (
+            (qv_hbm, qv_ref),
+            (seen_hbm, seen_ref),
+            (own_hbm, own_ref),
+            (full_hbm, full_ref),
+            (low_hbm, low_ref),
+            (pair_hbm, pair_ref),
+        )
+    ):
+        copy = pltpu.make_async_copy(source, target, load_sem.at[slot])
+        copy.start()
+        loads.append(copy)
+    mine = pl.ds(pl.multiple_of(t * tile, tile), tile)
+    moved = {}
+    for head in range(heads):
+        lanes = pl.ds(head * HEAD_DIM, HEAD_DIM)
+        copy = pltpu.make_async_copy(
+            gm_ref.at[t, :, lanes], grad_ref.at[head, mine], gm_local.at[head]
+        )
+        copy.start()
+        moved[head, 0] = copy
+        for ahead in others:
+            target = lax.rem(t + ahead, groups)
+            copy = pltpu.make_async_remote_copy(
+                src_ref=gm_ref.at[target, :, lanes],
+                dst_ref=grad_ref.at[head, mine],
+                send_sem=gm_send.at[head * groups + ahead],
+                recv_sem=gm_recv.at[head * groups + ahead],
+                device_id={"tp": target},
+                device_id_type=MESH,
+            )
+            copy.start()
+            moved[head, ahead] = copy
+    out.begin()
+    down.start()
+    up.start()
+    for copy in loads:
+        copy.wait()
+    turned_ref[...] = low_ref[...].T
+    sent = {}
+
+    def attend(head):
+        for ahead in range(groups):
+            moved[head, ahead].wait()
+        key_ref[...] = unit_rows(qv_ref[head].astype(jnp.float32))[0].astype(jnp.bfloat16)
+        dk_ref[...] = jnp.zeros_like(dk_ref)
+        dv_ref[...] = jnp.zeros_like(dv_ref)
+        dq_ref[...] = jnp.zeros_like(dq_ref)
+
+        @pl.loop(0, length // tile)
+        def _(step):
+            attend_back_rows(
+                tile,
+                step,
+                prefix,
+                qv_ref.at[head],
+                key_ref,
+                qv_ref.at[heads + head],
+                seen_ref.at[head],
+                own_ref.at[head],
+                full_ref.at[head],
+                lse_ref[head, step, 0:1, :],
+                grad_ref.at[head],
+                dq_ref,
+                dk_ref,
+                dv_ref,
+            )
+
+        for ahead in list(others) + [0]:
+            target = lax.rem(t + ahead, groups)
+            here = pl.ds(pl.multiple_of(target * tile, tile), tile)
+            rows = qv_ref[head, here].astype(jnp.float32)
+            _, inv_norm = unit_rows(rows)
+            factor = HEAD_DIM ** (-0.5)
+            grad_keys = dk_ref[here] * factor
+            inner = jnp.mean(grad_keys * rows, axis=-1, keepdims=True)
+            total = dq_ref[here] * factor + inv_norm * grad_keys - rows * (inv_norm**3 * inner)
+            for piece, value in ((head, total), (heads + head, dv_ref[here])):
+                lanes = pl.ds(piece * HEAD_DIM, HEAD_DIM)
+                value = value.astype(jnp.bfloat16)
+                if ahead == 0:
+                    back_ref[t, :, lanes] = value
+                    continue
+                slot = piece * groups + ahead
+                leave_ref[slot] = value
+                copy = pltpu.make_async_remote_copy(
+                    src_ref=leave_ref.at[slot],
+                    dst_ref=back_ref.at[t, :, lanes],
+                    send_sem=back_send.at[slot],
+                    recv_sem=back_recv.at[slot],
+                    device_id={"tp": target},
+                    device_id_type=MESH,
+                )
+                copy.start()
+                sent[slot] = copy
+
+    attend(0)
+    down.follow(0)
+    for head in range(1, heads):
+        attend(head)
+    out.start()
+    for step in range(1, steps):
+        up.follow(step - 1)
+        down.follow(step)
+    out.follow(0)
+    up.follow(steps - 1)
+    for copy in sent.values():
+        copy.wait()
+    first_ref[...] = jnp.zeros_like(first_ref)
+    for group in range(groups):
+        back = back_ref[group]
+        weights = pair_ref[group].reshape(model, back.shape[1])
+        first_ref[...] += dot_nt(back, weights)
+        partial = jnp.dot(turned_ref[...], back, preferred_element_type=jnp.float32)
+        pair_ref[group] = partial.astype(jnp.bfloat16).reshape(pair_ref.shape[1:])
+    pair.begin()
+    pair.start()
+    for step in range(1, steps):
+        out.follow(step)
+    chunk = x_ref.shape[0]
+    gain = gain_ref[...]
+
+    def rows_back(part, sums):
+        here = pl.ds(pl.multiple_of(part * chunk, chunk), chunk)
+        copies = [
+            pltpu.make_async_copy(x_hbm.at[here], x_ref, row_sem.at[0]),
+            pltpu.make_async_copy(cot_hbm.at[here], cot_ref, row_sem.at[1]),
+        ]
+        for copy in copies:
+            copy.start()
+        for copy in copies:
+            copy.wait()
+        norm, factor = normalize(x_ref[...])
+        part_second, by_norm, plain = norm_backward(first_ref[here], norm, factor, gain)
+        gis_ref[...] = cot_ref[...] + part_second
+        copy = pltpu.make_async_copy(gis_ref, gis_hbm.at[here], row_sem.at[2])
+        copy.start()
+        copy.wait()
+        return sums[0] + by_norm[None], sums[1] + plain[None]
+
+    zero = jnp.zeros((1, model), jnp.float32)
+    sums = lax.fori_loop(0, tile // chunk, rows_back, (zero, zero))
+    vector_own[...] = vector_ref[...]
+    for peer in range(peers):
+        for row in range(2):
+            cut = sums[row][:, peer * split : (peer + 1) * split]
+            for group in range(groups):
+                vector_own[group, peer, row : row + 1, :] = cut
+    vector.begin()
+    vector.start()
+    for step in range(steps):
+        pair.follow(step)
+        vector.follow(step)
+    for array in arrays:
+        array.finish()
+
+
+def backward(
+    groups, peers, prefix, gm, gain, vectors, lse, qv, seen, own, full, low, pair, x, cot, sums
+):
+    heads, length, _ = full.shape
+    tile, model = low.shape
+    down, up, out = (a.reshape(groups, peers, -1, a.shape[-1]) for a in sums)
+    pair = pair.reshape(groups, peers, -1, pair.shape[-1])
+    anywhere = pl.BlockSpec(memory_space=pl.ANY)
+    inside = pl.BlockSpec(memory_space=pltpu.VMEM)
+    totals = [down, up, out, pair, vectors]
+    f32, bf16 = jnp.float32, jnp.bfloat16
+    dma = pltpu.SemaphoreType.DMA
+    chunk = min(128, tile)
+    scratch = [pltpu.VMEM(a.shape, a.dtype) for a in (qv, seen, own, full, low, pair)]
+    scratch += [
+        dma((6,)),
+        pltpu.VMEM((heads, length, HEAD_DIM), bf16),
+        dma((heads * groups,)),
+        dma((heads * groups,)),
+        dma((heads,)),
+        pltpu.VMEM((length, HEAD_DIM), bf16),
+    ]
+    scratch += [pltpu.VMEM((length, HEAD_DIM), f32)] * 3
+    scratch += [
+        pltpu.VMEM((2 * heads * groups, tile, HEAD_DIM), bf16),
+        pltpu.VMEM((groups, tile, 2 * heads * HEAD_DIM), bf16),
+        dma((2 * heads * groups,)),
+        dma((2 * heads * groups,)),
+        pltpu.VMEM((model, tile), bf16),
+        pltpu.VMEM((tile, model), f32),
+    ]
+    scratch += [pltpu.VMEM((chunk, model), f32)] * 3
+    scratch += [dma((3,)), pltpu.VMEM(vectors.shape, f32)]
+    for place, a in enumerate(totals):
+        scratch += Summed.scratch(groups, peers, *a.shape[2:], a.dtype, place >= 3)
+    return pl.pallas_call(
+        functools.partial(backward_kernel, groups, peers),
+        in_specs=[pl.BlockSpec(memory_space=pltpu.SMEM)] + [inside] * 4 + [anywhere] * 11,
+        out_specs=[anywhere] + [inside] * 5,
+        out_shape=[jax.ShapeDtypeStruct((tile, model), f32)]
+        + [jax.ShapeDtypeStruct(a.shape[2:], f32) for a in totals],
+        scratch_shapes=scratch,
+        compiler_params=pltpu.CompilerParams(
+            collective_id=1, has_side_effects=True, vmem_limit_bytes=61 * 2**20
+        ),
+    )(prefix, gm, gain, vectors, lse, qv, seen, own, full, low, pair, x, cot, down, up, out)
+
+
 def on_device(
     in_first,
     in_second,
@@ -851,10 +1075,6 @@
     def dots(spec, left, right):
         return jnp.einsum(spec, left, right, preferred_element_type=jnp.float32)
 
-    def exchange(parts):
-        return lax.all_to_all(parts, "tp", 0, 0, tiled=True)
-
-    norm_one, factor_one = normalize(in_second)
     out_first = in_first + dots("trc,tdc->rd", merged, full_out)
     norm_two, factor_two = normalize(out_first)
     second_low = (norm_two * gain_b + shift_b).astype(jnp.bfloat16)
@@ -874,38 +1094,32 @@
     partial_down = dots("rd,trh->tdh", grad_up, hidden).astype(jnp.bfloat16)
     partial_up = dots("rd,trh->tdh", second_low, grad_pre).astype(jnp.bfloat16)
     grad_merged = dots("rd,tdc->trc", grad_branch, full_out).astype(jnp.bfloat16)
-    grad_merged = exchange(grad_merged).reshape(groups * rows, heads_wide)
     partial_out = dots("rd,trc->tdc", grad_branch, merged).astype(jnp.bfloat16)
-    grad_shared, grad_value = attend_back(
-        qv, seen_by, own_block, prefix_len, merged_full, lse, grad_merged
-    )
-    grad_pair = jnp.concatenate([grad_shared, grad_value], axis=1)
-    grad_pair = exchange(grad_pair.reshape(groups, rows, 2 * heads_wide))
-    partial_pair = dots("rd,trc->tdc", first_low, grad_pair).astype(jnp.bfloat16)
-    grad_first = dots("trc,tdc->rd", grad_pair, full_pair)
-    part_second, grad_gain_one, grad_shift_one = norm_backward(
-        grad_first, norm_one, factor_one, gain_a
-    )
-    grad_in_second = cot_second + part_second
-    grad_bias_up = jnp.sum(grad_pre, axis=1, dtype=jnp.float32)
-    vectors = [
-        jnp.sum(cot_second, axis=0),
-        grad_gain_one,
-        grad_shift_one,
-        grad_gain_two,
-        grad_shift_two,
-    ]
+    vectors = [grad_gain_two, grad_shift_two, jnp.sum(cot_second, axis=0)]
+    vectors = [jnp.broadcast_to(v.reshape(-1, split), (groups, peers, split)) for v in vectors]
+    vectors.append(jnp.sum(grad_pre, axis=1, dtype=jnp.float32).reshape(groups, peers, split))
+    vectors = jnp.pad(jnp.stack(vectors, axis=2), ((0, 0), (0, 0), (2, 2), (0, 0)))
+    grad_in_second, summed_down, summed_up, summed_out, summed_pair, vectors = backward(
+        groups,
+        peers,
+        prefix_len,
+        grad_merged,
+        gain_a[None],
+        vectors,
+        lse,
+        qv,
+        seen_by,
+        own_block,
+        merged_full,
+        first_low,
+        full_pair,
+        in_second,
+        cot_second,
+        [partial_down, partial_up, partial_out],
+    )
     piece = split // groups
-    vectors = [v.reshape(-1, groups, piece).transpose(1, 0, 2) for v in vectors]
-    vectors = jnp.concatenate([grad_bias_up.reshape(groups, -1, split)] + vectors, axis=2)
-    wide = vectors.shape[2]
-    vectors = jnp.pad(vectors, ((0, 0), (0, 0), (0, -wide % 1024)))
-    vectors = vectors.reshape(groups, -1, 8, vectors.shape[2] // 8)
-    summed_down, summed_up, summed_pair, summed_out, vectors = sum_everywhere(
-        groups, vectors.shape[1], [partial_down, partial_up, partial_pair, partial_out, vectors]
-    )
-    vectors = vectors.reshape(-1)
-    tails = [vectors[split + which * piece : split + (which + 1) * piece] for which in range(5)]
+    group = lax.axis_index("tp")
+    tails = lax.dynamic_slice_in_dim(vectors[:5], group * piece, piece, axis=1)
     return (
         out_first,
         out_second,
@@ -915,9 +1129,13 @@
         summed_pair[:, heads_wide:],
         summed_out.T,
         summed_up,
-        vectors[:split],
+        vectors[5],
         summed_down.T,
-        *tails,
+        tails[4],
+        tails[0],
+        tails[1],
+        tails[2],
+        tails[3],
     )
 
 

time: 555 us -> 464 us (0.84)
  waiting for transfers between devices: 28.1 us -> 0 us
  starting transfers between devices: 22.6 us -> 0 us
  Pallas kernels: 371 us -> 350 us
  matrix products: 86.2 us -> 74.3 us
  local copies, waits for them, and re-layouts: 29.3 us -> 22.8 us
    all_to_all x2 -> x0, waiting for transfers between devices: 28.1 us -> none  [exchange(): return lax.all_to_all(parts, 'tp', 0, 0, tiled=True)]
    all_to_all x2 -> x0, starting transfers between devices: 22.6 us -> none  [exchange(): return lax.all_to_all(parts, 'tp', 0, 0, tiled=True)]
    pallas_call x2 -> x1, Pallas kernels: 188 us -> 166 us  [backward(): pl.pallas_call(functools.partial(backward_kernel, groups, peers), in_spec...]
    dot_general x11 -> x9, matrix products: 86.2 us -> 74.3 us  [dots(): return jnp.einsum(spec, left, right, preferred_element_type=jnp.float32)]
    convert_element_type x1 -> x0, local copies, waits for them, and re-layouts: 6.21 us -> none  [on_device(): dots('rd,trc->tdc', first_low, grad_pair).astype(jnp.bfloat16)]
    unnamed x43 -> x27, local copies, waits for them, and re-layouts: 10.4 us -> 11.6 us
  transfers between devices with their start and end apart: 2 -> 0, of which waited for: 2 -> 0; matrix products, arithmetic and copies ran while one was open for 8% -> 0% of each run, Pallas kernels for 0% -> 0%
where the time goes in v5:
time: 464 us; the launch traced here: 457 us
  Pallas kernels  350 us (75%)
  matrix products  74.3 us (16%)
  local copies, waits for them, and re-layouts  22.8 us (5%)
  other arithmetic  8.32 us (2%)
    pallas_call x1, Pallas kernels, forward(): pl.pallas_call(functools.partial(forward_kernel, groups, peers), in_specs...  184 us
    pallas_call x1, Pallas kernels, backward(): pl.pallas_call(functools.partial(backward_kernel, groups, peers), in_spec...  166 us
    dot_general x9, matrix products, dots(): return jnp.einsum(spec, left, right, preferred_element_type=jnp.float32)  74.3 us
    unnamed x27, local copies, waits for them, and re-layouts  11.6 us

profile of v5, /device:TPU:0, one launch (start us, length us, event | category | flops | bytes accessed | tf_op | source)
XLA Modules:
  0.0 456.7 jit_solution(6403158981359547584)
XLA Ops:
  1.3 0.8 stack.30
  2.1 0.6 pad.8.small_ref
  2.7 1.7 reduce_sum.78
  4.4 1.6 copy.32
  6.0 1.5 pad_maximum_fusion.pair_ref
  7.5 1.8 copy.33
  9.3 183.8 %shard_map.280 = (bf16[4,4,2,16,128]{4,3,2,1,0:T(8,128)(2,1)}, bf16[4,4,2,128,512]{4,3,2,1,0:T(8,128)(2,1)}, bf16[4,4,2,128,256]{4,3,2,1,0:T(8,128)(2,1)}, bf16[...) custom-call(s32[1]{0:T(128)S(6)} %copy.56.prefix_ref, ...), custom_call_target="tpu_custom_call" | custom-call | tf_op jit(solution)/shard_map/pallas_call | solution.py:636
  193.2 0.8 fusion.25
  194.0 0.9 convert.1
  194.9 0.6 slice_bitcast_fusion.gain_ref
  195.6 0.0 copy-start.5
  195.6 4.1 fusion.26
  199.6 0.0 copy-start.2
  199.7 0.3 multiply_reduce_fusion.1
  200.0 0.5 copy-done.5
  200.5 7.1 %fusion.22 = f32[4,1024,512]{1,2,0:T(8,128)} fusion(bf16[4,1024,1024]{2,1,0:T(8,128)(2,1)S(1)} %bitcast.149, f32[512,1024]{1,0:T(8,128)S(1)} %get-tuple-element.102, f32[1024]{0:T(1024)S(1)} %bitcast.140, f32[1024]{0:T(1024)S(1)} %bitcast.130, f32[512]{0:T(512)S(1)} %add_rsqrt_fusion, f32[512]{0:T(512)S(1)} %broadcast_multiply_fusion.2), kind=kOutput, calls=%fused_computation.60 | convolution fusion | flops 4297588736 | bytes 18886656 | tf_op jit(solution)/shard_map/rd,tdh->trh/dot_general | solution.py:1076
  207.6 0.0 copy-done
  207.6 12.6 %fusion.8 = f32[512,1024]{1,0:T(8,128)} fusion(f32[512,1024]{1,0:T(8,128)S(1)} %copy-done, bf16[4,1024,1024]{2,1,0:T(8,128)(2,1)} %bitcast.153, f32[1024]{0:T(1024)S(1)} %bitcast.142, f32[4,1024,512]{1,2,0:T(8,128)} %fusion.22, f32[4,1024]{1,0:T(4,128)S(1)} %bitcast.134), kind=kOutput, calls=%fused_computation.19 | convolution fusion | flops 4316987392 | bytes 20992000 | tf_op jit(solution)/shard_map/trh,tdh->rd/dot_general | solution.py:1076
  220.2 0.0 copy-done.1
  220.2 15.5 %convert_reduce_fusion = (f32[4,1024]{1,0:T(4,128)S(1)}, bf16[4,512,1024]{2,1,0:T(8,128)(2,1)}) fusion(f32[4,1024,512]{1,2,0:T(8,128)} %fusion.22, f32[4,1024]{1,0:T(4,128)S(1)} %bitcast.135, bf16[4,1024,1024]{2,1,0:T(8,128)(2,1)} %bitcast.154, f32[512,1024]{1,0:T(8,128)S(1)} %copy-done.1), kind=kOutput, calls=%fused_computation.10 | convolution fusion | flops 4341624832 | bytes 23101440 | tf_op jit(solution)/shard_map/rd,tdh->trh/dot_general | solution.py:1076
  235.8 0.0 slice-start.1
  235.8 11.9 %convolution_convert_fusion.1 = bf16[4,1024,1024]{1,2,0:T(8,128)(2,1)} fusion(f32[512,1024]{1,0:T(8,128)S(1)} %copy-done.1, f32[4,1024,512]{1,2,0:T(8,128)} %fusion.22, f32[4,1024]{1,0:T(4,128)S(1)} %bitcast.136), kind=kOutput, calls=%fused_computation.13 | convolution fusion | flops 4320657408 | bytes 18890752 | tf_op jit(solution)/shard_map/rd,trh->tdh/dot_general | solution.py:1076
  247.6 0.0 slice-done
  247.6 0.0 slice-done.1
  247.6 8.4 %fusion.7 = (f32[1024]{0:T(1024)S(1)}, f32[512]{0:T(512)S(1)}, f32[512]{0:T(512)S(1)}, f32[1024]{0:T(1024)S(1)}, f32[512,1024,1]{1,0,2:T(8,128)}) fusion(f32[512,1024]{1,0:T(8,128)S(1)} %get-tuple-element.102, f32[512]{0:T(512)S(1)} %add_rsqrt_fusion, f32[512]{0:T(512)S(1)} %broadcast_multiply_fusion.2, f32[1024]{0:T(1024)S(1)} %bitcast.131, ...), kind=kOutput, calls=%fused_computation.17 | convolution fusion | flops 4299682816 | bytes 16797696 | tf_op jit(solution)/shard_map/trh,tdh->rd/dot_general | solution.py:1076
  256.1 0.0 copy-start.6
  256.1 3.0 multiply_add_fusion.1
  259.1 0.0 copy-done.6
  259.1 0.0 copy-start.3
  259.1 0.0 copy-start.7
  259.1 2.2 fusion.10.gm_ref
  261.4 0.7 select_maximum_fusion.vector_ref
  262.1 0.0 copy-done.3
  262.1 0.0 copy-done.7
  262.1 2.6 convert_bitcast_fusion
  264.8 4.1 copy.40
  268.9 0.0 copy-done.2
  268.9 9.9 %convolution_convert_fusion = bf16[4,1024,1024]{1,2,0:T(8,128)(2,1)} fusion(bf16[4,512,1024]{2,1,0:T(8,128)(2,1)} %get-tuple-element.84, f32[512,1024]{1,0:T(8,128)S(1)} %get-tuple-element.102, f32[1024]{0:T(1024)S(1)} %bitcast.141, f32[1024]{0:T(1024)S(1)} %bitcast.133, f32[512]{0:T(512)S(1)} %add_rsqrt_fusion, f32[512]{0:T(512)S(1)} %broadcast_multiply_fusion.2), kind=kOutput, calls=%fused_computation.12 | convolution fusion | flops 4301783040 | bytes 14692352 | tf_op jit(solution)/shard_map/rd,trh->tdh/dot_general | solution.py:1076
  278.8 165.8 %shard_map.281 = (f32[512,1024]{1,0:T(8,128)}, f32[128,1024]{1,0:T(8,128)}, f32[128,1024]{1,0:T(8,128)}, f32[128,256]{1,0:T(8,128)}, f32[128,512]{1,0:T(8,128)}, /*index=5*/f32[8,128]{1,0:T(8,128)}) custom-call(s32[1]{0:T(128)S(6)} %copy.56.prefix_ref, bf16[4,512,256]{2,1,0:T(8,128)(2,1)} %fusion.10.gm_ref, f32[1,1024]{1,0:T(1,128)} %slice_bitcast_fusion.gain_ref, ...), custom_call_target="tpu_custom_call" | custom-call | tf_op jit(solution)/shard_map/pallas_call | solution.py:998
  444.6 0.0 copy-start.4
  444.6 1.2 slice_bitcast_fusion.6
  445.9 0.7 constant_dynamic-slice_fusion
  446.6 0.5 slice_bitcast_fusion.1
  447.1 1.7 copy.41
  448.8 1.7 fusion.24
  450.5 2.0 copy.42
  452.5 3.2 copy.57
  455.7 0.8 copy.58
  (14 shorter events, 0.1 us)
Async XLA Ops:
  195.6 5.0 %copy-start.5 = (bf16[4,4,2,128,1024]{4,3,2,1,0:T(8,128)(2,1)S(1)}, bf16[4,4,2,128,1024]{4,3,2,1,0:T(8,128)(2,1)}, u32[]{:S(2)}) copy-start(bf16[4,4,2,128,1024]{4,3,2,1,0:T(8,128)(2,1)} %get-tuple-element.35) | copy-start | bytes 25165828
  199.6 69.2 %copy-start.2 = (f32[512,1024]{1,0:T(8,128)}, f32[512,1024]{1,0:T(8,128)S(1)}, u32[]{:S(2)}) copy-start(f32[512,1024]{1,0:T(8,128)S(1)} %get-tuple-element.102) | copy-start | bytes 6291460
  200.5 7.1 %copy-start = (f32[512,1024]{1,0:T(8,128)S(1)}, f32[512,1024]{1,0:T(8,128)}, u32[]{:S(2)}) copy-start(f32[512,1024]{1,0:T(8,128)} %x_hbm.1) | copy-start | bytes 6291460
  207.6 12.6 %copy-start.1 = (f32[512,1024]{1,0:T(8,128)S(1)}, f32[512,1024]{1,0:T(8,128)}, u32[]{:S(2)}) copy-start(f32[512,1024]{1,0:T(8,128)} %cot_hbm.1) | copy-start | bytes 6291460
  220.2 27.4 %slice-start = ((s8[8388608]{0:T(1024)(128)(4,1)}), s8[4194304]{0:T(1024)(128)(4,1)S(1)}, s32[]{:S(2)}) async-start(s8[8388608]{0:T(1024)(128)(4,1)} %bitcast.150), calls=%async_computation | async-start | bytes 8388608
  235.8 11.9 %slice-start.1 = ((s8[8388608]{0:T(1024)(128)(4,1)}), s8[4194304]{0:T(1024)(128)(4,1)S(1)}, s32[]{:S(2)}) async-start(s8[8388608]{0:T(1024)(128)(4,1)} %bitcast.150), calls=%async_computation.1 | async-start | bytes 8388608
  256.1 3.0 copy-start.6
  259.1 3.0 copy-start.3
  259.1 3.0 copy-start.7
  444.6 11.1 %copy-start.4 = (f32[128,1024]{1,0:T(8,128)S(1)}, f32[128,1024]{1,0:T(8,128)}, u32[]{:S(2)}) copy-start(f32[128,1024]{1,0:T(8,128)} %get-tuple-element.109) | copy-start | bytes 1572868
